TPU v7x, 32 devices: a whole 2x2x4 slice. The times are simulated.
32 devices in a mesh: trk: 8 (over z, y), mod: 4 (over x, core).
Axes of the slice: x: 2, y: 2, z: 4, core: 2. Of those that a mesh axis runs over, the one named last changes fastest.
Arguments:
- local_deriv: float32 [5, 12, 16384], P(None, None, ('trk', 'mod')), may hold values from -6 to 6
- global_deriv: float32 [8, 12, 16384], P(None, None, ('trk', 'mod')), may hold values from -6 to 6
- measured: float32 [12, 16384], P(None, ('trk', 'mod')), may hold values from -5 to 5
- hit_weight: float32 [12, 16384], P(None, ('trk', 'mod')), may hold values from 0.25 to 4
- hit_module: int32 [12, 16384], P(None, ('trk', 'mod')), may hold values from 0 to 65535, as said below
- hit_count: int32 [16384], P(('trk', 'mod')), may hold values from 6 to 12
- track_road: int32 [16384], P(('trk', 'mod')), may hold values from 0 to 8191, as said below
- road_start: int32 [8192], P(('trk', 'mod')), may hold values from 0 to 65535, as said below
- prior_weight: float32 [65536, 8], P(('trk', 'mod')), may hold values from 0.5 to 8
Outputs:
- normal_blocks: float32 [8192, 128, 128], P(('trk', 'mod'))
- rhs: float32 [65536, 8], P(('trk', 'mod'))
- corrections: float32 [65536, 8], P(('trk', 'mod'))
Inputs may be any that keep to these rules, and one draw needn't show every extreme that they name: `hit_module`: each hit slot of track t, padding too, names one of the 16 modules (road_start[track_road[t]] + k) mod 65536, k = 0 to 15; the slots of one track name different modules. `track_road`: call the device that holds road_start[r] the owner of road r. At most 64 of the 512 tracks of one device belong to roads of one owner; one owner receives exactly 64 tracks from every device. road_start[r] lies between 16 / 2 * r and 16 / 2 * r + 16 / 2 - 1.
All inputs are finite; a program needn't handle non-finite values.
Results may differ from a plain program's by a relative error of at most 0.00016.
Values sent between devices are 32-bit elements; how exact they have to be, the bound alone decides.
No kernel may reach another device: no remote copies, remote signals or barrier semaphores. Data moves between devices by JAX's collectives and lax.ppermute only.
A program may use at most 128 MiB of HBM per device.

v0:
```python
import jax
import jax.numpy as jnp
from jax import lax
from jax.sharding import PartitionSpec as P

NPAR = 8
NHIT = 12
ROAD = 16
NMOD = 65536


EPS = 1e-06
HIGHEST = lax.Precision.HIGHEST


def from_behind(value, axis, steps):
    count = lax.axis_size(axis)
    pairs = [(source, (source + steps) % count) for source in range(count)]
    return lax.ppermute(value, axis, pairs)


def local_fit(local_deriv, measured, hit_weight, hit_count):
    nlocal = local_deriv.shape[0]
    hit_slots = local_deriv.shape[1]
    position = lax.broadcasted_iota(jnp.int32, hit_weight.shape, 0)
    weight = jnp.where(position < hit_count[None, :], hit_weight, jnp.zeros_like(hit_weight))
    weighted = local_deriv * weight[None]
    local_gram = jnp.sum(weighted[:, None] * local_deriv[None, :], axis=2)
    factor = {}
    for row_num in range(nlocal):
        for col_num in range(row_num + 1):
            running = local_gram[row_num, col_num]
            if row_num == col_num:
                running = running + 1.0
            for inner_num in range(col_num):
                running = running - factor[row_num, inner_num] * factor[col_num, inner_num]
            if row_num == col_num:
                factor[row_num, col_num] = jnp.sqrt(running)
            else:
                factor[row_num, col_num] = running / factor[col_num, col_num]
    solved_rows = []
    for row_num in range(nlocal):
        running = weighted[row_num]
        for col_num in range(row_num):
            running = running - factor[row_num, col_num][None] * solved_rows[col_num]
        solved_rows.append(running / factor[row_num, row_num][None])
    projected = jnp.stack(solved_rows)
    diagonal = jnp.eye(hit_slots, dtype=jnp.float32)[:, :, None] * weight[None]
    schur_block = diagonal - jnp.sum(projected[:, :, None] * projected[:, None, :], axis=0)
    solved = jnp.sum(schur_block * measured[None], axis=1)
    return (schur_block, solved, projected, weight)


def minres_finish(beta_one, alpha_one, beta_two, alpha_two, beta_three, lanczos_one, lanczos_two):
    entry_first = alpha_one * alpha_one + beta_two * beta_two
    entry_cross = beta_two * (alpha_one + alpha_two)
    entry_second = beta_two * beta_two + alpha_two * alpha_two + beta_three * beta_three
    determinant = entry_first * entry_second - entry_cross * entry_cross
    coef_one = beta_one * (entry_second * alpha_one - entry_cross * beta_two) / determinant
    coef_two = beta_one * (entry_first * beta_two - entry_cross * alpha_one) / determinant
    return coef_one * lanczos_one + coef_two * lanczos_two


def global_sum(local_term):
    return lax.psum(local_term, ("trk", "mod"))


def lanczos_pair(direction, mapped):
    alpha_val = global_sum(jnp.sum(direction * mapped))
    residue = mapped - alpha_val * direction
    beta_val = jnp.sqrt(global_sum(jnp.sum(residue * residue)) + EPS)
    return (alpha_val, beta_val, residue)


def fold_rim(extended, owned_rows):
    returned = from_behind(extended[owned_rows:], ("trk", "mod"), 1)
    return extended[:owned_rows].at[: returned.shape[0]].add(returned)


def on_device(
    local_deriv,
    global_deriv,
    measured,
    hit_weight,
    hit_module,
    hit_count,
    track_road,
    road_start,
    prior_weight,
):
    devices = lax.axis_size(("trk", "mod"))
    road_dev = road_start.shape[0]
    owned_rows = prior_weight.shape[0]
    tracks_here = hit_count.shape[0]
    capacity = 4 * tracks_here // devices
    slots_all = devices * capacity
    schur_block, solved, projected, weight = local_fit(local_deriv, measured, hit_weight, hit_count)
    global_rows = jnp.transpose(global_deriv, (2, 1, 0)).reshape(tracks_here, NHIT * NPAR)
    payload = jnp.concatenate(
        [
            global_rows,
            jnp.transpose(schur_block, (2, 0, 1)).reshape(tracks_here, NHIT * NHIT),
            solved.T,
        ],
        axis=1,
    )
    width_all = payload.shape[1]
    owner_dev = track_road // road_dev
    member = (
        owner_dev[:, None] == lax.broadcasted_iota(jnp.int32, (tracks_here, devices), 1)
    ).astype(jnp.int32)
    rank_in = jnp.sum(jnp.cumsum(member, axis=0) * member, axis=1) - 1
    target = owner_dev * capacity + rank_in
    send_values = jnp.zeros((slots_all, width_all), jnp.float32).at[target].set(payload)
    send_modules = jnp.zeros((slots_all, NHIT), jnp.int32).at[target].set(hit_module.T)
    send_roads = jnp.zeros((slots_all,), jnp.int32).at[target].set(track_road % road_dev)
    recv_values, recv_modules, recv_roads = (
        lax.all_to_all(send_values, ("trk", "mod"), split_axis=0, concat_axis=0, tiled=True),
        lax.all_to_all(send_modules, ("trk", "mod"), split_axis=0, concat_axis=0, tiled=True),
        lax.all_to_all(send_roads, ("trk", "mod"), split_axis=0, concat_axis=0, tiled=True),
    )
    columns_global = NHIT * NPAR
    recv_global = recv_values[:, :columns_global].reshape(slots_all, NHIT, NPAR)
    recv_solved = recv_values[:, width_all - NHIT :]
    recv_schur = recv_values[:, columns_global : columns_global + NHIT * NHIT].reshape(
        slots_all, NHIT, NHIT
    )
    road_match = (
        recv_roads[:, None] == lax.broadcasted_iota(jnp.int32, (slots_all, road_dev), 1)
    ).astype(jnp.int32)
    road_hot = road_match.astype(jnp.float32)
    start_of = jnp.sum(road_match * road_start[None, :], axis=1)
    slot_num = jnp.clip((recv_modules - start_of[:, None]) % NMOD, 0, ROAD - 1)
    slot_hot = (
        slot_num[:, :, None] == lax.broadcasted_iota(jnp.int32, (slots_all, NHIT, ROAD), 2)
    ).astype(jnp.float32)
    laid = (slot_hot[:, :, :, None] * recv_global[:, :, None, :]).reshape(
        slots_all, NHIT, ROAD * NPAR
    )
    block_count = 8
    rows_each = slots_all // block_count
    block_width = ROAD * NPAR

    def accumulate(total, pieces):
        part_laid, part_schur, part_road = pieces
        outer = jnp.zeros((rows_each, block_width, block_width), jnp.float32)
        for row_num in range(NHIT):
            mixed_row = jnp.zeros((rows_each, block_width), jnp.float32)
            for col_num in range(NHIT):
                mixed_row = (
                    mixed_row + part_schur[:, row_num, col_num][:, None] * part_laid[:, col_num]
                )
            outer = outer + part_laid[:, row_num][:, :, None] * mixed_row[:, None, :]
        flat_outer = outer.reshape(rows_each, block_width * block_width)
        return (
            total
            + jnp.dot(
                part_road.T, flat_outer, precision=HIGHEST, preferred_element_type=jnp.float32
            ),
            None,
        )

    start_total = jnp.zeros((road_dev, block_width * block_width), jnp.float32)
    total, unused = lax.scan(
        accumulate,
        start_total,
        (
            laid.reshape(block_count, rows_each, NHIT, block_width),
            recv_schur.reshape(block_count, rows_each, NHIT, NHIT),
            road_hot.reshape(block_count, rows_each, road_dev),
        ),
    )
    normal_blocks = total.reshape(road_dev, block_width, block_width)
    spacing = ROAD // 2
    local_start = spacing * lax.broadcasted_iota(jnp.int32, (road_dev,), 0) + road_start % spacing
    gather_index = local_start[:, None] + lax.broadcasted_iota(jnp.int32, (road_dev, ROAD), 1)
    track_rhs = jnp.sum(laid * recv_solved[:, :, None], axis=1)
    road_rhs = jnp.dot(road_hot.T, track_rhs, precision=HIGHEST, preferred_element_type=jnp.float32)
    extended = (
        jnp.zeros((owned_rows + ROAD, NPAR), jnp.float32)
        .at[gather_index.reshape(-1)]
        .add(road_rhs.reshape(-1, NPAR))
    )
    rhs = fold_rim(extended, owned_rows)

    def apply_normal(vector):
        rim_rows = from_behind(vector[:ROAD], ("trk", "mod"), -1)
        extended_vec = jnp.concatenate([vector, rim_rows], axis=0)
        pieces = extended_vec[gather_index].reshape(road_dev, ROAD * NPAR)
        mapped = jnp.sum(normal_blocks * pieces[:, None, :], axis=2)
        spread = (
            jnp.zeros_like(extended_vec).at[gather_index.reshape(-1)].add(mapped.reshape(-1, NPAR))
        )
        return prior_weight * vector + fold_rim(spread, owned_rows)

    beta_one = jnp.sqrt(global_sum(jnp.sum(rhs * rhs)) + EPS)
    lanczos_one = rhs / beta_one
    alpha_one, beta_two, residue = lanczos_pair(lanczos_one, apply_normal(lanczos_one))
    lanczos_two = residue / beta_two
    alpha_two, beta_three, residue = lanczos_pair(
        lanczos_two, apply_normal(lanczos_two) - beta_two * lanczos_one
    )
    corrections = minres_finish(
        beta_one, alpha_one, beta_two, alpha_two, beta_three, lanczos_one, lanczos_two
    )
    return (normal_blocks, rhs, corrections)


def solution(mesh):
    in_specs = (
        P(None, None, ("trk", "mod")),
        P(None, None, ("trk", "mod")),
        P(None, ("trk", "mod")),
        P(None, ("trk", "mod")),
        P(None, ("trk", "mod")),
        P(("trk", "mod")),
        P(("trk", "mod")),
        P(("trk", "mod")),
        P(("trk", "mod"), None),
    )
    out_specs = (P(("trk", "mod"), None, None), P(("trk", "mod"), None), P(("trk", "mod"), None))
    return jax.shard_map(
        on_device, mesh=mesh, in_specs=in_specs, out_specs=out_specs, check_vma=False
    )
```

profile of v0, /device:TPU:0, one launch (start us, length us, event | category | flops | bytes accessed | tf_op | source)
XLA Modules:
  0.0 1374.5 jit_solution(11927756184174185879)
XLA Ops:
  47.2 39.4 %all-to-all-done.2 = f32[32,64,252]{2,1,0:T(8,128)S(1)} async-done(((f32[32,64,252]{2,1,0:T(8,128)}), f32[32,64,252]{2,1,0:T(8,128)S(1)}, u32[]{:S(2)}, u32[]{:S(2)}) %all-to-all-start.2) | async-done | bytes 2064416 | tf_op jit(solution)/shard_map/all_to_all | solution.py:118
  102.6 22.9 %scatter_custom_fusion.3 = f32[2064,8]{1,0:T(8,128)S(1)} fusion(s32[4096]{0:T(1024)S(1)} %bitcast.815, f32[4096,8]{1,0:T(8,128)} %reshape.2166, f32[]{:T(128)} %constant.151.clone.1), kind=kCustom, calls=%fused_computation.71 | custom fusion | flops 32768 | bytes 66560 | tf_op jit(solution)/shard_map/scatter-add | solution.py:182
  130.9 15.5 %copy.131 = f32[192,8,8,256]{3,2,1,0:T(8,128)} copy(f32[192,8,8,256]{3,1,2,0:T(8,128)} %bitcast.622) | data formatting | bytes 25165824
  148.5 38.4 %psum.35 = f32[]{:T(128)} all-reduce(f32[]{:T(128)} %multiply_reduce_fusion.10), channel_id=1, replica_groups=mesh['trk'=8,'mod'=4] {'trk','mod'}, use_global_device_ids=true, to_apply=%region_15.16 | all-reduce | flops 1 | bytes 8 | tf_op jit(solution)/shard_map/psum | solution.py:65
  191.0 895.5 %while.14 = (s32[]{:T(128)}, f32[256,16384]{1,0:T(8,128)}, f32[8,256,256]{2,1,0:T(8,128)}, f32[8,256,12,128]{1,0,3,2:T(8,128)}, f32[8,256,12,12]{1,0,3,2:T(8,128)S(1)}, /*index=5*/s32[]{:T(128)}, s32[]{:T(128)}) while((s32[]{:T(128)}, f32[256,16384]{1,0:T(8,128)}, f32[8,256,256]{2,1,0:T(8,128)}, f32[8,256,12,128]{1,0,3,2:T(8,128)}, ...), condition=%wide.region_11.12_spmd.clone, body=%wide.region_10.11_spmd.clone.sunk | while | flops 12998803456 | bytes 111110376 | solution.py:164
  223.2 57.4 %multiply_add_fusion.4 = f32[256,128,128]{2,1,0:T(8,128)} fusion(f32[256,128]{1,0:T(8,128)S(1)} %add_bitcast_fusion.26, f32[256,128]{1,0:T(8,128)S(1)} %get-tuple-element.551, f32[256,128]{1,0:T(8,128)S(1)} %add_bitcast_fusion.27, f32[256,128]{1,0:T(8,128)S(1)} %get-tuple-element.564, f32[256,128]{1,0:T(8,128)S(1)} %add_bitcast_fusion.28, ...), kind=kLoop, calls=%fused_computation.11.clone.1 | loop fusion | flops 96468992 | bytes 19922944 | tf_op jit(solution)/shard_map/while/body/eval_jaxpr/add | solution.py:153
  280.6 31.2 %convolution_add_fusion.2 = f32[256,16384]{1,0:T(8,128)} fusion(f32[32,8,128,128]{3,2,1,0:T(8,128)} %bitcast.617, f32[256,16384]{1,0:T(8,128)} %get-tuple-element.703, pred[]{:T(512)S(6)} %compare.26, f32[8,256,256]{2,1,0:T(8,128)} %get-tuple-element.711, s32[]{:T(128)} %get-tuple-element.702), kind=kOutput, calls=%fused_computation.8.clone.1 | convolution fusion | flops 12893290496 | bytes 50594304 | tf_op jit(solution)/shard_map/while/body/eval_jaxpr/dot_general | solution.py:157
  332.6 57.4 %multiply_add_fusion.4 = f32[256,128,128]{2,1,0:T(8,128)} fusion(f32[256,128]{1,0:T(8,128)S(1)} %add_bitcast_fusion.26, f32[256,128]{1,0:T(8,128)S(1)} %get-tuple-element.551, f32[256,128]{1,0:T(8,128)S(1)} %add_bitcast_fusion.27, f32[256,128]{1,0:T(8,128)S(1)} %get-tuple-element.564, f32[256,128]{1,0:T(8,128)S(1)} %add_bitcast_fusion.28, ...), kind=kLoop, calls=%fused_computation.11.clone.1 | loop fusion | flops 96468992 | bytes 19922944 | tf_op jit(solution)/shard_map/while/body/eval_jaxpr/add | solution.py:153
  390.1 32.4 %convolution_add_fusion.2 = f32[256,16384]{1,0:T(8,128)} fusion(f32[32,8,128,128]{3,2,1,0:T(8,128)} %bitcast.617, f32[256,16384]{1,0:T(8,128)} %get-tuple-element.703, pred[]{:T(512)S(6)} %compare.26, f32[8,256,256]{2,1,0:T(8,128)} %get-tuple-element.711, s32[]{:T(128)} %get-tuple-element.702), kind=kOutput, calls=%fused_computation.8.clone.1 | convolution fusion | flops 12893290496 | bytes 50594304 | tf_op jit(solution)/shard_map/while/body/eval_jaxpr/dot_general | solution.py:157
  443.3 57.4 %multiply_add_fusion.4 = f32[256,128,128]{2,1,0:T(8,128)} fusion(f32[256,128]{1,0:T(8,128)S(1)} %add_bitcast_fusion.26, f32[256,128]{1,0:T(8,128)S(1)} %get-tuple-element.551, f32[256,128]{1,0:T(8,128)S(1)} %add_bitcast_fusion.27, f32[256,128]{1,0:T(8,128)S(1)} %get-tuple-element.564, f32[256,128]{1,0:T(8,128)S(1)} %add_bitcast_fusion.28, ...), kind=kLoop, calls=%fused_computation.11.clone.1 | loop fusion | flops 96468992 | bytes 19922944 | tf_op jit(solution)/shard_map/while/body/eval_jaxpr/add | solution.py:153
  500.7 32.4 %convolution_add_fusion.2 = f32[256,16384]{1,0:T(8,128)} fusion(f32[32,8,128,128]{3,2,1,0:T(8,128)} %bitcast.617, f32[256,16384]{1,0:T(8,128)} %get-tuple-element.703, pred[]{:T(512)S(6)} %compare.26, f32[8,256,256]{2,1,0:T(8,128)} %get-tuple-element.711, s32[]{:T(128)} %get-tuple-element.702), kind=kOutput, calls=%fused_computation.8.clone.1 | convolution fusion | flops 12893290496 | bytes 50594304 | tf_op jit(solution)/shard_map/while/body/eval_jaxpr/dot_general | solution.py:157
  553.9 57.4 %multiply_add_fusion.4 = f32[256,128,128]{2,1,0:T(8,128)} fusion(f32[256,128]{1,0:T(8,128)S(1)} %add_bitcast_fusion.26, f32[256,128]{1,0:T(8,128)S(1)} %get-tuple-element.551, f32[256,128]{1,0:T(8,128)S(1)} %add_bitcast_fusion.27, f32[256,128]{1,0:T(8,128)S(1)} %get-tuple-element.564, f32[256,128]{1,0:T(8,128)S(1)} %add_bitcast_fusion.28, ...), kind=kLoop, calls=%fused_computation.11.clone.1 | loop fusion | flops 96468992 | bytes 19922944 | tf_op jit(solution)/shard_map/while/body/eval_jaxpr/add | solution.py:153
  611.4 32.4 %convolution_add_fusion.2 = f32[256,16384]{1,0:T(8,128)} fusion(f32[32,8,128,128]{3,2,1,0:T(8,128)} %bitcast.617, f32[256,16384]{1,0:T(8,128)} %get-tuple-element.703, pred[]{:T(512)S(6)} %compare.26, f32[8,256,256]{2,1,0:T(8,128)} %get-tuple-element.711, s32[]{:T(128)} %get-tuple-element.702), kind=kOutput, calls=%fused_computation.8.clone.1 | convolution fusion | flops 12893290496 | bytes 50594304 | tf_op jit(solution)/shard_map/while/body/eval_jaxpr/dot_general | solution.py:157
  664.6 57.4 %multiply_add_fusion.4 = f32[256,128,128]{2,1,0:T(8,128)} fusion(f32[256,128]{1,0:T(8,128)S(1)} %add_bitcast_fusion.26, f32[256,128]{1,0:T(8,128)S(1)} %get-tuple-element.551, f32[256,128]{1,0:T(8,128)S(1)} %add_bitcast_fusion.27, f32[256,128]{1,0:T(8,128)S(1)} %get-tuple-element.564, f32[256,128]{1,0:T(8,128)S(1)} %add_bitcast_fusion.28, ...), kind=kLoop, calls=%fused_computation.11.clone.1 | loop fusion | flops 96468992 | bytes 19922944 | tf_op jit(solution)/shard_map/while/body/eval_jaxpr/add | solution.py:153
  722.0 32.4 %convolution_add_fusion.2 = f32[256,16384]{1,0:T(8,128)} fusion(f32[32,8,128,128]{3,2,1,0:T(8,128)} %bitcast.617, f32[256,16384]{1,0:T(8,128)} %get-tuple-element.703, pred[]{:T(512)S(6)} %compare.26, f32[8,256,256]{2,1,0:T(8,128)} %get-tuple-element.711, s32[]{:T(128)} %get-tuple-element.702), kind=kOutput, calls=%fused_computation.8.clone.1 | convolution fusion | flops 12893290496 | bytes 50594304 | tf_op jit(solution)/shard_map/while/body/eval_jaxpr/dot_general | solution.py:157
  775.2 57.4 %multiply_add_fusion.4 = f32[256,128,128]{2,1,0:T(8,128)} fusion(f32[256,128]{1,0:T(8,128)S(1)} %add_bitcast_fusion.26, f32[256,128]{1,0:T(8,128)S(1)} %get-tuple-element.551, f32[256,128]{1,0:T(8,128)S(1)} %add_bitcast_fusion.27, f32[256,128]{1,0:T(8,128)S(1)} %get-tuple-element.564, f32[256,128]{1,0:T(8,128)S(1)} %add_bitcast_fusion.28, ...), kind=kLoop, calls=%fused_computation.11.clone.1 | loop fusion | flops 96468992 | bytes 19922944 | tf_op jit(solution)/shard_map/while/body/eval_jaxpr/add | solution.py:153
  832.7 32.4 %convolution_add_fusion.2 = f32[256,16384]{1,0:T(8,128)} fusion(f32[32,8,128,128]{3,2,1,0:T(8,128)} %bitcast.617, f32[256,16384]{1,0:T(8,128)} %get-tuple-element.703, pred[]{:T(512)S(6)} %compare.26, f32[8,256,256]{2,1,0:T(8,128)} %get-tuple-element.711, s32[]{:T(128)} %get-tuple-element.702), kind=kOutput, calls=%fused_computation.8.clone.1 | convolution fusion | flops 12893290496 | bytes 50594304 | tf_op jit(solution)/shard_map/while/body/eval_jaxpr/dot_general | solution.py:157
  885.9 57.4 %multiply_add_fusion.4 = f32[256,128,128]{2,1,0:T(8,128)} fusion(f32[256,128]{1,0:T(8,128)S(1)} %add_bitcast_fusion.26, f32[256,128]{1,0:T(8,128)S(1)} %get-tuple-element.551, f32[256,128]{1,0:T(8,128)S(1)} %add_bitcast_fusion.27, f32[256,128]{1,0:T(8,128)S(1)} %get-tuple-element.564, f32[256,128]{1,0:T(8,128)S(1)} %add_bitcast_fusion.28, ...), kind=kLoop, calls=%fused_computation.11.clone.1 | loop fusion | flops 96468992 | bytes 19922944 | tf_op jit(solution)/shard_map/while/body/eval_jaxpr/add | solution.py:153
  943.3 32.4 %convolution_add_fusion.2 = f32[256,16384]{1,0:T(8,128)} fusion(f32[32,8,128,128]{3,2,1,0:T(8,128)} %bitcast.617, f32[256,16384]{1,0:T(8,128)} %get-tuple-element.703, pred[]{:T(512)S(6)} %compare.26, f32[8,256,256]{2,1,0:T(8,128)} %get-tuple-element.711, s32[]{:T(128)} %get-tuple-element.702), kind=kOutput, calls=%fused_computation.8.clone.1 | convolution fusion | flops 12893290496 | bytes 50594304 | tf_op jit(solution)/shard_map/while/body/eval_jaxpr/dot_general | solution.py:157
  996.5 57.4 %multiply_add_fusion.4 = f32[256,128,128]{2,1,0:T(8,128)} fusion(f32[256,128]{1,0:T(8,128)S(1)} %add_bitcast_fusion.26, f32[256,128]{1,0:T(8,128)S(1)} %get-tuple-element.551, f32[256,128]{1,0:T(8,128)S(1)} %add_bitcast_fusion.27, f32[256,128]{1,0:T(8,128)S(1)} %get-tuple-element.564, f32[256,128]{1,0:T(8,128)S(1)} %add_bitcast_fusion.28, ...), kind=kLoop, calls=%fused_computation.11.clone.1 | loop fusion | flops 96468992 | bytes 19922944 | tf_op jit(solution)/shard_map/while/body/eval_jaxpr/add | solution.py:153
  1054.0 32.4 %convolution_add_fusion.2 = f32[256,16384]{1,0:T(8,128)} fusion(f32[32,8,128,128]{3,2,1,0:T(8,128)} %bitcast.617, f32[256,16384]{1,0:T(8,128)} %get-tuple-element.703, pred[]{:T(512)S(6)} %compare.26, f32[8,256,256]{2,1,0:T(8,128)} %get-tuple-element.711, s32[]{:T(128)} %get-tuple-element.702), kind=kOutput, calls=%fused_computation.8.clone.1 | convolution fusion | flops 12893290496 | bytes 50594304 | tf_op jit(solution)/shard_map/while/body/eval_jaxpr/dot_general | solution.py:157
  1086.6 14.2 %copy.133 = f32[32,8,128,128]{3,2,1,0:T(8,128)} copy(f32[32,8,128,128]{3,1,2,0:T(8,128)} %bitcast.618) | data formatting | bytes 33554432
  1101.8 10.8 gather_fusion
  1113.7 8.2 multiply_reduce_fusion.1
  1123.0 22.7 %scatter_custom_fusion.4 = f32[2064,8]{1,0:T(8,128)S(1)} fusion(s32[4096]{0:T(1024)} %bitcast.816, f32[4096,8]{1,0:T(8,128)S(1)} %reshape.2174, f32[]{:T(128)} %constant.151.clone.1), kind=kCustom, calls=%fused_computation.69 | custom fusion | flops 32768 | bytes 66560 | tf_op jit(solution)/shard_map/scatter-add | solution.py:192
  1153.2 37.1 %psum.36 = f32[]{:T(128)} all-reduce(f32[]{:T(128)} %multiply_reduce_fusion.9), channel_id=1, replica_groups=mesh['trk'=8,'mod'=4] {'trk','mod'}, use_global_device_ids=true, to_apply=%region_19.20 | all-reduce | flops 1 | bytes 8 | tf_op jit(solution)/shard_map/psum | solution.py:65
  1191.6 41.3 %psum.37 = f32[]{:T(128)} all-reduce(f32[]{:T(128)} %get-tuple-element.140), channel_id=1, replica_groups=mesh['trk'=8,'mod'=4] {'trk','mod'}, use_global_device_ids=true, to_apply=%region_21.22 | all-reduce | flops 1 | bytes 8 | tf_op jit(solution)/shard_map/psum | solution.py:65
  1237.5 11.0 gather_fusion.1
  1249.5 8.2 multiply_reduce_fusion
  1258.9 22.7 %scatter_custom_fusion.5 = f32[2064,8]{1,0:T(8,128)S(1)} fusion(s32[4096]{0:T(1024)} %bitcast.817, f32[4096,8]{1,0:T(8,128)S(1)} %reshape.2182, f32[]{:T(128)} %constant.151.clone.1), kind=kCustom, calls=%fused_computation.67 | custom fusion | flops 32768 | bytes 66560 | tf_op jit(solution)/shard_map/scatter-add | solution.py:192
  1289.1 37.0 %psum.38 = f32[]{:T(128)} all-reduce(f32[]{:T(128)} %multiply_reduce_fusion.7), channel_id=1, replica_groups=mesh['trk'=8,'mod'=4] {'trk','mod'}, use_global_device_ids=true, to_apply=%region_25.26 | all-reduce | flops 1 | bytes 8 | tf_op jit(solution)/shard_map/psum | solution.py:65
  1330.0 41.4 %psum.39 = f32[]{:T(128)} all-reduce(f32[]{:T(128)} %multiply_reduce_fusion.6), channel_id=1, replica_groups=mesh['trk'=8,'mod'=4] {'trk','mod'}, use_global_device_ids=true, to_apply=%region_27.28 | all-reduce | flops 1 | bytes 8 | tf_op jit(solution)/shard_map/psum | solution.py:65
  (1307 shorter events, 257.1 us)
Async XLA Ops:
  0.6 16.9 %copy-start.69 = (s32[12,512]{1,0:T(8,128)S(1)}, s32[12,512]{1,0:T(8,128)}, u32[]{:S(2)}) copy-start(s32[12,512]{1,0:T(8,128)} %param.21) | copy-start | bytes 73732
  6.0 14.8 %all-to-all-start = ((s32[32,64,1]{1,2,0:T(1,128)}), s32[32,64,1]{1,2,0:T(1,128)S(1)}, u32[]{:S(2)}, u32[]{:S(2)}) async-start(s32[32,64,1]{1,2,0:T(1,128)} %all_to_all.22), calls=%async_computation | async-start | bytes 32768 | tf_op jit(solution)/shard_map/all_to_all | solution.py:120
  17.4 9.3 copy-start.70
  17.7 9.3 copy-start.10
  20.9 13.7 all-to-all-start.1
  34.5 52.0 %all-to-all-start.2 = ((f32[32,64,252]{2,1,0:T(8,128)}), f32[32,64,252]{2,1,0:T(8,128)S(1)}, u32[]{:S(2)}, u32[]{:S(2)}) async-start(f32[32,64,252]{2,1,0:T(8,128)} %bitcast.635), calls=%async_computation.2 | async-start | bytes 4194304 | tf_op jit(solution)/shard_map/all_to_all | solution.py:118
  38.7 63.9 %copy-start.71 = (s32[4096,1]{0,1:T(1,128)}, s32[4096,1]{0,1:T(1,128)S(1)}, u32[]{:S(2)}) copy-start(s32[4096,1]{0,1:T(1,128)S(1)} %compare_select_fusion.1) | copy-start | bytes 49156
  125.6 21.6 %collective-permute-start = (f32[16,8]{0,1:T(8,128)S(1)}, f32[16,8]{0,1:T(8,128)S(1)}, u32[]{:S(2)}, u32[]{:S(2)}) collective-permute-start(f32[16,8]{0,1:T(8,128)S(1)} %copy.122), channel_id=1, source_target_pairs={{0,1},{1,2},{2,3},{3,4},{4,5},{5,6},{6,7},{7,8},{8,9},{9,10},{10,1... | collective-permute-start | bytes 1544 | tf_op jit(solution)/shard_map/ppermute | solution.py:19
  130.9 15.5 %copy-start = (f32[2048,144]{1,0:T(8,128)S(1)}, f32[2048,144]{1,0:T(8,128)}, u32[]{:S(2)}) copy-start(f32[2048,144]{1,0:T(8,128)} %slice.1145) | copy-start | bytes 3538948
  147.5 43.5 %copy-start.3 = (f32[2048,8]{0,1:T(8,128)}, f32[2048,8]{0,1:T(8,128)S(1)}, u32[]{:S(2)}) copy-start(f32[2048,8]{0,1:T(8,128)S(1)} %scatter-add.37) | copy-start | bytes 196612
  188.3 912.5 %collective-permute-start.1 = (f32[16,8]{0,1:T(8,128)}, f32[16,8]{0,1:T(8,128)}, u32[]{:S(2)}, u32[]{:S(2)}) collective-permute-start(f32[16,8]{0,1:T(8,128)} %slice.1150), channel_id=1, source_target_pairs={{0,31},{1,0},{2,1},{3,2},{4,3},{5,4},{6,5},{7,6},{8,7},{9,8},{10,9... | collective-permute-start | bytes 1544 | tf_op jit(solution)/shard_map/ppermute | solution.py:19
  202.4 4.7 copy-start.5
  280.6 31.2 %copy-start.6 = (f32[8,256,12,12]{1,0,3,2:T(8,128)S(1)}, f32[8,256,12,12]{1,0,3,2:T(8,128)}, u32[]{:S(2)}) copy-start(f32[8,256,12,12]{1,0,3,2:T(8,128)} %copy-done.5) | copy-start | bytes 3538948 | tf_op jit(solution)/shard_map/while
  311.8 4.6 copy-start.5
  390.1 32.4 %copy-start.6 = (f32[8,256,12,12]{1,0,3,2:T(8,128)S(1)}, f32[8,256,12,12]{1,0,3,2:T(8,128)}, u32[]{:S(2)}) copy-start(f32[8,256,12,12]{1,0,3,2:T(8,128)} %copy-done.5) | copy-start | bytes 3538948 | tf_op jit(solution)/shard_map/while
  422.5 4.6 copy-start.5
  500.7 32.4 %copy-start.6 = (f32[8,256,12,12]{1,0,3,2:T(8,128)S(1)}, f32[8,256,12,12]{1,0,3,2:T(8,128)}, u32[]{:S(2)}) copy-start(f32[8,256,12,12]{1,0,3,2:T(8,128)} %copy-done.5) | copy-start | bytes 3538948 | tf_op jit(solution)/shard_map/while
  533.1 4.6 copy-start.5
  611.4 32.4 %copy-start.6 = (f32[8,256,12,12]{1,0,3,2:T(8,128)S(1)}, f32[8,256,12,12]{1,0,3,2:T(8,128)}, u32[]{:S(2)}) copy-start(f32[8,256,12,12]{1,0,3,2:T(8,128)} %copy-done.5) | copy-start | bytes 3538948 | tf_op jit(solution)/shard_map/while
  643.8 4.6 copy-start.5
  722.0 32.4 %copy-start.6 = (f32[8,256,12,12]{1,0,3,2:T(8,128)S(1)}, f32[8,256,12,12]{1,0,3,2:T(8,128)}, u32[]{:S(2)}) copy-start(f32[8,256,12,12]{1,0,3,2:T(8,128)} %copy-done.5) | copy-start | bytes 3538948 | tf_op jit(solution)/shard_map/while
  754.4 4.6 copy-start.5
  832.7 32.4 %copy-start.6 = (f32[8,256,12,12]{1,0,3,2:T(8,128)S(1)}, f32[8,256,12,12]{1,0,3,2:T(8,128)}, u32[]{:S(2)}) copy-start(f32[8,256,12,12]{1,0,3,2:T(8,128)} %copy-done.5) | copy-start | bytes 3538948 | tf_op jit(solution)/shard_map/while
  943.3 32.4 %copy-start.6 = (f32[8,256,12,12]{1,0,3,2:T(8,128)S(1)}, f32[8,256,12,12]{1,0,3,2:T(8,128)}, u32[]{:S(2)}) copy-start(f32[8,256,12,12]{1,0,3,2:T(8,128)} %copy-done.5) | copy-start | bytes 3538948 | tf_op jit(solution)/shard_map/while
  1054.0 32.4 %copy-start.6 = (f32[8,256,12,12]{1,0,3,2:T(8,128)S(1)}, f32[8,256,12,12]{1,0,3,2:T(8,128)}, u32[]{:S(2)}) copy-start(f32[8,256,12,12]{1,0,3,2:T(8,128)} %copy-done.5) | copy-start | bytes 3538948 | tf_op jit(solution)/shard_map/while
  1086.6 14.2 %copy-start.9 = (f32[2048,8]{0,1:T(8,128)S(1)}, f32[2048,8]{0,1:T(8,128)}, u32[]{:S(2)}) copy-start(f32[2048,8]{0,1:T(8,128)} %copy-done.8) | copy-start | bytes 196612
  1086.6 15.2 %copy-start.1 = (s32[4096]{0:T(1024)S(1)}, s32[4096]{0:T(1024)}, u32[]{:S(2)}) copy-start(s32[4096]{0:T(1024)} %broadcast_clamp_fusion) | copy-start | bytes 49156
  1123.0 29.6 %copy-start.4 = (f32[2048,8]{0,1:T(8,128)S(1)}, f32[2048,8]{0,1:T(8,128)}, u32[]{:S(2)}) copy-start(f32[2048,8]{0,1:T(8,128)} %copy-done.3) | copy-start | bytes 196612
  1123.0 29.6 %copy-start.7 = (f32[2048,8]{0,1:T(8,128)S(1)}, f32[2048,8]{0,1:T(8,128)}, u32[]{:S(2)}) copy-start(f32[2048,8]{0,1:T(8,128)} %param.25) | copy-start | bytes 196612
  1145.8 6.6 collective-permute-start.2
  1233.6 3.5 collective-permute-start.3
  1281.7 6.6 collective-permute-start.4
  (469 other events, 888.1 us)
where the time goes:
time: 1380 us; the launch traced here: 1370 us
  other arithmetic  633 us (46%)
  matrix products  261 us (19%)
  blocking collectives  195 us (14%)
  local copies, waits for them, and re-layouts  179 us (13%)
  waiting for transfers between devices  55.2 us (4%)
  starting transfers between devices  21.7 us (2%)
  loops' own time  20 us (1%)
    add x8, other arithmetic, accumulate(): outer = outer + part_laid[:, row_num][:, :, None] * mixed_row[:, None, :]  459 us
    dot_general x8, matrix products, accumulate(): jnp.dot(part_road.T, flat_outer, precision=HIGHEST, preferred_element_typ...  258 us
    psum x5, blocking collectives, global_sum(): return lax.psum(local_term, ('trk', 'mod'))  195 us
    mul x96, other arithmetic, accumulate(): outer = outer + part_laid[:, row_num][:, :, None] * mixed_row[:, None, :]  62.5 us
    dynamic_slice x32, local copies, waits for them, and re-layouts, on_device(): lax.scan(accumulate, start_total, (laid.reshape(block_count, rows_each, N...  56.4 us
    scatter-add x2, other arithmetic, apply_normal(): jnp.zeros_like(extended_vec).at[gather_index.reshape(-1)]  45.4 us
    all_to_all x1, waiting for transfers between devices, on_device(): lax.all_to_all(send_values, ('trk', 'mod'), split_axis=0, concat_axis=0,...  39.4 us
    slice x64, local copies, waits for them, and re-layouts, accumulate(): part_schur[:, row_num, col_num][:, None] * part_laid[:, col_num]  36.1 us
  transfers between devices with their start and end apart: 8, of which 5 were waited for; matrix products, arithmetic and copies ran while one was open for 68% of the time, Pallas kernels for 0%

commit v1 on v0

v1 whole, which is shorter than its diff:
```python
import functools

import jax
import jax.numpy as jnp
from jax import lax
from jax.experimental import pallas as pl
from jax.experimental.pallas import tpu as pltpu
from jax.sharding import PartitionSpec as P

NPAR = 8
NHIT = 12
NLOC = 5
ROAD = 16
LANES = 128
EPS = 1e-06
AXES = ("trk", "mod")

W_SOLVED = NHIT * NPAR
W_SLOT = W_SOLVED + NHIT
W_ROAD = W_SLOT + NHIT
W_PROJ0 = W_ROAD + 1
W_PROJ1 = W_PROJ0 + 1
W_PROJ = W_PROJ1 + 2
WORDS = W_PROJ + NLOC * (NHIT - 2)

PER_ITEM = 8
UNROLL = 4
GROUPS = 8
F32 = jnp.float32
BF16 = jnp.bfloat16


def iota(shape, dim):
    return lax.broadcasted_iota(jnp.int32, shape, dim)


def dot(lhs, rhs, lhs_dim, rhs_dim):
    return lax.dot_general(
        lhs, rhs, (((lhs_dim,), (rhs_dim,)), ((), ())), preferred_element_type=F32
    )


def split_three(value):
    high = value.astype(BF16)
    rest = value - high.astype(F32)
    middle = rest.astype(BF16)
    low = (rest - middle.astype(F32)).astype(BF16)
    return high, middle, low


def householder(rows, first, column):
    vector = [row[column : column + 1] for row in rows[first:]]
    norm = jnp.sqrt(sum(part * part for part in vector))
    vector[0] = vector[0] + jnp.where(vector[0] >= 0.0, norm, -norm)
    square = sum(part * part for part in vector)
    scale = jnp.where(square > 1e-30, 2.0 / jnp.maximum(square, 1e-30), 0.0)
    along = sum(part * row for part, row in zip(vector, rows[first:])) * scale
    return rows[:first] + [row - part * along for part, row in zip(vector, rows[first:])]


def send_kernel(
    cap, road_dev, rows_each, ld_ref, gd_ref, me_ref, hw_ref, hm_ref, hc_ref, tr_ref, trc_ref,
    out_ref, words_ref, parts_ref,
):
    tracks = hc_ref.shape[1]
    split = LANES // cap
    words_all = rows_each * split
    weight = jnp.where(iota((NHIT, tracks), 0) < hc_ref[...], hw_ref[...], 0.0)
    root = jnp.sqrt(weight)
    scaled = [ld_ref[a] * root for a in range(NLOC)]
    factor = {}
    for a in range(NLOC):
        for b in range(a + 1):
            running = jnp.sum(scaled[a] * scaled[b], axis=0, keepdims=True)
            if a == b:
                running = running + 1.0
            for c in range(b):
                running = running - factor[a, c] * factor[b, c]
            factor[a, b] = jnp.sqrt(running) if a == b else running / factor[b, b]
    proj = []
    for a in range(NLOC):
        running = scaled[a]
        for b in range(a):
            running = running - factor[a, b] * proj[b]
        proj.append(running / factor[a, a])
    residual = me_ref[...] * root
    solved = residual
    for a in range(NLOC):
        solved = solved - proj[a] * jnp.sum(proj[a] * residual, axis=0, keepdims=True)
    proj = householder(proj, 0, 0)
    proj = householder(proj, 1, 1)
    for i in range(NHIT):
        words_ref[i * NPAR : (i + 1) * NPAR, :] = gd_ref[:, i, :] * root[i : i + 1]
    words_ref[W_SOLVED:W_SLOT, :] = solved
    words_ref[W_SLOT:W_ROAD, :] = (hm_ref[...] & (ROAD - 1)).astype(F32)
    owner = tr_ref[...] // road_dev
    words_ref[W_ROAD:W_PROJ0, :] = (tr_ref[...] - owner * road_dev + 1).astype(F32)
    words_ref[W_PROJ0:W_PROJ1, :] = proj[0][0:1]
    words_ref[W_PROJ1 : W_PROJ1 + 1, :] = proj[0][1:2]
    words_ref[W_PROJ1 + 1 : W_PROJ, :] = proj[1][1:2]
    for a in range(NLOC):
        at = W_PROJ + a * (NHIT - 2)
        words_ref[at : at + NHIT - 2, :] = proj[a][2:]
    words_ref[WORDS:, :] = jnp.zeros((words_all - WORDS, tracks), F32)
    for num, part in enumerate(split_three(words_ref[...])):
        parts_ref[num * words_all : (num + 1) * words_all, :] = part
    owner_col = trc_ref[...] // road_dev
    earlier = iota((tracks, tracks), 0) < iota((tracks, tracks), 1)
    same = jnp.where(jnp.logical_and(owner_col == owner, earlier), 1.0, 0.0)
    rank = jnp.sum(same, axis=0, keepdims=True).astype(jnp.int32)
    target = owner * cap + rank
    blocks = out_ref.shape[0] // split
    lane_part = iota((rows_each, LANES), 1) // cap
    per = 2
    for pair in range(blocks // per):
        hot = jnp.where(
            target == iota((per * LANES, tracks), 0) + pair * per * LANES, 1.0, 0.0
        ).astype(BF16)
        moved = dot(parts_ref[...], hot, 1, 1)
        moved = moved[:words_all] + moved[words_all : 2 * words_all] + moved[2 * words_all :]
        for sub in range(per):
            block = moved[:, sub * LANES : (sub + 1) * LANES]
            for k in range(split):
                made = None
                for m in range(split):
                    piece = block[m * rows_each : (m + 1) * rows_each]
                    if m != k:
                        piece = pltpu.roll(piece, (cap * (m - k)) % LANES, 1)
                    made = piece if made is None else jnp.where(lane_part == m, piece, made)
                out_ref[(pair * per + sub) * split + k] = made


def sort_kernel(cap, recv_ref, off_ref, list_ref, item_ref, bound_ref, off_out_ref, road_ref):
    split = LANES // cap
    roads = off_ref.shape[0]
    blocks = road_ref.shape[0]
    lane_part = iota((1, LANES), 1) // cap
    shift_of = road_part(cap)
    for e in range(blocks):
        made = None
        for k in range(split):
            piece = recv_ref[e * split + k, 0:1, :]
            if k != shift_of:
                piece = pltpu.roll(piece, (cap * (k - shift_of)) % LANES, 1)
            made = piece if made is None else jnp.where(lane_part == k, piece, made)
        road_ref[e : e + 1, :] = made
    road_num = (iota((roads, LANES), 0) + 1).astype(F32)
    upper = jnp.where(iota((LANES, LANES), 0) < iota((LANES, LANES), 1), 1.0, 0.0).astype(BF16)
    offset = off_ref[...]
    counts = jnp.zeros((roads, 1), F32)
    ranks = []
    for e in range(blocks):
        hot = jnp.where(road_ref[e : e + 1, :] == road_num, 1.0, 0.0)
        before = dot(hot.astype(BF16), upper, 1, 0) + counts
        ranks.append(jnp.sum(hot * before, axis=0, keepdims=True))
        off_out_ref[e : e + 1, :] = jnp.sum(hot * offset, axis=0, keepdims=True)
        counts = counts + jnp.sum(hot, axis=1, keepdims=True)
    items = jnp.maximum(jnp.floor((counts + (PER_ITEM - 1)) * (1.0 / PER_ITEM)), 1.0)
    items = jnp.broadcast_to(items, (roads, LANES))
    lower = jnp.where(iota((roads, roads), 1) < iota((roads, roads), 0), 1.0, 0.0).astype(BF16)
    begin = dot(lower, items.astype(BF16), 1, 0)
    rows = list_ref.shape[0]
    total = jnp.zeros((rows, 2 * LANES), F32)
    row_num = iota((rows, LANES), 0).astype(F32)
    lane_num = iota((LANES, LANES), 0).astype(F32)
    track_lane = iota((1, LANES), 1).astype(F32)
    for e in range(blocks):
        road = road_ref[e : e + 1, :]
        hot = jnp.where(road == road_num, 1.0, 0.0)
        place = PER_ITEM * jnp.sum(hot * begin, axis=0, keepdims=True) + ranks[e]
        place = jnp.where(road > 0.5, place, -1.0)
        high = jnp.floor(place * (1.0 / LANES))
        low = place - high * LANES
        pick = jnp.where(high == row_num, 1.0, 0.0).astype(BF16)
        match = low == lane_num
        values = jnp.concatenate(
            [jnp.where(match, float(e + 1), 0.0), jnp.where(match, track_lane, 0.0)], axis=0
        )
        total = total + dot(pick, values.astype(BF16), 1, 1)
    found = total[:, :LANES]
    track = jnp.where(found > 0.5, (found - 1.0) * LANES + total[:, LANES:], float(blocks * LANES))
    list_ref[...] = track.astype(jnp.int32)
    item_rows = item_ref.shape[0]
    for row in range(item_rows):
        item = (iota((1, LANES), 1) + row * LANES).astype(F32)
        road = jnp.sum(jnp.where(begin <= item, 1.0, 0.0), axis=0, keepdims=True) - 1.0
        first = jnp.sum(jnp.where(begin == item, 1.0, 0.0), axis=0, keepdims=True)
        item_ref[row : row + 1, :] = (2.0 * road + first).astype(jnp.int32)
    each = roads // GROUPS
    begins = jnp.where(iota((roads, LANES), 0) == iota((roads, LANES), 1) * each, begin, 0.0)
    bound = jnp.sum(begins, axis=0, keepdims=True)
    last = jnp.sum(items, axis=0, keepdims=True)
    bound = jnp.where(iota((1, LANES), 1) < GROUPS, bound, last)
    bound_ref[...] = jnp.broadcast_to(bound, bound_ref.shape).astype(jnp.int32)


def rows_of(cap):
    split = LANES // cap
    least = -(-WORDS // split)
    return -(-least // 8) * 8


def road_part(cap):
    return W_ROAD // rows_of(cap)


def blocks_kernel(
    cap, bound_ref, list_ref, item_ref, recv_ref, off_ref, out_ref, sums_ref, tiles_ref, words_ref,
    held_ref,
):
    group = pl.program_id(0)
    each = out_ref.shape[0]
    split = LANES // cap
    rows_each = recv_ref.shape[1]
    blocks = off_ref.shape[0]
    width = ROAD * NPAR

    @pl.when(group == 0)
    def _():
        lane_part = iota((rows_each, LANES), 1) // cap
        tiles_ref[blocks * LANES] = jnp.zeros((8, width), F32)

        def lay(e, carry):
            for m in range(split):
                made = None
                for k in range(split):
                    piece = recv_ref[e * split + k]
                    if k != m:
                        piece = pltpu.roll(piece, (cap * (k - m)) % LANES, 1)
                    made = piece if made is None else jnp.where(lane_part == k, piece, made)
                words_ref[m * rows_each : (m + 1) * rows_each, :] = made
            offset = off_ref[pl.ds(e, 1), :]
            slots = []
            for i in range(NHIT):
                slot = words_ref[W_SLOT + i : W_SLOT + i + 1, :] - offset
                slots.append(jnp.where(slot < 0.0, slot + ROAD, slot))
            laid = [jnp.zeros((NPAR, LANES), F32) for s in range(ROAD)]
            for i in range(NHIT):
                value = words_ref[i * NPAR : (i + 1) * NPAR, :]
                wide = jnp.broadcast_to(slots[i], (NPAR, LANES))
                for s in range(ROAD):
                    laid[s] = jnp.where(wide == float(s), value, laid[s])
            slot_num = iota((ROAD, LANES), 0).astype(F32)
            placed = [jnp.zeros((ROAD, LANES), F32) for a in range(NLOC + 1)]
            for i in range(NHIT):
                match = slots[i] == slot_num
                for a in range(NLOC + 1):
                    if a == NLOC:
                        at = W_SOLVED + i
                    elif i == 0:
                        at = W_PROJ0 if a == 0 else None
                    elif i == 1:
                        at = W_PROJ1 + a if a < 2 else None
                    else:
                        at = W_PROJ + a * (NHIT - 2) + i - 2
                    if at is not None:
                        placed[a] = jnp.where(match, words_ref[at : at + 1, :], placed[a])
            start = pl.multiple_of(e * LANES, LANES)
            for a in range(NLOC + 1):
                mixed = jnp.concatenate(
                    [laid[s] * placed[a][s : s + 1] for s in range(ROAD)], axis=0
                )
                at = a if a < NLOC else NLOC + 1
                tiles_ref[pl.ds(start, LANES), at, :] = mixed.T
            tiles_ref[pl.ds(start, LANES), NLOC, :] = jnp.concatenate(laid, axis=0).T
            tiles_ref[pl.ds(start, LANES), NLOC + 2, :] = jnp.zeros((LANES, width), F32)
            return carry

        lax.fori_loop(0, blocks, lay, 0)

    row_kind = iota((PER_ITEM * 8, width), 0) % 8
    is_proj = row_kind < NLOC
    is_own = row_kind == NLOC
    same_slot = iota((width, width), 0) // NPAR == iota((width, width), 1) // NPAR
    begin = bound_ref[0, group]
    end = bound_ref[0, group + 1]

    def step(num, carry):
        for u in range(UNROLL):
            item = begin + num * UNROLL + u
            live = item < end
            item = jnp.minimum(item, end - 1)
            info = item_ref[item // LANES, item % LANES]
            road = info // 2
            first = jnp.logical_and(info % 2 == 1, live)
            local = road - group * each
            at = item * PER_ITEM
            parts = []
            for j in range(PER_ITEM):
                track = list_ref[(at + j) // LANES, (at + j) % LANES]
                track = jnp.where(live, track, blocks * LANES)
                parts.append(tiles_ref[track])
            tall = jnp.concatenate(parts, axis=0)
            high = tall.astype(BF16)
            high32 = high.astype(F32)
            low32 = tall - high32
            low = low32.astype(BF16)
            left = jnp.concatenate([high, high, low], axis=0)
            high_p = jnp.where(is_proj, high32, 0.0).astype(BF16)
            high_o = jnp.where(is_own, high32, 0.0).astype(BF16)
            low_p = jnp.where(is_proj, low32, 0.0).astype(BF16)
            low_o = jnp.where(is_own, low32, 0.0).astype(BF16)
            right = jnp.concatenate(
                [
                    jnp.concatenate([high_p, low_p, high_p], axis=0),
                    jnp.concatenate([high_o, low_o, high_o], axis=0),
                ],
                axis=1,
            )
            both = dot(left, right, 0, 0)
            value = jnp.where(same_slot, both[:, width:], 0.0) - both[:, :width]
            out_ref[local] = value + jnp.where(first, 0.0, out_ref[local])
            added = parts[0]
            for part in parts[1:]:
                added = added + part
            held_ref[local] = added + jnp.where(first, 0.0, held_ref[local])
        return carry

    lax.fori_loop(0, (end - begin + UNROLL - 1) // UNROLL, step, 0)
    sums_ref[...] = held_ref[:, NLOC + 1, :]


def lane_bits(offset, bit):
    return (offset // (1 << bit)) % 2 == 1


def gathered(rows, offset, odd):
    lane = iota(rows.shape, 1)
    here = rows
    there = jnp.concatenate([rows[1:], jnp.zeros((1, LANES), F32)], axis=0)
    if odd:
        half = LANES // 2
        turned_here, turned_there = pltpu.roll(here, half, 1), pltpu.roll(there, half, 1)
        here = jnp.where(lane < LANES - half, turned_here, turned_there)
        there = turned_there
    for bit in range(3):
        step = NPAR << bit
        take = lane_bits(offset, bit)
        turned_here, turned_there = (
            pltpu.roll(here, LANES - step, 1),
            pltpu.roll(there, LANES - step, 1),
        )
        moved = jnp.where(lane < LANES - step, turned_here, turned_there)
        here = jnp.where(take, moved, here)
        there = jnp.where(take, turned_there, there)
    return here


def scattered(rows, offset, odd):
    lane = iota(rows.shape, 1)
    here, there = rows, jnp.zeros_like(rows)
    steps = [(NPAR << bit, bit) for bit in range(3)] + ([(LANES // 2, None)] if odd else [])
    for step, bit in steps:
        turned_here, turned_there = pltpu.roll(here, step, 1), pltpu.roll(there, step, 1)
        new_here = jnp.where(lane < step, 0.0, turned_here)
        new_there = jnp.where(lane < step, turned_here, turned_there)
        if bit is None:
            here, there = new_here, new_there
        else:
            take = lane_bits(offset, bit)
            here = jnp.where(take, new_here, here)
            there = jnp.where(take, new_there, there)
    return here, there


EDGE = 8
NEXT_ROADS = 2
PREV_ROADS = 4


def krylov_kernel(
    blocks_hbm, sums_ref, off_ref, prior_ref, from_prev_ref, from_next_ref,
    first_ref, second_ref, third_ref, dots_ref,
    held, sems, even_sum, odd_sum, even_off, odd_off, prior, even_part, odd_part, turned_even,
    turned_odd, even_out, odd_out, rows_scr,
):
    roads, width = sums_ref.shape
    half = roads // 2
    chunks = sems.shape[0]
    each = roads // chunks
    own = slice(EDGE, EDGE + half)
    total = half + 2 * EDGE
    copies = [
        pltpu.make_async_copy(
            blocks_hbm.at[pl.ds(c * each, each)], held.at[pl.ds(c * each, each)], sems.at[c]
        )
        for c in range(chunks)
    ]
    for copy in copies:
        copy.start()

    two = 2 * EDGE
    at_prev = PREV_ROADS * width
    at_next = NEXT_ROADS * width
    for parity, total_sum, total_off in ((0, even_sum, even_off), (1, odd_sum, odd_off)):
        pick = lambda ref, start, count: ref[pl.ds(start + parity, count, stride=2), :]
        total_sum[0:EDGE] = pick(from_prev_ref, at_prev, EDGE)
        total_sum[own] = pick(sums_ref, 0, half)
        total_sum[EDGE + half :] = pick(from_next_ref, at_next, EDGE)
        total_off[0:EDGE] = pick(from_prev_ref, at_prev + two, EDGE).astype(jnp.int32)
        total_off[own] = pick(off_ref, 0, half).astype(jnp.int32)
        total_off[EDGE + half :] = pick(from_next_ref, at_next + two, EDGE).astype(jnp.int32)
    prior[0:EDGE] = from_prev_ref[at_prev + 2 * two : at_prev + 2 * two + EDGE]
    prior[own] = prior_ref[...]
    prior[EDGE + half :] = from_next_ref[at_next + 2 * two : at_next + 2 * two + EDGE]

    def spread(even, odd):
        even_here, even_there = scattered(even, even_off[...], False)
        odd_here, odd_there = scattered(odd, odd_off[...], True)
        over = even_there + odd_there
        return (
            even_here
            + odd_here
            + jnp.concatenate([jnp.zeros((1, LANES), F32), over[:-1]], axis=0)
        )

    def column_product(tile_at, column):
        acc = None
        for s in range(width // 8):
            term = tile_at(s) * column[s * 8 : (s + 1) * 8]
            acc = term if acc is None else acc + term
        return acc

    def apply(vector, wait):
        even = gathered(vector, even_off[...], False)
        odd = gathered(vector, odd_off[...], True)
        even_part[...] = jnp.zeros_like(even_part)
        odd_part[...] = jnp.zeros_like(odd_part)
        edge_even = jnp.concatenate(
            [even[:EDGE], even[EDGE + half :], jnp.zeros((LANES - 2 * EDGE, LANES), F32)], axis=0
        ).T
        edge_odd = jnp.concatenate(
            [odd[:EDGE], odd[EDGE + half :], jnp.zeros((LANES - 2 * EDGE, LANES), F32)], axis=0
        ).T
        for num in range(PREV_ROADS):
            row = EDGE - PREV_ROADS // 2 + num // 2
            column = (edge_even if num % 2 == 0 else edge_odd)[:, row : row + 1]
            part = even_part if num % 2 == 0 else odd_part
            part[row] = column_product(
                lambda s, num=num: from_prev_ref[num * width + s * 8 : num * width + s * 8 + 8],
                column,
            )
        for num in range(NEXT_ROADS):
            column = (edge_even if num % 2 == 0 else edge_odd)[:, EDGE : EDGE + 1]
            part = even_part if num % 2 == 0 else odd_part
            part[EDGE + half] = column_product(
                lambda s, num=num: from_next_ref[num * width + s * 8 : num * width + s * 8 + 8],
                column,
            )
        turned_even[:, :half] = even[own].T
        turned_odd[:, :half] = odd[own].T
        per = each // 2

        def chunk(c, carry):
            if wait:
                pltpu.make_async_copy(
                    blocks_hbm.at[pl.ds(c * each, each)],
                    held.at[pl.ds(c * each, each)],
                    sems.at[c],
                ).wait()
            columns_even = turned_even[...]
            columns_odd = turned_odd[...]
            for j in range(per):
                for parity, columns, part in (
                    (0, columns_even, even_part),
                    (1, columns_odd, odd_part),
                ):
                    road = c * each + 2 * j + parity
                    part[EDGE + c * per + j] = column_product(
                        lambda s, road=road: held[road, s * 8 : s * 8 + 8, :],
                        columns[:, j : j + 1],
                    )
            turned_even[...] = pltpu.roll(columns_even, columns_even.shape[1] - per, 1)
            turned_odd[...] = pltpu.roll(columns_odd, columns_odd.shape[1] - per, 1)
            return carry

        lax.fori_loop(0, chunks, chunk, 0)
        even = even_part[:, 0, :]
        odd = odd_part[:, 0, :]
        for k in range(1, 8):
            even = even + even_part[:, k, :]
            odd = odd + odd_part[:, k, :]
        return prior[...] * vector + spread(even, odd)

    first = spread(even_sum[...], odd_sum[...])
    second = apply(first, True)
    third = apply(second, False)
    first, second, third = first[own], second[own], third[own]
    first_ref[...] = first
    second_ref[...] = second
    third_ref[...] = third
    lane = iota(dots_ref.shape, 1)
    dots = jnp.zeros(dots_ref.shape, F32)
    pairs = ((first, first), (first, second), (second, second), (second, third), (third, third))
    for num, (one, other) in enumerate(pairs):
        dots = dots + jnp.where(lane == num, jnp.sum(one * other), 0.0)
    dots_ref[...] = dots


def finish_kernel(dots_ref, first_ref, second_ref, out_ref):
    sums = jnp.sum(dots_ref[...], axis=0, keepdims=True)
    s00, s01, s11, s12, s22 = (sums[:, num : num + 1] for num in range(5))
    square_one = s00 + EPS
    beta_one = jnp.sqrt(square_one)
    alpha_one = s01 / square_one
    square_two = (s11 - 2.0 * alpha_one * s01 + alpha_one * alpha_one * s00) / square_one + EPS
    beta_two = jnp.sqrt(square_two)
    scale = 1.0 / (beta_one * beta_two)
    s02 = s11
    cross = s12 - alpha_one * s11 - square_two * s01
    cross = cross - alpha_one * (s02 - alpha_one * s01 - square_two * s00)
    alpha_two = cross * scale * scale
    near = alpha_one + alpha_two
    far = alpha_one * alpha_two - square_two
    square_three = s22 - 2.0 * near * s12 + near * near * s11
    square_three = square_three + 2.0 * far * s02 - 2.0 * near * far * s01 + far * far * s00
    square_three = square_three * scale * scale + EPS
    entry_first = alpha_one * alpha_one + square_two
    entry_cross = beta_two * near
    entry_second = square_two + alpha_two * alpha_two + square_three
    determinant = entry_first * entry_second - entry_cross * entry_cross
    coef_one = beta_one * (entry_second * alpha_one - entry_cross * beta_two) / determinant
    coef_two = beta_one * (entry_first * beta_two - entry_cross * alpha_one) / determinant
    on_second = coef_two * scale
    on_first = coef_one / beta_one - alpha_one * on_second
    out_ref[...] = on_first * first_ref[...] + on_second * second_ref[...]


def neighbour(value, steps):
    count = lax.axis_size(AXES)
    return lax.ppermute(value, AXES, [(s, (s + steps) % count) for s in range(count)])


def shape(*dims, dtype=F32):
    return jax.ShapeDtypeStruct(dims, dtype)


def on_device(
    local_deriv, global_deriv, measured, hit_weight, hit_module, hit_count, track_road, road_start,
    prior_weight,
):
    devices = lax.axis_size(AXES)
    roads = road_start.shape[0]
    tracks = hit_count.shape[0]
    modules = prior_weight.shape[0]
    cap = 4 * tracks // devices
    split = LANES // cap
    rows_each = rows_of(cap)
    slots = devices * cap
    width = ROAD * NPAR
    half = modules // ROAD
    vmem = pl.BlockSpec(memory_space=pltpu.VMEM)
    smem = pl.BlockSpec(memory_space=pltpu.SMEM)
    limit = pltpu.CompilerParams(vmem_limit_bytes=50 * 1024 * 1024)

    send = pl.pallas_call(
        functools.partial(send_kernel, cap, roads, rows_each),
        out_shape=shape(devices, rows_each, LANES),
        in_specs=[vmem] * 8,
        out_specs=vmem,
        scratch_shapes=[
            pltpu.VMEM((rows_each * split, tracks), F32),
            pltpu.VMEM((3 * rows_each * split, tracks), BF16),
        ],
        compiler_params=limit,
        name="fit_and_pack",
    )(
        local_deriv, global_deriv, measured, hit_weight, hit_module, hit_count[None, :],
        track_road[None, :], track_road[:, None],
    )
    recv = lax.all_to_all(send, AXES, split_axis=0, concat_axis=0, tiled=True)

    offset = road_start % ROAD
    list_rows = -(-(PER_ITEM * roads + slots) // (8 * LANES)) * 8
    item_rows = -(-(list_rows * LANES // PER_ITEM) // LANES)
    road_row = W_ROAD % rows_each
    track_list, items, bounds, track_off = pl.pallas_call(
        functools.partial(sort_kernel, cap),
        grid=(1,),
        out_shape=(
            shape(list_rows, LANES, dtype=jnp.int32),
            shape(item_rows, LANES, dtype=jnp.int32),
            shape(8, LANES, dtype=jnp.int32),
            shape(slots // LANES, LANES),
        ),
        in_specs=[
            pl.BlockSpec((devices, 8, LANES), lambda i: (0, road_row // 8, 0)),
            pl.BlockSpec((roads, 1), lambda i: (0, 0)),
        ],
        out_specs=(
            pl.BlockSpec((list_rows, LANES), lambda i: (0, 0)),
            pl.BlockSpec((item_rows, LANES), lambda i: (0, 0)),
            pl.BlockSpec((8, LANES), lambda i: (0, 0)),
            pl.BlockSpec((slots // LANES, LANES), lambda i: (0, 0)),
        ),
        scratch_shapes=[pltpu.VMEM((slots // LANES, LANES), F32)],
        compiler_params=limit,
        name="sort_by_road",
    )(recv, offset.astype(F32)[:, None])

    each = roads // GROUPS
    normal_blocks, sums = pl.pallas_call(
        functools.partial(blocks_kernel, cap),
        grid=(GROUPS,),
        out_shape=(shape(roads, width, width), shape(roads, width)),
        in_specs=[
            smem,
            smem,
            smem,
            pl.BlockSpec((devices, rows_each, LANES), lambda g: (0, 0, 0)),
            pl.BlockSpec((slots // LANES, LANES), lambda g: (0, 0)),
        ],
        out_specs=(
            pl.BlockSpec((each, width, width), lambda g: (g, 0, 0)),
            pl.BlockSpec((each, width), lambda g: (g, 0)),
        ),
        scratch_shapes=[
            pltpu.VMEM((slots + 8, 8, width), F32),
            pltpu.VMEM((rows_each * split, LANES), F32),
            pltpu.VMEM((each, 8, width), F32),
        ],
        compiler_params=limit,
        name="assemble_blocks",
    )(bounds, track_list, items, recv, track_off)

    prior = prior_weight.reshape(half, width)
    off_rows = jnp.broadcast_to((offset % (ROAD // 2)).astype(F32)[:, None], (roads, LANES))
    two = 2 * EDGE
    to_next = jnp.concatenate(
        [
            normal_blocks[-PREV_ROADS:].reshape(-1, width),
            sums[-two:],
            off_rows[-two:],
            prior[-EDGE:],
        ]
    )
    to_prev = jnp.concatenate(
        [
            normal_blocks[:NEXT_ROADS].reshape(-1, width),
            sums[:two],
            off_rows[:two],
            prior[:EDGE],
        ]
    )
    from_prev = neighbour(to_next, 1)
    from_next = neighbour(to_prev, -1)
    total = half + 2 * EDGE
    chunks = 16 if roads >= 256 else 4
    rows = pltpu.VMEM((total, LANES), F32)
    int_rows = pltpu.VMEM((total, LANES), jnp.int32)
    tiles = pltpu.VMEM((total, 8, LANES), F32)
    turned = pltpu.VMEM((LANES, LANES), F32)
    first, second, third, dots = pl.pallas_call(
        krylov_kernel,
        out_shape=(shape(half, width), shape(half, width), shape(half, width), shape(1, LANES)),
        in_specs=[pl.BlockSpec(memory_space=pl.ANY)] + [vmem] * 5,
        out_specs=(vmem,) * 4,
        scratch_shapes=[
            pltpu.VMEM((roads, width, width), F32),
            pltpu.SemaphoreType.DMA((chunks,)),
            rows, rows, int_rows, int_rows, rows, tiles, tiles, turned, turned, rows, rows, rows,
        ],
        compiler_params=limit,
        name="two_products",
    )(normal_blocks, sums, off_rows, prior, from_prev, from_next)
    del third
    everyone = lax.all_to_all(
        jnp.broadcast_to(dots[None], (devices, 1, LANES)), AXES, split_axis=0, concat_axis=0,
        tiled=True,
    )
    corrections = pl.pallas_call(
        finish_kernel,
        out_shape=shape(half, width),
        in_specs=[vmem] * 3,
        out_specs=vmem,
        name="combine",
    )(everyone.reshape(devices, LANES), first, second)
    return (
        normal_blocks, first.reshape(modules, NPAR), corrections.reshape(modules, NPAR),
    )


def solution(mesh):
    track = P(None, None, AXES)
    in_specs = (
        track, track, P(None, AXES), P(None, AXES), P(None, AXES), P(AXES), P(AXES), P(AXES),
        P(AXES, None),
    )
    out_specs = (P(AXES, None, None), P(AXES, None), P(AXES, None))
    return jax.shard_map(
        on_device, mesh=mesh, in_specs=in_specs, out_specs=out_specs, check_vma=False
    )
```

time: 1380 us -> 156 us (0.11)
  other arithmetic: 633 us -> 0.26 us
  matrix products: 261 us -> 0 us
  blocking collectives: 195 us -> 0 us
  local copies, waits for them, and re-layouts: 179 us -> 15.7 us
  Pallas kernels: 0 us -> 71.4 us
  loops' own time: 20 us -> 0 us
    add x14 -> x0, other arithmetic: 460 us -> none  [the longest x8 459 us: accumulate(): outer = outer + part_laid[:, row_num][:, :, None] * mixed_row[:, None, :]]
    dot_general x9 -> x0, matrix products: 261 us -> none  [the longest x8 258 us: accumulate(): jnp.dot(part_road.T, flat_outer, precision=HIGHEST, preferred_element_typ...]
    psum x5 -> x0, blocking collectives: 195 us -> none  [global_sum(): return lax.psum(local_term, ('trk', 'mod'))]
    pallas_call x0 -> x5, Pallas kernels: none -> 71.4 us  [the longest x1 47.2 us: on_device(): pl.pallas_call(functools.partial(blocks_kernel, cap), grid=(GROUPS,), out...]
    scatter-add x3 -> x0, other arithmetic: 68.3 us -> none  [the longest x2 45.4 us: apply_normal(): jnp.zeros_like(extended_vec).at[gather_index.reshape(-1)]]
    mul x98 -> x0, other arithmetic: 64.2 us -> none  [the longest x96 62.5 us: accumulate(): outer = outer + part_laid[:, row_num][:, :, None] * mixed_row[:, None, :]]
    dynamic_slice x32 -> x0, local copies, waits for them, and re-layouts: 56.4 us -> none  [on_device(): lax.scan(accumulate, start_total, (laid.reshape(block_count, rows_each, N...]
    slice x78 -> x9, local copies, waits for them, and re-layouts: 44.8 us -> 2.35 us  [the longest x1 0.97 us: on_device(): normal_blocks[-PREV_ROADS:].reshape(-1, width)]
  transfers between devices with their start and end apart: 8 -> 4, of which waited for: 5 -> 4; matrix products, arithmetic and copies ran while one was open for 68% -> 2% of each run, Pallas kernels for 0% -> 0%
where the time goes in v1:
time: 156 us; the launch traced here: 158 us
  Pallas kernels  71.4 us (46%)
  waiting for transfers between devices  43.1 us (28%)
  starting transfers between devices  26.8 us (17%)
  local copies, waits for them, and re-layouts  15.7 us (10%)
    pallas_call x1, Pallas kernels, on_device(): pl.pallas_call(functools.partial(blocks_kernel, cap), grid=(GROUPS,), out...  47.2 us
    all_to_all x1, waiting for transfers between devices, on_device(): recv = lax.all_to_all(send, AXES, split_axis=0, concat_axis=0, tiled=True)  34.2 us
    pallas_call x1, Pallas kernels, on_device(): pl.pallas_call(krylov_kernel, out_shape=(shape(half, width), shape(half,...  16.8 us
    ppermute x2, starting transfers between devices, neighbour(): lax.ppermute(value, AXES, [(s, (s + steps) % count) for s in range(count)])  15 us
    unnamed x26, local copies, waits for them, and re-layouts  9.02 us
    all_to_all x1, starting transfers between devices, on_device(): recv = lax.all_to_all(send, AXES, split_axis=0, concat_axis=0, tiled=True)  7.29 us
    all_to_all x1, waiting for transfers between devices, on_device(): lax.all_to_all(jnp.broadcast_to(dots[None], (devices, 1, LANES)), AXES, s...  5.63 us
    all_to_all x1, starting transfers between devices, on_device(): lax.all_to_all(jnp.broadcast_to(dots[None], (devices, 1, LANES)), AXES, s...  4.48 us
  transfers between devices with their start and end apart: 4, of which 4 were waited for; matrix products, arithmetic and copies ran while one was open for 2% of the time, Pallas kernels for 0%

profile of v1, /device:TPU:0, one launch (start us, length us, event | category | flops | bytes accessed | tf_op | source)
XLA Modules:
  0.0 158.0 jit_solution(2000905782068031211)
XLA Ops:
  0.6 1.0 copy.26.gd_ref
  1.7 0.8 copy.27.trc_ref
  2.5 0.9 copy-done.1
  3.4 0.8 copy-done.3
  4.2 0.8 copy-done.4
  4.9 0.8 copy-done.5
  5.7 0.7 copy-done.6
  6.4 0.7 copy-done.7
  7.1 3.1 %fit_and_pack.1 = f32[32,88,128]{2,1,0:T(8,128)} custom-call(f32[5,12,512]{2,1,0:T(8,128)S(1)} %copy-done.1, f32[8,12,512]{2,1,0:T(8,128)S(1)} %copy.26.gd_ref, f32[12,512]{1,0:T(8,128)S(1)} %copy-done.3, f32[12,512]{1,0:T(8,128)S(1)} %copy-done.4, s32[12,512]{1,0:T(8,128)S(1)} %copy-done.5, s32[1,512]{1,0:T(1,128)S(1)} %bitcast.10, s32[1,512]{1,0:T(1,128)S(1)} %bitcast.9, ...), custom_call_target="tpu_custom_call" | custom-call | tf_op jit(solution)/shard_map/fit_and_pack/pallas_call | solution.py:556
  10.2 7.3 %all-to-all-start = ((f32[32,88,128]{2,1,0:T(8,128)}), f32[32,88,128]{2,1,0:T(8,128)S(1)}, u32[]{:S(2)}, u32[]{:S(2)}) async-start(f32[32,88,128]{2,1,0:T(8,128)} %fit_and_pack.1), calls=%async_computation | async-start | bytes 2883584 | tf_op jit(solution)/shard_map/all_to_all | solution.py:571
  18.3 34.2 %all-to-all-done.recv_ref = f32[32,88,128]{2,1,0:T(8,128)S(1)} async-done(((f32[32,88,128]{2,1,0:T(8,128)}), f32[32,88,128]{2,1,0:T(8,128)S(1)}, u32[]{:S(2)}, u32[]{:S(2)}) %all-to-all-start) | async-done | bytes 1441824 | tf_op jit(solution)/shard_map/all_to_all | solution.py:571
  52.5 1.9 %sort_by_road.1 = (s32[32,128]{1,0:T(8,128)S(1)}, s32[4,128]{1,0:T(4,128)S(1)}, s32[8,128]{1,0:T(8,128)S(1)}, f32[16,128]{1,0:T(8,128)S(1)}) custom-call(f32[32,88,128]{2,1,0:T(8,128)S(1)} %all-to-all-done.recv_ref, f32[256,1]{1,0:T(8,128)S(1)} %copy.28.off_ref), custom_call_target="tpu_custom_call" | custom-call | tf_op jit(solution)/shard_map/sort_by_road/pallas_call | solution.py:577
  54.4 47.2 %assemble_blocks.1 = (f32[256,128,128]{2,1,0:T(8,128)}, f32[256,128]{1,0:T(8,128)S(1)}) custom-call(s32[8,128]{1,0:T(8,128)S(1)} %get-tuple-element.12.bound_ref, s32[32,128]{1,0:T(8,128)S(1)} %get-tuple-element.13.list_ref, s32[4,128]{1,0:T(4,128)S(1)} %get-tuple-element.14.item_ref, f32[32,88,128]{2,1,0:T(8,128)S(1)} %all-to-all-done.recv_ref, ...), custom_call_target="tpu_custom_call" | custom-call | tf_op jit(solution)/shard_map/assemble_blocks/pallas_call | solution.py:602
  101.6 1.0 slice.32
  102.6 0.9 slice.37
  103.5 0.1 pad_maximum_fusion
  103.9 15.0 %collective-permute-start.1 = (f32[296,128]{1,0:T(8,128)S(1)}, f32[296,128]{1,0:T(8,128)S(1)}, u32[]{:S(2)}, u32[]{:S(2)}) collective-permute-start(f32[296,128]{1,0:T(8,128)S(1)} %pad_maximum_fusion.1), channel_id=1, source_target_pairs={{0,31},{1,0},{2,1},{3,2},{4,3},{5,4},{6,5},{7,6},{8,7},{9,8},{10,9... | collective-permute-start | bytes 454664 | tf_op jit(solution)/shard_map/ppermute | solution.py:531
  118.8 0.3 copy.29
  119.2 0.5 reshape.30.prior_ref
  119.7 1.9 %collective-permute-done.1.from_next_ref = f32[296,128]{1,0:T(8,128)S(1)} collective-permute-done((f32[296,128]{1,0:T(8,128)S(1)}, f32[296,128]{1,0:T(8,128)S(1)}, u32[]{:S(2)}, u32[]{:S(2)}) %collective-permute-start.1) | collective-permute-done | bytes 151584 | tf_op jit(solution)/shard_map/ppermute | solution.py:531
  121.5 1.4 collective-permute-done.from_prev_ref
  123.0 16.8 %two_products.1 = (f32[128,128]{1,0:T(8,128)S(1)}, f32[128,128]{1,0:T(8,128)S(1)}, f32[128,128]{1,0:T(8,128)}, f32[1,128]{1,0:T(1,128)S(1)}) custom-call(f32[256,128,128]{2,1,0:T(8,128)} %get-tuple-element.27.blocks_hbm, f32[256,128]{1,0:T(8,128)S(1)} %get-tuple-element.17.sums_ref, f32[256,128]{1,0:T(8,128)S(1)} %broadcast_in_dim.34.off_ref, ...), custom_call_target="tpu_custom_call" | custom-call | tf_op jit(solution)/shard_map/two_products/pallas_call | solution.py:653
  139.9 0.6 copy-done.2
  140.5 0.6 broadcast_in_dim.38
  141.1 4.5 %all-to-all-start.1 = ((f32[32,1,128]{2,1,0:T(1,128)}), f32[32,1,128]{2,1,0:T(1,128)S(1)}, u32[]{:S(2)}, u32[]{:S(2)}) async-start(f32[32,1,128]{2,1,0:T(1,128)} %broadcast_in_dim.38), calls=%async_computation.1 | async-start | bytes 32768 | tf_op jit(solution)/shard_map/all_to_all | solution.py:667
  145.6 0.6 reshape.33
  146.2 0.9 copy.32
  147.1 5.6 %all-to-all-done.1 = f32[32,1,128]{2,1,0:T(1,128)S(1)} async-done(((f32[32,1,128]{2,1,0:T(1,128)}), f32[32,1,128]{2,1,0:T(1,128)S(1)}, u32[]{:S(2)}, u32[]{:S(2)}) %all-to-all-start.1) | async-done | bytes 16416 | tf_op jit(solution)/shard_map/all_to_all | solution.py:667
  152.7 0.6 copy-done.9
  153.3 2.4 %combine.1 = f32[128,128]{1,0:T(8,128)} custom-call(f32[32,128]{1,0:T(8,128)} %bitcast.14, f32[128,128]{1,0:T(8,128)} %copy-done, f32[128,128]{1,0:T(8,128)} %copy-done.2), custom_call_target="tpu_custom_call" | custom-call | tf_op jit(solution)/shard_map/combine/pallas_call | solution.py:671
  155.7 1.4 reshape.35
  157.1 0.9 copy.33
  (29 shorter events, 1.0 us)
Async XLA Ops:
  2.5 0.9 copy-start.1
  3.4 0.8 copy-start.3
  4.2 0.8 copy-start.4
  4.9 0.8 copy-start.5
  5.7 0.7 copy-start.6
  6.4 0.7 copy-start.7
  10.2 7.3 %copy-start.10 = (s32[256]{0:T(256)S(1)}, s32[256]{0:T(256)}, u32[]{:S(2)}) copy-start(s32[256]{0:T(256)} %param.16) | copy-start | bytes 3076
  10.2 7.5 %copy-start.8 = (f32[2048,8]{0,1:T(8,128)S(1)}, f32[2048,8]{0,1:T(8,128)}, u32[]{:S(2)}) copy-start(f32[2048,8]{0,1:T(8,128)} %param.17) | copy-start | bytes 196612
  10.2 42.3 %all-to-all-start = ((f32[32,88,128]{2,1,0:T(8,128)}), f32[32,88,128]{2,1,0:T(8,128)S(1)}, u32[]{:S(2)}, u32[]{:S(2)}) async-start(f32[32,88,128]{2,1,0:T(8,128)} %fit_and_pack.1), calls=%async_computation | async-start | bytes 2883584 | tf_op jit(solution)/shard_map/all_to_all | solution.py:571
  103.7 19.2 %collective-permute-start = (f32[552,128]{1,0:T(8,128)S(1)}, f32[552,128]{1,0:T(8,128)S(1)}, u32[]{:S(2)}, u32[]{:S(2)}) collective-permute-start(f32[552,128]{1,0:T(8,128)S(1)} %pad_maximum_fusion), channel_id=1, source_target_pairs={{0,1},{1,2},{2,3},{3,4},{4,5},{5,6},{6,7},{7,8},{8,9},{9,10},{10,1... | collective-permute-start | bytes 847880 | tf_op jit(solution)/shard_map/ppermute | solution.py:531
  103.9 17.7 %collective-permute-start.1 = (f32[296,128]{1,0:T(8,128)S(1)}, f32[296,128]{1,0:T(8,128)S(1)}, u32[]{:S(2)}, u32[]{:S(2)}) collective-permute-start(f32[296,128]{1,0:T(8,128)S(1)} %pad_maximum_fusion.1), channel_id=1, source_target_pairs={{0,31},{1,0},{2,1},{3,2},{4,3},{5,4},{6,5},{7,6},{8,7},{9,8},{10,9... | collective-permute-start | bytes 454664 | tf_op jit(solution)/shard_map/ppermute | solution.py:531
  139.9 0.6 copy-start.2
  140.5 12.3 %copy-start = (f32[128,128]{1,0:T(8,128)}, f32[128,128]{1,0:T(8,128)S(1)}, u32[]{:S(2)}) copy-start(f32[128,128]{1,0:T(8,128)S(1)} %get-tuple-element.18.first_ref) | copy-start | bytes 196612
  141.1 11.6 %all-to-all-start.1 = ((f32[32,1,128]{2,1,0:T(1,128)}), f32[32,1,128]{2,1,0:T(1,128)S(1)}, u32[]{:S(2)}, u32[]{:S(2)}) async-start(f32[32,1,128]{2,1,0:T(1,128)} %broadcast_in_dim.38), calls=%async_computation.1 | async-start | bytes 32768 | tf_op jit(solution)/shard_map/all_to_all | solution.py:667
  152.7 0.6 copy-start.9

commit v2 on v1

--- a/solution.py
+++ b/solution.py
@@ -24,8 +24,12 @@
 WORDS = W_PROJ + NLOC * (NHIT - 2)
 
 PER_ITEM = 8
-UNROLL = 4
-GROUPS = 8
+UNROLL = 16
+GROUPS = 16
+SUM_ROW = NLOC + 1
+EDGE = 8
+NEXT_ROADS = 2
+PREV_ROADS = 4
 F32 = jnp.float32
 BF16 = jnp.bfloat16
 
@@ -59,15 +63,21 @@
 
 
 def send_kernel(
-    cap, road_dev, rows_each, ld_ref, gd_ref, me_ref, hw_ref, hm_ref, hc_ref, tr_ref, trc_ref,
-    out_ref, words_ref, parts_ref,
+    cap, road_dev, rows_each, in_ref, out_ref, words_ref, parts_ref,
 ):
-    tracks = hc_ref.shape[1]
+    tracks = in_ref.shape[1]
+    ld_at = NPAR * NHIT
+    me_at = ld_at + NLOC * NHIT
+    hw_at, hm_at, hc_at = me_at + NHIT, me_at + 2 * NHIT, me_at + 3 * NHIT
+    owned = in_ref[hc_at + 1 : hc_at + 2, :].astype(jnp.int32)
     split = LANES // cap
     words_all = rows_each * split
-    weight = jnp.where(iota((NHIT, tracks), 0) < hc_ref[...], hw_ref[...], 0.0)
+    weight = jnp.where(
+        iota((NHIT, tracks), 0).astype(F32) < in_ref[hc_at : hc_at + 1, :],
+        in_ref[hw_at:hm_at, :], 0.0,
+    )
     root = jnp.sqrt(weight)
-    scaled = [ld_ref[a] * root for a in range(NLOC)]
+    scaled = [in_ref[ld_at + a * NHIT : ld_at + (a + 1) * NHIT, :] * root for a in range(NLOC)]
     factor = {}
     for a in range(NLOC):
         for b in range(a + 1):
@@ -83,18 +93,18 @@
         for b in range(a):
             running = running - factor[a, b] * proj[b]
         proj.append(running / factor[a, a])
-    residual = me_ref[...] * root
+    residual = in_ref[me_at:hw_at, :] * root
     solved = residual
     for a in range(NLOC):
         solved = solved - proj[a] * jnp.sum(proj[a] * residual, axis=0, keepdims=True)
     proj = householder(proj, 0, 0)
     proj = householder(proj, 1, 1)
     for i in range(NHIT):
-        words_ref[i * NPAR : (i + 1) * NPAR, :] = gd_ref[:, i, :] * root[i : i + 1]
+        words_ref[i * NPAR : (i + 1) * NPAR, :] = in_ref[i * NPAR : (i + 1) * NPAR, :] * root[i : i + 1]
     words_ref[W_SOLVED:W_SLOT, :] = solved
-    words_ref[W_SLOT:W_ROAD, :] = (hm_ref[...] & (ROAD - 1)).astype(F32)
-    owner = tr_ref[...] // road_dev
-    words_ref[W_ROAD:W_PROJ0, :] = (tr_ref[...] - owner * road_dev + 1).astype(F32)
+    words_ref[W_SLOT:W_ROAD, :] = (in_ref[hm_at:hc_at, :].astype(jnp.int32) & (ROAD - 1)).astype(F32)
+    owner = owned // road_dev
+    words_ref[W_ROAD:W_PROJ0, :] = (owned - owner * road_dev + 1).astype(F32)
     words_ref[W_PROJ0:W_PROJ1, :] = proj[0][0:1]
     words_ref[W_PROJ1 : W_PROJ1 + 1, :] = proj[0][1:2]
     words_ref[W_PROJ1 + 1 : W_PROJ, :] = proj[1][1:2]
@@ -104,7 +114,13 @@
     words_ref[WORDS:, :] = jnp.zeros((words_all - WORDS, tracks), F32)
     for num, part in enumerate(split_three(words_ref[...])):
         parts_ref[num * words_all : (num + 1) * words_all, :] = part
-    owner_col = trc_ref[...] // road_dev
+    owner_col = jnp.concatenate(
+        [
+            jnp.broadcast_to(owner[:, at : at + LANES], (LANES, LANES)).astype(F32).T[:, :1]
+            for at in range(0, tracks, LANES)
+        ],
+        axis=0,
+    ).astype(jnp.int32)
     earlier = iota((tracks, tracks), 0) < iota((tracks, tracks), 1)
     same = jnp.where(jnp.logical_and(owner_col == owner, earlier), 1.0, 0.0)
     rank = jnp.sum(same, axis=0, keepdims=True).astype(jnp.int32)
@@ -204,92 +220,83 @@
     return W_ROAD // rows_of(cap)
 
 
-def blocks_kernel(
-    cap, bound_ref, list_ref, item_ref, recv_ref, off_ref, out_ref, sums_ref, tiles_ref, words_ref,
-    held_ref,
-):
-    group = pl.program_id(0)
-    each = out_ref.shape[0]
+def lay_tiles(cap, recv_ref, off_ref, tiles_ref, words_ref):
     split = LANES // cap
     rows_each = recv_ref.shape[1]
     blocks = off_ref.shape[0]
     width = ROAD * NPAR
-
-    @pl.when(group == 0)
-    def _():
-        lane_part = iota((rows_each, LANES), 1) // cap
-        tiles_ref[blocks * LANES] = jnp.zeros((8, width), F32)
-
-        def lay(e, carry):
-            for m in range(split):
-                made = None
-                for k in range(split):
-                    piece = recv_ref[e * split + k]
-                    if k != m:
-                        piece = pltpu.roll(piece, (cap * (k - m)) % LANES, 1)
-                    made = piece if made is None else jnp.where(lane_part == k, piece, made)
-                words_ref[m * rows_each : (m + 1) * rows_each, :] = made
-            offset = off_ref[pl.ds(e, 1), :]
-            slots = []
-            for i in range(NHIT):
-                slot = words_ref[W_SLOT + i : W_SLOT + i + 1, :] - offset
-                slots.append(jnp.where(slot < 0.0, slot + ROAD, slot))
-            laid = [jnp.zeros((NPAR, LANES), F32) for s in range(ROAD)]
-            for i in range(NHIT):
-                value = words_ref[i * NPAR : (i + 1) * NPAR, :]
-                wide = jnp.broadcast_to(slots[i], (NPAR, LANES))
-                for s in range(ROAD):
-                    laid[s] = jnp.where(wide == float(s), value, laid[s])
-            slot_num = iota((ROAD, LANES), 0).astype(F32)
-            placed = [jnp.zeros((ROAD, LANES), F32) for a in range(NLOC + 1)]
-            for i in range(NHIT):
-                match = slots[i] == slot_num
-                for a in range(NLOC + 1):
-                    if a == NLOC:
-                        at = W_SOLVED + i
-                    elif i == 0:
-                        at = W_PROJ0 if a == 0 else None
-                    elif i == 1:
-                        at = W_PROJ1 + a if a < 2 else None
-                    else:
-                        at = W_PROJ + a * (NHIT - 2) + i - 2
-                    if at is not None:
-                        placed[a] = jnp.where(match, words_ref[at : at + 1, :], placed[a])
-            start = pl.multiple_of(e * LANES, LANES)
+    lane_part = iota((rows_each, LANES), 1) // cap
+    tiles_ref[blocks * LANES] = jnp.zeros((8, width), F32)
+
+    def lay(e, held):
+        words = words_ref.at[held]
+        for m in range(split):
+            made = None
+            for k in range(split):
+                piece = recv_ref[e * split + k]
+                if k != m:
+                    piece = pltpu.roll(piece, (cap * (k - m)) % LANES, 1)
+                made = piece if made is None else jnp.where(lane_part == k, piece, made)
+            words[m * rows_each : (m + 1) * rows_each, :] = made
+        offset = off_ref[pl.ds(e, 1), :]
+        slots = []
+        for i in range(NHIT):
+            slot = words[W_SLOT + i : W_SLOT + i + 1, :] - offset
+            slots.append(jnp.where(slot < 0.0, slot + ROAD, slot))
+        laid = [jnp.zeros((NPAR, LANES), F32) for s in range(ROAD)]
+        for i in range(NHIT):
+            value = words[i * NPAR : (i + 1) * NPAR, :]
+            wide = jnp.broadcast_to(slots[i], (NPAR, LANES))
+            for s in range(ROAD):
+                laid[s] = jnp.where(wide == float(s), value, laid[s])
+        slot_num = iota((ROAD, LANES), 0).astype(F32)
+        placed = [jnp.zeros((ROAD, LANES), F32) for a in range(NLOC + 1)]
+        for i in range(NHIT):
+            match = slots[i] == slot_num
             for a in range(NLOC + 1):
-                mixed = jnp.concatenate(
-                    [laid[s] * placed[a][s : s + 1] for s in range(ROAD)], axis=0
-                )
-                at = a if a < NLOC else NLOC + 1
-                tiles_ref[pl.ds(start, LANES), at, :] = mixed.T
-            tiles_ref[pl.ds(start, LANES), NLOC, :] = jnp.concatenate(laid, axis=0).T
-            tiles_ref[pl.ds(start, LANES), NLOC + 2, :] = jnp.zeros((LANES, width), F32)
-            return carry
-
-        lax.fori_loop(0, blocks, lay, 0)
-
+                if a == NLOC:
+                    at = W_SOLVED + i
+                elif i == 0:
+                    at = W_PROJ0 if a == 0 else None
+                elif i == 1:
+                    at = W_PROJ1 + a if a < 2 else None
+                else:
+                    at = W_PROJ + a * (NHIT - 2) + i - 2
+                if at is not None:
+                    placed[a] = jnp.where(match, words[at : at + 1, :], placed[a])
+        start = pl.multiple_of(e * LANES, LANES)
+        for a in range(NLOC + 1):
+            mixed = jnp.concatenate([laid[s] * placed[a][s : s + 1] for s in range(ROAD)], axis=0)
+            tiles_ref[pl.ds(start, LANES), a if a < NLOC else SUM_ROW, :] = mixed.T
+        tiles_ref[pl.ds(start, LANES), NLOC, :] = jnp.concatenate(laid, axis=0).T
+        tiles_ref[pl.ds(start, LANES), SUM_ROW + 1, :] = jnp.zeros((LANES, width), F32)
+
+    def lay_two(num, carry):
+        lay(2 * num, 0)
+        lay(2 * num + 1, 1)
+        return carry
+
+    lax.fori_loop(0, blocks // 2, lay_two, 0)
+
+
+def item_steps(list_ref, item_ref, tiles_ref, out_ref, held_ref):
+    width = ROAD * NPAR
     row_kind = iota((PER_ITEM * 8, width), 0) % 8
     is_proj = row_kind < NLOC
     is_own = row_kind == NLOC
     same_slot = iota((width, width), 0) // NPAR == iota((width, width), 1) // NPAR
-    begin = bound_ref[0, group]
-    end = bound_ref[0, group + 1]
-
-    def step(num, carry):
+    spare = list_ref.shape[0] // PER_ITEM - 1
+
+    def step(begin, end, num):
         for u in range(UNROLL):
             item = begin + num * UNROLL + u
             live = item < end
-            item = jnp.minimum(item, end - 1)
-            info = item_ref[item // LANES, item % LANES]
-            road = info // 2
-            first = jnp.logical_and(info % 2 == 1, live)
-            local = road - group * each
+            item = jnp.where(live, item, spare)
+            info = item_ref[item]
+            first = (info & 1) == 1
+            road = jnp.where(live, info >> 1, 0)
             at = item * PER_ITEM
-            parts = []
-            for j in range(PER_ITEM):
-                track = list_ref[(at + j) // LANES, (at + j) % LANES]
-                track = jnp.where(live, track, blocks * LANES)
-                parts.append(tiles_ref[track])
+            parts = [tiles_ref[list_ref[at + j]] for j in range(PER_ITEM)]
             tall = jnp.concatenate(parts, axis=0)
             high = tall.astype(BF16)
             high32 = high.astype(F32)
@@ -309,15 +316,84 @@
             )
             both = dot(left, right, 0, 0)
             value = jnp.where(same_slot, both[:, width:], 0.0) - both[:, :width]
-            out_ref[local] = value + jnp.where(first, 0.0, out_ref[local])
+            out_ref[road] = value + jnp.where(first, 0.0, out_ref[road])
             added = parts[0]
             for part in parts[1:]:
                 added = added + part
-            held_ref[local] = added + jnp.where(first, 0.0, held_ref[local])
-        return carry
-
-    lax.fori_loop(0, (end - begin + UNROLL - 1) // UNROLL, step, 0)
-    sums_ref[...] = held_ref[:, NLOC + 1, :]
+            held_ref[road] = added + jnp.where(first, 0.0, held_ref[road])
+
+    return step
+
+
+def edge_kernel(
+    cap, bound_ref, list_ref, item_ref, recv_ref, off_ref, off_rows_ref, prior_ref,
+    tiles_ref, out_ref, sums_ref, to_next_ref, to_prev_ref, words_ref, held_ref,
+):
+    roads, width = sums_ref.shape
+    edge = roads // GROUPS
+    lay_tiles(cap, recv_ref, off_ref, tiles_ref, words_ref)
+    step = item_steps(list_ref, item_ref, tiles_ref, out_ref, held_ref)
+    for group in (0, GROUPS - 1):
+        begin, end = bound_ref[group], bound_ref[group + 1]
+
+        def body(num, carry, begin=begin, end=end):
+            step(begin, end, num)
+            return carry
+
+        lax.fori_loop(0, (end - begin + UNROLL - 1) // UNROLL, body, 0)
+    sums_ref[:edge] = held_ref[:edge, SUM_ROW, :]
+    sums_ref[roads - edge :] = held_ref[roads - edge :, SUM_ROW, :]
+    two = 2 * EDGE
+    for ref, first_block, count, first_road, first_row in (
+        (to_next_ref, roads - PREV_ROADS, PREV_ROADS, roads - two, prior_ref.shape[0] - EDGE),
+        (to_prev_ref, 0, NEXT_ROADS, 0, 0),
+    ):
+        for num in range(count):
+            ref[num * width : (num + 1) * width] = out_ref[first_block + num]
+        at = count * width
+        ref[at : at + two] = sums_ref[first_road : first_road + two]
+        ref[at + two : at + 2 * two] = off_rows_ref[first_road : first_road + two]
+        ref[at + 2 * two :] = prior_ref[first_row : first_row + EDGE]
+
+
+def inner_kernel(
+    bound_ref, list_ref, item_ref, tiles_ref, edge_ref, edge_sums_ref,
+    blocks_hbm, out_ref, sums_ref, held_ref, sems,
+):
+    roads, width = sums_ref.shape
+    edge = roads // GROUPS
+    step = item_steps(list_ref, item_ref, tiles_ref, out_ref, held_ref)
+    outer = [
+        pltpu.make_async_copy(
+            out_ref.at[pl.ds(at, edge)], blocks_hbm.at[pl.ds(at, edge)], sems.at[num]
+        )
+        for num, at in enumerate((0, roads - edge))
+    ]
+    begin, end = bound_ref[1], bound_ref[GROUPS - 1]
+    done = 0
+    copies = []
+    pieces = (GROUPS - 2) // 2
+    for piece in range(pieces):
+        group = 1 + 2 * piece
+        until = (bound_ref[group + 2] - begin + UNROLL - 1) // UNROLL
+
+        def body(num, carry):
+            step(begin, end, num)
+            return carry
+
+        lax.fori_loop(done, until, body, 0)
+        done = until
+        where = pl.ds(group * edge, 2 * edge)
+        copies.append(
+            pltpu.make_async_copy(out_ref.at[where], blocks_hbm.at[where], sems.at[2 + piece])
+        )
+        copies[-1].start()
+    for copy in outer:
+        copy.start()
+    sums_ref[edge : roads - edge] = held_ref[edge : roads - edge, SUM_ROW, :]
+    for copy in outer + copies:
+        copy.wait()
+    del edge_ref, edge_sums_ref
 
 
 def lane_bits(offset, bit):
@@ -363,32 +439,17 @@
     return here, there
 
 
-EDGE = 8
-NEXT_ROADS = 2
-PREV_ROADS = 4
-
-
 def krylov_kernel(
-    blocks_hbm, sums_ref, off_ref, prior_ref, from_prev_ref, from_next_ref,
-    first_ref, second_ref, third_ref, dots_ref,
-    held, sems, even_sum, odd_sum, even_off, odd_off, prior, even_part, odd_part, turned_even,
-    turned_odd, even_out, odd_out, rows_scr,
+    held, sums_ref, off_ref, prior_ref, from_prev_ref, from_next_ref,
+    first_ref, second_ref, dots_ref,
+    even_sum, odd_sum, even_off, odd_off, prior, even_part, odd_part, turned_even,
+    turned_odd,
 ):
     roads, width = sums_ref.shape
     half = roads // 2
-    chunks = sems.shape[0]
-    each = roads // chunks
+    each = min(roads, 64)
+    chunks = roads // each
     own = slice(EDGE, EDGE + half)
-    total = half + 2 * EDGE
-    copies = [
-        pltpu.make_async_copy(
-            blocks_hbm.at[pl.ds(c * each, each)], held.at[pl.ds(c * each, each)], sems.at[c]
-        )
-        for c in range(chunks)
-    ]
-    for copy in copies:
-        copy.start()
-
     two = 2 * EDGE
     at_prev = PREV_ROADS * width
     at_next = NEXT_ROADS * width
@@ -421,7 +482,7 @@
             acc = term if acc is None else acc + term
         return acc
 
-    def apply(vector, wait):
+    def apply(vector):
         even = gathered(vector, even_off[...], False)
         odd = gathered(vector, odd_off[...], True)
         even_part[...] = jnp.zeros_like(even_part)
@@ -451,25 +512,25 @@
         turned_odd[:, :half] = odd[own].T
         per = each // 2
 
+        copies_of = iota((3 * per, per * width), 0) % per == iota((3 * per, per * width), 1) // width
+        copies_of = jnp.where(copies_of, 1.0, 0.0).astype(BF16)
+
         def chunk(c, carry):
-            if wait:
-                pltpu.make_async_copy(
-                    blocks_hbm.at[pl.ds(c * each, each)],
-                    held.at[pl.ds(c * each, each)],
-                    sems.at[c],
-                ).wait()
             columns_even = turned_even[...]
             columns_odd = turned_odd[...]
+            spread_odd = dot(
+                jnp.concatenate(split_three(columns_odd[:, :per]), axis=1), copies_of, 1, 0
+            )
             for j in range(per):
-                for parity, columns, part in (
-                    (0, columns_even, even_part),
-                    (1, columns_odd, odd_part),
-                ):
-                    road = c * each + 2 * j + parity
-                    part[EDGE + c * per + j] = column_product(
-                        lambda s, road=road: held[road, s * 8 : s * 8 + 8, :],
-                        columns[:, j : j + 1],
-                    )
+                road = c * each + 2 * j
+                even_part[EDGE + c * per + j] = column_product(
+                    lambda s, road=road: held[road, s * 8 : s * 8 + 8, :],
+                    columns_even[:, j : j + 1],
+                )
+                odd_part[EDGE + c * per + j] = column_product(
+                    lambda s, road=road: held[road + 1, s * 8 : s * 8 + 8, :],
+                    spread_odd[:, j * width : (j + 1) * width],
+                )
             turned_even[...] = pltpu.roll(columns_even, columns_even.shape[1] - per, 1)
             turned_odd[...] = pltpu.roll(columns_odd, columns_odd.shape[1] - per, 1)
             return carry
@@ -483,13 +544,12 @@
         return prior[...] * vector + spread(even, odd)
 
     first = spread(even_sum[...], odd_sum[...])
-    second = apply(first, True)
-    third = apply(second, False)
+    second = apply(first)
+    third = apply(second)
     first, second, third = first[own], second[own], third[own]
     first_ref[...] = first
     second_ref[...] = second
-    third_ref[...] = third
-    lane = iota(dots_ref.shape, 1)
+    lane = iota(dots_ref.shape, 2)
     dots = jnp.zeros(dots_ref.shape, F32)
     pairs = ((first, first), (first, second), (second, second), (second, third), (third, third))
     for num, (one, other) in enumerate(pairs):
@@ -497,7 +557,7 @@
     dots_ref[...] = dots
 
 
-def finish_kernel(dots_ref, first_ref, second_ref, out_ref):
+def finish_kernel(dots_ref, first_ref, second_ref, out_hbm, out_ref, sem):
     sums = jnp.sum(dots_ref[...], axis=0, keepdims=True)
     s00, s01, s11, s12, s22 = (sums[:, num : num + 1] for num in range(5))
     square_one = s00 + EPS
@@ -524,6 +584,9 @@
     on_second = coef_two * scale
     on_first = coef_one / beta_one - alpha_one * on_second
     out_ref[...] = on_first * first_ref[...] + on_second * second_ref[...]
+    copy = pltpu.make_async_copy(out_ref, out_hbm, sem)
+    copy.start()
+    copy.wait()
 
 
 def neighbour(value, steps):
@@ -551,12 +614,19 @@
     half = modules // ROAD
     vmem = pl.BlockSpec(memory_space=pltpu.VMEM)
     smem = pl.BlockSpec(memory_space=pltpu.SMEM)
-    limit = pltpu.CompilerParams(vmem_limit_bytes=50 * 1024 * 1024)
-
+    limit = pltpu.CompilerParams(vmem_limit_bytes=32 * 1024 * 1024)
+    small = pltpu.CompilerParams(vmem_limit_bytes=12 * 1024 * 1024)
+
+    sent = [
+        jnp.transpose(global_deriv, (1, 0, 2)).reshape(NHIT * NPAR, tracks),
+        local_deriv.reshape(NLOC * NHIT, tracks), measured, hit_weight, hit_module.astype(F32),
+        hit_count.astype(F32)[None, :], track_road.astype(F32)[None, :],
+    ]
+    sent = jnp.concatenate(sent)
     send = pl.pallas_call(
         functools.partial(send_kernel, cap, roads, rows_each),
         out_shape=shape(devices, rows_each, LANES),
-        in_specs=[vmem] * 8,
+        in_specs=[vmem],
         out_specs=vmem,
         scratch_shapes=[
             pltpu.VMEM((rows_each * split, tracks), F32),
@@ -564,15 +634,12 @@
         ],
         compiler_params=limit,
         name="fit_and_pack",
-    )(
-        local_deriv, global_deriv, measured, hit_weight, hit_module, hit_count[None, :],
-        track_road[None, :], track_road[:, None],
-    )
+    )(sent)
     recv = lax.all_to_all(send, AXES, split_axis=0, concat_axis=0, tiled=True)
 
     offset = road_start % ROAD
-    list_rows = -(-(PER_ITEM * roads + slots) // (8 * LANES)) * 8
-    item_rows = -(-(list_rows * LANES // PER_ITEM) // LANES)
+    list_rows = ((PER_ITEM * roads + slots) // (8 * LANES) + 1) * 8
+    item_rows = -(-(list_rows * LANES // PER_ITEM) // (8 * LANES)) * 8
     road_row = W_ROAD % rows_each
     track_list, items, bounds, track_off = pl.pallas_call(
         functools.partial(sort_kernel, cap),
@@ -598,86 +665,70 @@
         name="sort_by_road",
     )(recv, offset.astype(F32)[:, None])
 
-    each = roads // GROUPS
-    normal_blocks, sums = pl.pallas_call(
-        functools.partial(blocks_kernel, cap),
-        grid=(GROUPS,),
-        out_shape=(shape(roads, width, width), shape(roads, width)),
-        in_specs=[
-            smem,
-            smem,
-            smem,
-            pl.BlockSpec((devices, rows_each, LANES), lambda g: (0, 0, 0)),
-            pl.BlockSpec((slots // LANES, LANES), lambda g: (0, 0)),
-        ],
-        out_specs=(
-            pl.BlockSpec((each, width, width), lambda g: (g, 0, 0)),
-            pl.BlockSpec((each, width), lambda g: (g, 0)),
-        ),
-        scratch_shapes=[
-            pltpu.VMEM((slots + 8, 8, width), F32),
-            pltpu.VMEM((rows_each * split, LANES), F32),
-            pltpu.VMEM((each, 8, width), F32),
-        ],
-        compiler_params=limit,
-        name="assemble_blocks",
-    )(bounds, track_list, items, recv, track_off)
-
+    edge = roads // GROUPS
     prior = prior_weight.reshape(half, width)
     off_rows = jnp.broadcast_to((offset % (ROAD // 2)).astype(F32)[:, None], (roads, LANES))
-    two = 2 * EDGE
-    to_next = jnp.concatenate(
-        [
-            normal_blocks[-PREV_ROADS:].reshape(-1, width),
-            sums[-two:],
-            off_rows[-two:],
-            prior[-EDGE:],
-        ]
-    )
-    to_prev = jnp.concatenate(
-        [
-            normal_blocks[:NEXT_ROADS].reshape(-1, width),
-            sums[:two],
-            off_rows[:two],
-            prior[:EDGE],
-        ]
-    )
+    lists = (bounds.reshape(-1), track_list.reshape(-1), items.reshape(-1))
+    halo = 4 * EDGE + EDGE
+    tiles, edge_blocks, edge_sums, to_next, to_prev = pl.pallas_call(
+        functools.partial(edge_kernel, cap),
+        out_shape=(
+            shape(slots + 8, 8, width), shape(roads, width, width), shape(roads, width),
+            shape(PREV_ROADS * width + halo, width), shape(NEXT_ROADS * width + halo, width),
+        ),
+        in_specs=[smem] * 3 + [vmem] * 4,
+        out_specs=(vmem,) * 5,
+        scratch_shapes=[
+            pltpu.VMEM((2, rows_each * split, LANES), F32),
+            pltpu.VMEM((roads, 8, width), F32),
+        ],
+        compiler_params=small,
+        name="lay_and_assemble_edges",
+    )(*lists, recv, track_off, off_rows, prior)
     from_prev = neighbour(to_next, 1)
     from_next = neighbour(to_prev, -1)
+    normal_blocks, held_blocks, sums = pl.pallas_call(
+        inner_kernel,
+        out_shape=(
+            shape(roads, width, width), shape(roads, width, width), shape(roads, width),
+        ),
+        in_specs=[smem] * 3 + [vmem] * 3,
+        out_specs=(pl.BlockSpec(memory_space=pltpu.HBM), vmem, vmem),
+        scratch_shapes=[
+            pltpu.VMEM((roads, 8, width), F32),
+            pltpu.SemaphoreType.DMA((2 + (GROUPS - 2) // 2,)),
+        ],
+        input_output_aliases={4: 1, 5: 2},
+        compiler_params=small,
+        name="assemble_blocks",
+    )(*lists, tiles, edge_blocks, edge_sums)
+
     total = half + 2 * EDGE
-    chunks = 16 if roads >= 256 else 4
     rows = pltpu.VMEM((total, LANES), F32)
     int_rows = pltpu.VMEM((total, LANES), jnp.int32)
-    tiles = pltpu.VMEM((total, 8, LANES), F32)
+    parts = pltpu.VMEM((total, 8, LANES), F32)
     turned = pltpu.VMEM((LANES, LANES), F32)
-    first, second, third, dots = pl.pallas_call(
+    first, second, dots = pl.pallas_call(
         krylov_kernel,
-        out_shape=(shape(half, width), shape(half, width), shape(half, width), shape(1, LANES)),
-        in_specs=[pl.BlockSpec(memory_space=pl.ANY)] + [vmem] * 5,
-        out_specs=(vmem,) * 4,
-        scratch_shapes=[
-            pltpu.VMEM((roads, width, width), F32),
-            pltpu.SemaphoreType.DMA((chunks,)),
-            rows, rows, int_rows, int_rows, rows, tiles, tiles, turned, turned, rows, rows, rows,
-        ],
-        compiler_params=limit,
+        out_shape=(shape(half, width), shape(half, width), shape(devices, 1, LANES)),
+        in_specs=[vmem] * 6,
+        out_specs=(vmem,) * 3,
+        scratch_shapes=[rows, rows, int_rows, int_rows, rows, parts, parts, turned, turned],
+        compiler_params=small,
         name="two_products",
-    )(normal_blocks, sums, off_rows, prior, from_prev, from_next)
-    del third
-    everyone = lax.all_to_all(
-        jnp.broadcast_to(dots[None], (devices, 1, LANES)), AXES, split_axis=0, concat_axis=0,
-        tiled=True,
-    )
+    )(held_blocks, sums, off_rows, prior, from_prev, from_next)
+    everyone = lax.all_to_all(dots, AXES, split_axis=0, concat_axis=0, tiled=True)
+    rhs = first.reshape(modules, NPAR)
+    summed = (everyone.reshape(devices, LANES), rhs.T, second.reshape(modules, NPAR).T)
     corrections = pl.pallas_call(
         finish_kernel,
-        out_shape=shape(half, width),
+        out_shape=shape(NPAR, modules),
         in_specs=[vmem] * 3,
-        out_specs=vmem,
+        out_specs=pl.BlockSpec(memory_space=pltpu.HBM),
+        scratch_shapes=[pltpu.VMEM((NPAR, modules), F32), pltpu.SemaphoreType.DMA],
         name="combine",
-    )(everyone.reshape(devices, LANES), first, second)
-    return (
-        normal_blocks, first.reshape(modules, NPAR), corrections.reshape(modules, NPAR),
-    )
+    )(*summed)
+    return (normal_blocks, rhs, corrections.T)
 
 
 def solution(mesh):

time: 156 us -> 105 us (0.67)
  Pallas kernels: 71.4 us -> 42.1 us
  starting transfers between devices: 26.8 us -> 15.2 us
  local copies, waits for them, and re-layouts: 15.7 us -> 9.09 us
  waiting for transfers between devices: 43.1 us -> 36.5 us
  other arithmetic: 0.26 us -> 2.83 us
    pallas_call x2 -> x3, Pallas kernels: 49.6 us -> 26 us  [the longest x1 13.5 us: on_device(): pl.pallas_call(inner_kernel, out_shape=(shape(roads, width, width), shape...]
    ppermute x2, starting transfers between devices: 15 us -> 5.39 us  [neighbour(): lax.ppermute(value, AXES, [(s, (s + steps) % count) for s in range(count)])]
    unnamed x26 -> x4, local copies, waits for them, and re-layouts: 9.02 us -> 2.71 us
    pallas_call x1, Pallas kernels: 16.8 us -> 10.9 us  [on_device(): pl.pallas_call(krylov_kernel, out_shape=(shape(half, width), shape(half,...]
    ppermute x2, waiting for transfers between devices: 3.27 us -> 0.01 us  [neighbour(): lax.ppermute(value, AXES, [(s, (s + steps) % count) for s in range(count)])]
    concatenate x2 -> x1, local copies, waits for them, and re-layouts: 0.15 us -> 2.66 us  [on_device(): sent = jnp.concatenate(sent)]
    slice x9 -> x0, local copies, waits for them, and re-layouts: 2.35 us -> none  [the longest x1 0.97 us: on_device(): normal_blocks[-PREV_ROADS:].reshape(-1, width)]
    convert_element_type x0 -> x3, other arithmetic: none -> 2.13 us  [the longest x1 0.76 us: on_device(): hit_module.astype(F32)]
  transfers between devices with their start and end apart: 4 -> 4, of which waited for: 4 -> 2; matrix products, arithmetic and copies ran while one was open for 2% -> 5% of each run, Pallas kernels for 0% -> 13%
where the time goes in v2:
time: 105 us; the launch traced here: 107 us
  Pallas kernels  42.1 us (40%)
  waiting for transfers between devices  36.5 us (35%)
  starting transfers between devices  15.2 us (14%)
  local copies, waits for them, and re-layouts  9.09 us (9%)
  other arithmetic  2.83 us (3%)
    all_to_all x1, waiting for transfers between devices, on_device(): recv = lax.all_to_all(send, AXES, split_axis=0, concat_axis=0, tiled=True)  32.5 us
    pallas_call x1, Pallas kernels, on_device(): pl.pallas_call(inner_kernel, out_shape=(shape(roads, width, width), shape...  13.5 us
    pallas_call x1, Pallas kernels, on_device(): pl.pallas_call(krylov_kernel, out_shape=(shape(half, width), shape(half,...  10.9 us
    pallas_call x1, Pallas kernels, on_device(): pl.pallas_call(functools.partial(edge_kernel, cap), out_shape=(shape(slot...  10.1 us
    all_to_all x1, starting transfers between devices, on_device(): recv = lax.all_to_all(send, AXES, split_axis=0, concat_axis=0, tiled=True)  7.3 us
    ppermute x2, starting transfers between devices, neighbour(): lax.ppermute(value, AXES, [(s, (s + steps) % count) for s in range(count)])  5.39 us
    all_to_all x1, waiting for transfers between devices, on_device(): lax.all_to_all(dots, AXES, split_axis=0, concat_axis=0, tiled=True)  4.05 us
    pallas_call x1, Pallas kernels, on_device(): pl.pallas_call(functools.partial(send_kernel, cap, roads, rows_each), out...  3.23 us
  transfers between devices with their start and end apart: 4, of which 2 were waited for; matrix products, arithmetic and copies ran while one was open for 5% of the time, Pallas kernels for 13%

profile of v2, /device:TPU:0, one launch (start us, length us, event | category | flops | bytes accessed | tf_op | source)
XLA Modules:
  0.0 106.7 jit_solution(16918889448628790606)
XLA Ops:
  0.6 0.7 convert_element_type.16
  1.3 0.7 convert_element_type.17
  2.0 0.8 convert_element_type.15
  2.8 0.9 reshape.35
  3.7 2.7 %concatenate.3.in_ref = f32[194,512]{1,0:T(8,128)S(1)} concatenate(f32[96,512]{1,0:T(8,128)} %bitcast.21, f32[60,512]{1,0:T(8,128)S(1)} %reshape.35, f32[12,512]{1,0:T(8,128)} %param.11, f32[12,512]{1,0:T(8,128)} %param.12, f32[12,512]{1,0:T(8,128)S(1)} %convert_element_type.15, f32[1,512]{1,0:T(1,128)S(1)} %bitcast.24, f32[1,512]{1,0:T(1,128)S(1)} %bitcast.25), dimensions={0} | concatenate | bytes 794624 | tf_op jit(solution)/shard_map/concatenate | solution.py:625
  6.4 3.2 %fit_and_pack.1 = f32[32,88,128]{2,1,0:T(8,128)} custom-call(f32[194,512]{1,0:T(8,128)S(1)} %concatenate.3.in_ref), custom_call_target="tpu_custom_call" | custom-call | tf_op jit(solution)/shard_map/fit_and_pack/pallas_call | solution.py:626
  9.6 7.3 %all-to-all-start = ((f32[32,88,128]{2,1,0:T(8,128)}), f32[32,88,128]{2,1,0:T(8,128)S(1)}, u32[]{:S(2)}, u32[]{:S(2)}) async-start(f32[32,88,128]{2,1,0:T(8,128)} %fit_and_pack.1), calls=%async_computation | async-start | bytes 2883584 | tf_op jit(solution)/shard_map/all_to_all | solution.py:638
  16.9 0.7 fusion
  17.6 0.1 copy.22.off_ref
  17.7 1.2 %copy.23 = f32[2048,8]{1,0:T(8,128)S(1)} copy(f32[2048,8]{0,1:T(8,128)} %param.17) | data formatting | bytes 131072 | tf_op args[8]
  18.9 0.5 reshape.39.prior_ref
  19.4 32.5 %all-to-all-done.recv_ref = f32[32,88,128]{2,1,0:T(8,128)S(1)} async-done(((f32[32,88,128]{2,1,0:T(8,128)}), f32[32,88,128]{2,1,0:T(8,128)S(1)}, u32[]{:S(2)}, u32[]{:S(2)}) %all-to-all-start) | async-done | bytes 1441824 | tf_op jit(solution)/shard_map/all_to_all | solution.py:638
  51.9 2.0 %sort_by_road.1 = (s32[40,128]{1,0:T(8,128)S(1)}, s32[8,128]{1,0:T(8,128)S(1)}, s32[8,128]{1,0:T(8,128)S(1)}, f32[16,128]{1,0:T(8,128)S(1)}) custom-call(f32[32,88,128]{2,1,0:T(8,128)S(1)} %all-to-all-done.recv_ref, f32[256,1]{1,0:T(8,128)S(1)} %copy.22.off_ref), custom_call_target="tpu_custom_call" | custom-call | tf_op jit(solution)/shard_map/sort_by_road/pallas_call | solution.py:644
  53.9 0.1 broadcast_in_dim.18.off_rows_ref.off_ref
  54.0 10.1 %lay_and_assemble_edges.1 = (f32[2056,8,128]{2,1,0:T(8,128)S(1)}, f32[256,128,128]{2,1,0:T(8,128)S(1)}, f32[256,128]{1,0:T(8,128)S(1)}, f32[552,128]{1,0:T(8,128)S(1)}, f32[296,128]{1,0:T(8,128)S(1)}) custom-call(s32[1024]{0:T(1024)S(1)} %bitcast.17, s32[5120]{0:T(1024)S(1)} %bitcast.13, s32[1024]{0:T(1024)S(1)} %bitcast.15, ...), custom_call_target="tpu_custom_call" | custom-call | tf_op jit(solution)/shard_map/lay_and_assemble_edges/pallas_call | solution.py:673
  64.1 0.1 collective-permute-start
  64.1 5.3 %collective-permute-start.1 = (f32[296,128]{1,0:T(8,128)S(1)}, f32[296,128]{1,0:T(8,128)S(1)}, u32[]{:S(2)}, u32[]{:S(2)}) collective-permute-start(f32[296,128]{1,0:T(8,128)S(1)} %get-tuple-element.29), channel_id=1, source_target_pairs={{0,31},{1,0},{2,1},{3,2},{4,3},{5,4},{6,5},{7,6},{8,7},{9,8},{10,9... | collective-permute-start | bytes 454664 | tf_op jit(solution)/shard_map/ppermute | solution.py:594
  69.5 13.5 %assemble_blocks.1 = (f32[256,128,128]{2,1,0:T(8,128)}, f32[256,128,128]{2,1,0:T(8,128)S(1)}, f32[256,128]{1,0:T(8,128)S(1)}) custom-call(s32[1024]{0:T(1024)S(1)} %bitcast.18, s32[5120]{0:T(1024)S(1)} %bitcast.14, s32[1024]{0:T(1024)S(1)} %bitcast.16, ...), custom_call_target="tpu_custom_call", output_to_operand_aliasing={{1}: (4, {}), {2}: (5, {})} | custom-call | tf_op jit(solution)/shard_map/assemble_blocks/pallas_call | solution.py:690
  83.0 0.0 collective-permute-done.1.from_next_ref
  83.0 0.0 collective-permute-done.from_prev_ref
  83.0 10.9 %two_products.1 = (f32[128,128]{1,0:T(8,128)S(1)}, f32[128,128]{1,0:T(8,128)S(1)}, f32[32,1,128]{2,1,0:T(1,128)}) custom-call(f32[256,128,128]{2,1,0:T(8,128)S(1)} %get-tuple-element.26.held, f32[256,128]{1,0:T(8,128)S(1)} %get-tuple-element.27.sums_ref, f32[256,128]{1,0:T(8,128)S(1)} %broadcast_in_dim.18.off_rows_ref.off_ref, ...), custom_call_target="tpu_custom_call" | custom-call | tf_op jit(solution)/shard_map/two_products/pallas_call | solution.py:711
  93.9 2.5 %all-to-all-start.1 = ((f32[32,1,128]{2,1,0:T(1,128)}), f32[32,1,128]{2,1,0:T(1,128)S(1)}, u32[]{:S(2)}, u32[]{:S(2)}) async-start(f32[32,1,128]{2,1,0:T(1,128)} %get-tuple-element.31), calls=%async_computation.1 | async-start | bytes 32768 | tf_op jit(solution)/shard_map/all_to_all | solution.py:720
  96.5 0.6 reshape.40
  97.0 0.9 copy.26
  98.0 0.6 reshape.42
  98.6 0.9 copy.25
  99.5 4.1 %all-to-all-done.1 = f32[32,1,128]{2,1,0:T(1,128)S(1)} async-done(((f32[32,1,128]{2,1,0:T(1,128)}), f32[32,1,128]{2,1,0:T(1,128)S(1)}, u32[]{:S(2)}, u32[]{:S(2)}) %all-to-all-start.1) | async-done | bytes 16416 | tf_op jit(solution)/shard_map/all_to_all | solution.py:720
  103.5 0.0 copy-start
  103.5 0.6 copy-done
  104.1 2.4 %combine.1 = f32[8,2048]{1,0:T(8,128)} custom-call(f32[32,128]{1,0:T(8,128)} %bitcast.23, f32[8,2048]{1,0:T(8,128)} %bitcast.19, f32[8,2048]{1,0:T(8,128)} %bitcast.20), custom_call_target="tpu_custom_call" | custom-call | tf_op jit(solution)/shard_map/combine/pallas_call | solution.py:723
  (1 shorter events, 0.0 us)
Async XLA Ops:
  9.6 42.3 %all-to-all-start = ((f32[32,88,128]{2,1,0:T(8,128)}), f32[32,88,128]{2,1,0:T(8,128)S(1)}, u32[]{:S(2)}, u32[]{:S(2)}) async-start(f32[32,88,128]{2,1,0:T(8,128)} %fit_and_pack.1), calls=%async_computation | async-start | bytes 2883584 | tf_op jit(solution)/shard_map/all_to_all | solution.py:638
  64.1 18.9 %collective-permute-start = (f32[552,128]{1,0:T(8,128)S(1)}, f32[552,128]{1,0:T(8,128)S(1)}, u32[]{:S(2)}, u32[]{:S(2)}) collective-permute-start(f32[552,128]{1,0:T(8,128)S(1)} %get-tuple-element.28), channel_id=1, source_target_pairs={{0,1},{1,2},{2,3},{3,4},{4,5},{5,6},{6,7},{7,8},{8,9},{9,10},{10,1... | collective-permute-start | bytes 847880 | tf_op jit(solution)/shard_map/ppermute | solution.py:594
  64.1 18.9 %collective-permute-start.1 = (f32[296,128]{1,0:T(8,128)S(1)}, f32[296,128]{1,0:T(8,128)S(1)}, u32[]{:S(2)}, u32[]{:S(2)}) collective-permute-start(f32[296,128]{1,0:T(8,128)S(1)} %get-tuple-element.29), channel_id=1, source_target_pairs={{0,31},{1,0},{2,1},{3,2},{4,3},{5,4},{6,5},{7,6},{8,7},{9,8},{10,9... | collective-permute-start | bytes 454664 | tf_op jit(solution)/shard_map/ppermute | solution.py:594
  93.9 9.6 %all-to-all-start.1 = ((f32[32,1,128]{2,1,0:T(1,128)}), f32[32,1,128]{2,1,0:T(1,128)S(1)}, u32[]{:S(2)}, u32[]{:S(2)}) async-start(f32[32,1,128]{2,1,0:T(1,128)} %get-tuple-element.31), calls=%async_computation.1 | async-start | bytes 32768 | tf_op jit(solution)/shard_map/all_to_all | solution.py:720
  103.5 0.6 copy-start

commit v3 on v2

--- a/solution.py
+++ b/solution.py
@@ -15,14 +15,22 @@
 EPS = 1e-06
 AXES = ("trk", "mod")
 
-W_SOLVED = NHIT * NPAR
-W_SLOT = W_SOLVED + NHIT
-W_ROAD = W_SLOT + NHIT
-W_PROJ0 = W_ROAD + 1
-W_PROJ1 = W_PROJ0 + 1
-W_PROJ = W_PROJ1 + 2
-WORDS = W_PROJ + NLOC * (NHIT - 2)
-
+PART = 88
+USED = 82
+R_ROAD = 10 * NPAR
+R_FIRST = R_ROAD + 1
+R_SOLVED = PART + 2 * NPAR
+R_GAP = R_SOLVED + NHIT
+GAPS = ROAD - NHIT
+R_PROJ = [R_GAP + GAPS + a * NHIT - a * (a - 1) // 2 for a in range(NLOC)]
+ROWS = 2 * PART
+
+
+def derivative_row(hit):
+    return hit * NPAR if hit < 10 else PART + (hit - 10) * NPAR
+
+
+LARGE = 60
 PER_ITEM = 8
 UNROLL = 16
 GROUPS = 16
@@ -62,22 +70,71 @@
     return rows[:first] + [row - part * along for part, row in zip(vector, rows[first:])]
 
 
-def send_kernel(
-    cap, road_dev, rows_each, in_ref, out_ref, words_ref, parts_ref,
+def place_tracks(cap, road_dev, track_road, hot_ref):
+    tracks = track_road.shape[1]
+    owner = track_road // road_dev
+    owner_col = jnp.concatenate(
+        [
+            jnp.broadcast_to(owner[:, at : at + LANES], (LANES, LANES)).astype(F32).T[:, :1]
+            for at in range(0, tracks, LANES)
+        ],
+        axis=0,
+    ).astype(jnp.int32)
+    earlier = iota((tracks, tracks), 0) < iota((tracks, tracks), 1)
+    same = jnp.where(jnp.logical_and(owner_col == owner, earlier), 1.0, 0.0)
+    rank = jnp.sum(same, axis=0, keepdims=True).astype(jnp.int32)
+    target = owner * cap + rank
+    step = 2 * LANES
+    for at in range(0, hot_ref.shape[0], step):
+        hot = jnp.where(target == iota((step, tracks), 0) + at, 1.0, 0.0)
+        hot_ref[at : at + step, :] = hot.astype(BF16)
+
+
+def pack_kernel(
+    cap, road_dev, module_count, ld_hbm, gd_hbm, me_hbm, hw_hbm, hm_hbm, hc_hbm, tr_hbm,
+    out_ref, words_ref, parts_ref, mixed_ref, sorted_ref, hot_ref,
+    ld_ref, gd_ref, me_ref, hw_ref, hm_ref, hc_ref, tr_ref, sems,
 ):
-    tracks = in_ref.shape[1]
-    ld_at = NPAR * NHIT
-    me_at = ld_at + NLOC * NHIT
-    hw_at, hm_at, hc_at = me_at + NHIT, me_at + 2 * NHIT, me_at + 3 * NHIT
-    owned = in_ref[hc_at + 1 : hc_at + 2, :].astype(jnp.int32)
-    split = LANES // cap
-    words_all = rows_each * split
-    weight = jnp.where(
-        iota((NHIT, tracks), 0).astype(F32) < in_ref[hc_at : hc_at + 1, :],
-        in_ref[hw_at:hm_at, :], 0.0,
-    )
+    sources = (tr_hbm, hc_hbm, hw_hbm, ld_hbm, me_hbm, hm_hbm, gd_hbm)
+    targets = (tr_ref, hc_ref, hw_ref, ld_ref, me_ref, hm_ref, gd_ref)
+    copies = [
+        pltpu.make_async_copy(source, target, sems.at[num])
+        for num, (source, target) in enumerate(zip(sources, targets))
+    ]
+    for copy in copies:
+        copy.start()
+    copies[0].wait()
+    place_tracks(cap, road_dev, tr_ref[...], hot_ref)
+    for copy in copies[1:]:
+        copy.wait()
+    tracks = tr_ref.shape[1]
+    weight = jnp.where(iota((NHIT, tracks), 0) < hc_ref[...], hw_ref[...], 0.0)
     root = jnp.sqrt(weight)
-    scaled = [in_ref[ld_at + a * NHIT : ld_at + (a + 1) * NHIT, :] * root for a in range(NLOC)]
+    ahead = hm_ref[...] - tr_ref[...] * (ROAD // 2)
+    ahead = jnp.where(ahead < 0, ahead + module_count, ahead).astype(F32)
+    order = jnp.zeros((NHIT, tracks), F32)
+    for i in range(NHIT):
+        order = order + jnp.where(ahead[i : i + 1] < ahead, 1.0, 0.0)
+    for a in range(NLOC):
+        mixed_ref[:, a, :] = ld_ref[a] * root
+    mixed_ref[:, NLOC, :] = me_ref[...] * root
+    mixed_ref[:, NLOC + 1, :] = ahead
+    mixed_ref[:, NLOC + 2, :] = order
+    for at in range(0, tracks, LANES):
+        lanes = slice(at, at + LANES)
+        tiles = [mixed_ref[i, :, lanes] for i in range(NHIT)]
+        places = [jnp.broadcast_to(tile[NLOC + 2 : NLOC + 3], (8, LANES)) for tile in tiles]
+        derivs = [gd_ref[i, :, lanes] * root[i : i + 1, lanes] for i in range(NHIT)]
+        for k in range(NHIT):
+            tile, deriv = tiles[0], derivs[0]
+            for i in range(1, NHIT):
+                here = places[i] == float(k)
+                tile = jnp.where(here, tiles[i], tile)
+                deriv = jnp.where(here, derivs[i], deriv)
+            sorted_ref[k, :, lanes] = tile
+            row = derivative_row(k)
+            words_ref[row : row + NPAR, lanes] = deriv
+    scaled = [sorted_ref[:, a, :] for a in range(NLOC)]
     factor = {}
     for a in range(NLOC):
         for b in range(a + 1):
@@ -93,73 +150,61 @@
         for b in range(a):
             running = running - factor[a, b] * proj[b]
         proj.append(running / factor[a, a])
-    residual = in_ref[me_at:hw_at, :] * root
+    residual = sorted_ref[:, NLOC, :]
     solved = residual
     for a in range(NLOC):
         solved = solved - proj[a] * jnp.sum(proj[a] * residual, axis=0, keepdims=True)
-    proj = householder(proj, 0, 0)
-    proj = householder(proj, 1, 1)
-    for i in range(NHIT):
-        words_ref[i * NPAR : (i + 1) * NPAR, :] = in_ref[i * NPAR : (i + 1) * NPAR, :] * root[i : i + 1]
-    words_ref[W_SOLVED:W_SLOT, :] = solved
-    words_ref[W_SLOT:W_ROAD, :] = (in_ref[hm_at:hc_at, :].astype(jnp.int32) & (ROAD - 1)).astype(F32)
-    owner = owned // road_dev
-    words_ref[W_ROAD:W_PROJ0, :] = (owned - owner * road_dev + 1).astype(F32)
-    words_ref[W_PROJ0:W_PROJ1, :] = proj[0][0:1]
-    words_ref[W_PROJ1 : W_PROJ1 + 1, :] = proj[0][1:2]
-    words_ref[W_PROJ1 + 1 : W_PROJ, :] = proj[1][1:2]
+    for a in range(NLOC - 1):
+        proj = householder(proj, a, a)
+    ahead = sorted_ref[:, NLOC + 1, :]
+    skipped = ahead - ahead[0:1] - iota((NHIT, tracks), 0).astype(F32)
+    words_ref[R_ROAD:R_FIRST, :] = (tr_ref[...] % road_dev + 1).astype(F32)
+    words_ref[R_FIRST:USED, :] = ahead[0:1]
+    words_ref[USED:PART, :] = jnp.zeros((PART - USED, tracks), F32)
+    words_ref[R_SOLVED:R_GAP, :] = solved
+    for gap in range(GAPS):
+        words_ref[R_GAP + gap : R_GAP + gap + 1, :] = jnp.sum(
+            jnp.where(skipped < gap + 0.5, 1.0, 0.0), axis=0, keepdims=True
+        )
     for a in range(NLOC):
-        at = W_PROJ + a * (NHIT - 2)
-        words_ref[at : at + NHIT - 2, :] = proj[a][2:]
-    words_ref[WORDS:, :] = jnp.zeros((words_all - WORDS, tracks), F32)
+        words_ref[R_PROJ[a] : R_PROJ[a] + NHIT - a, :] = proj[a][a:]
+    words_ref[PART + USED :, :] = jnp.zeros((PART - USED, tracks), F32)
     for num, part in enumerate(split_three(words_ref[...])):
-        parts_ref[num * words_all : (num + 1) * words_all, :] = part
-    owner_col = jnp.concatenate(
-        [
-            jnp.broadcast_to(owner[:, at : at + LANES], (LANES, LANES)).astype(F32).T[:, :1]
-            for at in range(0, tracks, LANES)
-        ],
-        axis=0,
-    ).astype(jnp.int32)
-    earlier = iota((tracks, tracks), 0) < iota((tracks, tracks), 1)
-    same = jnp.where(jnp.logical_and(owner_col == owner, earlier), 1.0, 0.0)
-    rank = jnp.sum(same, axis=0, keepdims=True).astype(jnp.int32)
-    target = owner * cap + rank
-    blocks = out_ref.shape[0] // split
-    lane_part = iota((rows_each, LANES), 1) // cap
-    per = 2
-    for pair in range(blocks // per):
-        hot = jnp.where(
-            target == iota((per * LANES, tracks), 0) + pair * per * LANES, 1.0, 0.0
-        ).astype(BF16)
-        moved = dot(parts_ref[...], hot, 1, 1)
-        moved = moved[:words_all] + moved[words_all : 2 * words_all] + moved[2 * words_all :]
-        for sub in range(per):
-            block = moved[:, sub * LANES : (sub + 1) * LANES]
-            for k in range(split):
-                made = None
-                for m in range(split):
-                    piece = block[m * rows_each : (m + 1) * rows_each]
-                    if m != k:
-                        piece = pltpu.roll(piece, (cap * (m - k)) % LANES, 1)
-                    made = piece if made is None else jnp.where(lane_part == m, piece, made)
-                out_ref[(pair * per + sub) * split + k] = made
+        parts_ref[num * ROWS : (num + 1) * ROWS, :] = part
+    lower_half = iota((USED, LANES), 1) < LANES // 2
+    step = 2 * LANES
+    for at in range(0, hot_ref.shape[0], step):
+        moved = dot(parts_ref[...], hot_ref[at : at + step, :], 1, 1)
+        moved = moved[:ROWS] + moved[ROWS : 2 * ROWS] + moved[2 * ROWS :]
+        if not folded(cap):
+            out_ref[:, at : at + step] = moved
+            continue
+        for sub in range(2):
+            lanes = slice(sub * LANES, (sub + 1) * LANES)
+            one = moved[:USED, lanes]
+            two = moved[PART : PART + USED, lanes]
+            row = (at // LANES + sub) * 2 * USED
+            out_ref[row : row + USED] = jnp.where(lower_half, one, pltpu.roll(two, LANES // 2, 1))
+            out_ref[row + USED : row + 2 * USED] = jnp.where(
+                lower_half, pltpu.roll(one, LANES // 2, 1), two
+            )
+
+
+def folded(cap):
+    return 2 * cap == LANES
 
 
 def sort_kernel(cap, recv_ref, off_ref, list_ref, item_ref, bound_ref, off_out_ref, road_ref):
-    split = LANES // cap
     roads = off_ref.shape[0]
     blocks = road_ref.shape[0]
-    lane_part = iota((1, LANES), 1) // cap
-    shift_of = road_part(cap)
-    for e in range(blocks):
-        made = None
-        for k in range(split):
-            piece = recv_ref[e * split + k, 0:1, :]
-            if k != shift_of:
-                piece = pltpu.roll(piece, (cap * (k - shift_of)) % LANES, 1)
-            made = piece if made is None else jnp.where(lane_part == k, piece, made)
-        road_ref[e : e + 1, :] = made
+    if folded(cap):
+        even = recv_ref[pl.ds(R_ROAD, blocks, stride=2 * USED), :]
+        odd = recv_ref[pl.ds(R_ROAD + USED, blocks, stride=2 * USED), :]
+        lower_half = iota((blocks, LANES), 1) < LANES // 2
+        road_ref[...] = jnp.where(lower_half, even, pltpu.roll(odd, LANES // 2, 1))
+    else:
+        for e in range(blocks):
+            road_ref[e : e + 1, :] = recv_ref[R_ROAD : R_ROAD + 1, e * LANES : (e + 1) * LANES]
     road_num = (iota((roads, LANES), 0) + 1).astype(F32)
     upper = jnp.where(iota((LANES, LANES), 0) < iota((LANES, LANES), 1), 1.0, 0.0).astype(BF16)
     offset = off_ref[...]
@@ -210,60 +255,48 @@
     bound_ref[...] = jnp.broadcast_to(bound, bound_ref.shape).astype(jnp.int32)
 
 
-def rows_of(cap):
-    split = LANES // cap
-    least = -(-WORDS // split)
-    return -(-least // 8) * 8
-
-
-def road_part(cap):
-    return W_ROAD // rows_of(cap)
-
-
-def lay_tiles(cap, recv_ref, off_ref, tiles_ref, words_ref):
-    split = LANES // cap
-    rows_each = recv_ref.shape[1]
+def lay_tiles(cap, recv_ref, off_ref, tiles_ref, words_ref, shift_ref):
     blocks = off_ref.shape[0]
     width = ROAD * NPAR
-    lane_part = iota((rows_each, LANES), 1) // cap
+    lower_half = iota((USED, LANES), 1) < LANES // 2
+    slot_num = iota((ROAD, LANES), 0)
     tiles_ref[blocks * LANES] = jnp.zeros((8, width), F32)
-
-    def lay(e, held):
+    shift_ref[:, :8, :] = jnp.full((2, 8, LANES), -1.0, F32)
+
+    def lay(num, held):
         words = words_ref.at[held]
-        for m in range(split):
-            made = None
-            for k in range(split):
-                piece = recv_ref[e * split + k]
-                if k != m:
-                    piece = pltpu.roll(piece, (cap * (k - m)) % LANES, 1)
-                made = piece if made is None else jnp.where(lane_part == k, piece, made)
-            words[m * rows_each : (m + 1) * rows_each, :] = made
-        offset = off_ref[pl.ds(e, 1), :]
-        slots = []
-        for i in range(NHIT):
-            slot = words[W_SLOT + i : W_SLOT + i + 1, :] - offset
-            slots.append(jnp.where(slot < 0.0, slot + ROAD, slot))
+        shifts = shift_ref.at[held]
+        e = 2 * num + held
+        if folded(cap):
+            both = recv_ref.at[pl.ds(pl.multiple_of(num * 4 * USED, 8), 4 * USED)]
+            one = both[held * 2 * USED : held * 2 * USED + USED, :]
+            two = both[held * 2 * USED + USED : held * 2 * USED + 2 * USED, :]
+            words[:USED] = jnp.where(lower_half, one, pltpu.roll(two, LANES // 2, 1))
+            words[PART : PART + USED] = jnp.where(lower_half, pltpu.roll(one, LANES // 2, 1), two)
+        else:
+            words[...] = recv_ref[:, pl.ds(pl.multiple_of(e * LANES, LANES), LANES)]
+        shift = words[R_FIRST : R_FIRST + 1, :] - off_ref[pl.ds(e, 1), :]
+        for gap in range(GAPS):
+            reached = slot_num.astype(F32) >= words[R_GAP + gap : R_GAP + gap + 1, :]
+            shift = shift + jnp.where(reached, 1.0, 0.0)
+        shifts[8 : 8 + ROAD] = jnp.where(slot_num < NHIT, shift, -1.0)
         laid = [jnp.zeros((NPAR, LANES), F32) for s in range(ROAD)]
         for i in range(NHIT):
-            value = words[i * NPAR : (i + 1) * NPAR, :]
-            wide = jnp.broadcast_to(slots[i], (NPAR, LANES))
-            for s in range(ROAD):
-                laid[s] = jnp.where(wide == float(s), value, laid[s])
-        slot_num = iota((ROAD, LANES), 0).astype(F32)
+            row = derivative_row(i)
+            value = words[row : row + NPAR, :]
+            wide = jnp.broadcast_to(shifts[8 + i : 9 + i, :], (NPAR, LANES))
+            for move in range(GAPS + 1):
+                laid[i + move] = jnp.where(wide == float(move), value, laid[i + move])
         placed = [jnp.zeros((ROAD, LANES), F32) for a in range(NLOC + 1)]
-        for i in range(NHIT):
-            match = slots[i] == slot_num
+        for move in range(GAPS + 1):
+            match = shifts[8 - move : 8 - move + ROAD, :] == float(move)
             for a in range(NLOC + 1):
                 if a == NLOC:
-                    at = W_SOLVED + i
-                elif i == 0:
-                    at = W_PROJ0 if a == 0 else None
-                elif i == 1:
-                    at = W_PROJ1 + a if a < 2 else None
+                    row, valid = R_SOLVED - move, match
                 else:
-                    at = W_PROJ + a * (NHIT - 2) + i - 2
-                if at is not None:
-                    placed[a] = jnp.where(match, words[at : at + 1, :], placed[a])
+                    row = R_PROJ[a] - a - move
+                    valid = jnp.logical_and(match, slot_num >= a + move) if a else match
+                placed[a] = jnp.where(valid, words[row : row + ROAD, :], placed[a])
         start = pl.multiple_of(e * LANES, LANES)
         for a in range(NLOC + 1):
             mixed = jnp.concatenate([laid[s] * placed[a][s : s + 1] for s in range(ROAD)], axis=0)
@@ -272,8 +305,8 @@
         tiles_ref[pl.ds(start, LANES), SUM_ROW + 1, :] = jnp.zeros((LANES, width), F32)
 
     def lay_two(num, carry):
-        lay(2 * num, 0)
-        lay(2 * num + 1, 1)
+        lay(num, 0)
+        lay(num, 1)
         return carry
 
     lax.fori_loop(0, blocks // 2, lay_two, 0)
@@ -327,11 +360,11 @@
 
 def edge_kernel(
     cap, bound_ref, list_ref, item_ref, recv_ref, off_ref, off_rows_ref, prior_ref,
-    tiles_ref, out_ref, sums_ref, to_next_ref, to_prev_ref, words_ref, held_ref,
+    tiles_ref, out_ref, sums_ref, to_next_ref, to_prev_ref, words_ref, shift_ref, held_ref,
 ):
     roads, width = sums_ref.shape
     edge = roads // GROUPS
-    lay_tiles(cap, recv_ref, off_ref, tiles_ref, words_ref)
+    lay_tiles(cap, recv_ref, off_ref, tiles_ref, words_ref, shift_ref)
     step = item_steps(list_ref, item_ref, tiles_ref, out_ref, held_ref)
     for group in (0, GROUPS - 1):
         begin, end = bound_ref[group], bound_ref[group + 1]
@@ -607,59 +640,60 @@
     tracks = hit_count.shape[0]
     modules = prior_weight.shape[0]
     cap = 4 * tracks // devices
-    split = LANES // cap
-    rows_each = rows_of(cap)
     slots = devices * cap
     width = ROAD * NPAR
     half = modules // ROAD
     vmem = pl.BlockSpec(memory_space=pltpu.VMEM)
     smem = pl.BlockSpec(memory_space=pltpu.SMEM)
     limit = pltpu.CompilerParams(vmem_limit_bytes=32 * 1024 * 1024)
+    large = pltpu.CompilerParams(vmem_limit_bytes=LARGE * 1024 * 1024)
     small = pltpu.CompilerParams(vmem_limit_bytes=12 * 1024 * 1024)
 
-    sent = [
-        jnp.transpose(global_deriv, (1, 0, 2)).reshape(NHIT * NPAR, tracks),
-        local_deriv.reshape(NLOC * NHIT, tracks), measured, hit_weight, hit_module.astype(F32),
-        hit_count.astype(F32)[None, :], track_road.astype(F32)[None, :],
-    ]
-    sent = jnp.concatenate(sent)
+    sent = (
+        local_deriv, jnp.transpose(global_deriv, (1, 0, 2)), measured, hit_weight, hit_module,
+        hit_count[None, :], track_road[None, :],
+    )
+    message = (devices * USED, LANES) if folded(cap) else (ROWS, slots)
     send = pl.pallas_call(
-        functools.partial(send_kernel, cap, roads, rows_each),
-        out_shape=shape(devices, rows_each, LANES),
-        in_specs=[vmem],
+        functools.partial(pack_kernel, cap, roads, modules * devices),
+        out_shape=shape(*message),
+        in_specs=[pl.BlockSpec(memory_space=pltpu.HBM)] * len(sent),
         out_specs=vmem,
         scratch_shapes=[
-            pltpu.VMEM((rows_each * split, tracks), F32),
-            pltpu.VMEM((3 * rows_each * split, tracks), BF16),
+            pltpu.VMEM((ROWS, tracks), F32),
+            pltpu.VMEM((3 * ROWS, tracks), BF16),
+            pltpu.VMEM((NHIT, 8, tracks), F32),
+            pltpu.VMEM((NHIT, 8, tracks), F32),
+            pltpu.VMEM((slots, tracks), BF16),
+            *(pltpu.VMEM(x.shape, x.dtype) for x in sent),
+            pltpu.SemaphoreType.DMA((len(sent),)),
         ],
-        compiler_params=limit,
+        compiler_params=large,
         name="fit_and_pack",
-    )(sent)
+    )(*sent)
+    if folded(cap):
+        send = send.reshape(devices, USED, 1, LANES)
+    else:
+        send = jnp.transpose(send.reshape(ROWS, devices, cap), (1, 0, 2))
     recv = lax.all_to_all(send, AXES, split_axis=0, concat_axis=0, tiled=True)
-
-    offset = road_start % ROAD
+    if folded(cap):
+        recv = recv.reshape(message)
+    else:
+        recv = jnp.transpose(recv, (1, 0, 2)).reshape(message)
+
+    offset = road_start % (ROAD // 2)
     list_rows = ((PER_ITEM * roads + slots) // (8 * LANES) + 1) * 8
     item_rows = -(-(list_rows * LANES // PER_ITEM) // (8 * LANES)) * 8
-    road_row = W_ROAD % rows_each
     track_list, items, bounds, track_off = pl.pallas_call(
         functools.partial(sort_kernel, cap),
-        grid=(1,),
         out_shape=(
             shape(list_rows, LANES, dtype=jnp.int32),
             shape(item_rows, LANES, dtype=jnp.int32),
             shape(8, LANES, dtype=jnp.int32),
             shape(slots // LANES, LANES),
         ),
-        in_specs=[
-            pl.BlockSpec((devices, 8, LANES), lambda i: (0, road_row // 8, 0)),
-            pl.BlockSpec((roads, 1), lambda i: (0, 0)),
-        ],
-        out_specs=(
-            pl.BlockSpec((list_rows, LANES), lambda i: (0, 0)),
-            pl.BlockSpec((item_rows, LANES), lambda i: (0, 0)),
-            pl.BlockSpec((8, LANES), lambda i: (0, 0)),
-            pl.BlockSpec((slots // LANES, LANES), lambda i: (0, 0)),
-        ),
+        in_specs=[vmem] * 2,
+        out_specs=(vmem,) * 4,
         scratch_shapes=[pltpu.VMEM((slots // LANES, LANES), F32)],
         compiler_params=limit,
         name="sort_by_road",
@@ -667,7 +701,7 @@
 
     edge = roads // GROUPS
     prior = prior_weight.reshape(half, width)
-    off_rows = jnp.broadcast_to((offset % (ROAD // 2)).astype(F32)[:, None], (roads, LANES))
+    off_rows = jnp.broadcast_to(offset.astype(F32)[:, None], (roads, LANES))
     lists = (bounds.reshape(-1), track_list.reshape(-1), items.reshape(-1))
     halo = 4 * EDGE + EDGE
     tiles, edge_blocks, edge_sums, to_next, to_prev = pl.pallas_call(
@@ -679,7 +713,8 @@
         in_specs=[smem] * 3 + [vmem] * 4,
         out_specs=(vmem,) * 5,
         scratch_shapes=[
-            pltpu.VMEM((2, rows_each * split, LANES), F32),
+            pltpu.VMEM((2, ROWS, LANES), F32),
+            pltpu.VMEM((2, 8 + ROAD, LANES), F32),
             pltpu.VMEM((roads, 8, width), F32),
         ],
         compiler_params=small,
@@ -726,6 +761,7 @@
         in_specs=[vmem] * 3,
         out_specs=pl.BlockSpec(memory_space=pltpu.HBM),
         scratch_shapes=[pltpu.VMEM((NPAR, modules), F32), pltpu.SemaphoreType.DMA],
+        compiler_params=pltpu.CompilerParams(vmem_limit_bytes=4 * 1024 * 1024),
         name="combine",
     )(*summed)
     return (normal_blocks, rhs, corrections.T)

time: 105 us -> 94.7 us (0.902); the launches traced: 107 us -> 94.3 us
  local copies, waits for them, and re-layouts: 9.09 us -> 3.64 us
  Pallas kernels: 42.1 us -> 36.8 us
  other arithmetic: 2.83 us -> 0.69 us
  starting transfers between devices: 15.2 us -> 16.6 us
    pallas_call x1, Pallas kernels: 13.5 us -> 10.4 us  [on_device(): pl.pallas_call(inner_kernel, out_shape=(shape(roads, width, width), shape...]
    convert_element_type x4 -> x0, other arithmetic: 2.83 us -> none  [the longest x1 0.76 us: on_device(): hit_module.astype(F32)]
    concatenate x1 -> x0, local copies, waits for them, and re-layouts: 2.66 us -> none  [on_device(): sent = jnp.concatenate(sent)]
    pallas_call x1, Pallas kernels: 10.1 us -> 7.75 us  [on_device(): pl.pallas_call(functools.partial(edge_kernel, cap), out_shape=(shape(slot...]
    all_to_all x1, waiting for transfers between devices: 32.5 us -> 30.4 us  [on_device(): recv = lax.all_to_all(send, AXES, split_axis=0, concat_axis=0, tiled=True)]
    pallas_call x2, Pallas kernels: 5.22 us -> 6.66 us  [the longest x1 4.65 us: on_device(): pl.pallas_call(functools.partial(pack_kernel, cap, roads, modules * devic...]
    all_to_all x1, starting transfers between devices: 2.54 us -> 3.9 us  [on_device(): lax.all_to_all(dots, AXES, split_axis=0, concat_axis=0, tiled=True)]
    all_to_all x1, waiting for transfers between devices: 4.05 us -> 5.31 us  [on_device(): lax.all_to_all(dots, AXES, split_axis=0, concat_axis=0, tiled=True)]
  transfers between devices with their start and end apart: 4 -> 4, of which waited for: 2 -> 2; matrix products, arithmetic and copies ran while one was open for 5% -> 4% of each run, Pallas kernels for 13% -> 11%
where the time goes in v3:
time: 94.7 us; the launch traced here: 94.3 us
  Pallas kernels  36.8 us (39%)
  waiting for transfers between devices  35.7 us (38%)
  starting transfers between devices  16.6 us (18%)
  local copies, waits for them, and re-layouts  3.64 us (4%)
    all_to_all x1, waiting for transfers between devices, on_device(): recv = lax.all_to_all(send, AXES, split_axis=0, concat_axis=0, tiled=True)  30.4 us
    pallas_call x1, Pallas kernels, on_device(): pl.pallas_call(krylov_kernel, out_shape=(shape(half, width), shape(half,...  10.5 us
    pallas_call x1, Pallas kernels, on_device(): pl.pallas_call(inner_kernel, out_shape=(shape(roads, width, width), shape...  10.4 us
    pallas_call x1, Pallas kernels, on_device(): pl.pallas_call(functools.partial(edge_kernel, cap), out_shape=(shape(slot...  7.75 us
    all_to_all x1, starting transfers between devices, on_device(): recv = lax.all_to_all(send, AXES, split_axis=0, concat_axis=0, tiled=True)  7.3 us
    ppermute x2, starting transfers between devices, neighbour(): lax.ppermute(value, AXES, [(s, (s + steps) % count) for s in range(count)])  5.39 us
    all_to_all x1, waiting for transfers between devices, on_device(): lax.all_to_all(dots, AXES, split_axis=0, concat_axis=0, tiled=True)  5.31 us
    pallas_call x1, Pallas kernels, on_device(): pl.pallas_call(functools.partial(pack_kernel, cap, roads, modules * devic...  4.65 us
  transfers between devices with their start and end apart: 4, of which 2 were waited for; matrix products, arithmetic and copies ran while one was open for 4% of the time, Pallas kernels for 11%

profile of v3, /device:TPU:0, one launch (start us, length us, event | category | flops | bytes accessed | tf_op | source)
XLA Modules:
  0.0 94.3 jit_solution(6103028203920557226)
XLA Ops:
  0.6 4.7 %fit_and_pack.1 = f32[2624,128]{1,0:T(8,128)} custom-call(f32[5,12,512]{2,1,0:T(8,128)} %ld_hbm.1, f32[12,8,512]{2,1,0:T(8,128)} %bitcast.25, f32[12,512]{1,0:T(8,128)} %me_hbm.1, f32[12,512]{1,0:T(8,128)} %hw_hbm.1, s32[12,512]{1,0:T(8,128)} %hm_hbm.1, s32[1,512]{1,0:T(1,128)} %bitcast.28, s32[1,512]{1,0:T(1,128)} %bitcast.29), custom_call_target="tpu_custom_call" | custom-call | tf_op jit(solution)/shard_map/fit_and_pack/pallas_call | solution.py:657
  5.3 7.3 %all-to-all-start = ((f32[32,82,1,128]{3,2,1,0:T(1,128)}), f32[32,82,1,128]{3,2,1,0:T(1,128)S(1)}, u32[]{:S(2)}, u32[]{:S(2)}) async-start(f32[32,82,1,128]{3,2,1,0:T(1,128)} %bitcast.24), calls=%async_computation | async-start | bytes 2686976 | tf_op jit(solution)/shard_map/all_to_all | solution.py:678
  12.6 0.7 fusion
  13.3 0.1 copy.23.off_ref
  13.4 1.2 %copy.24 = f32[2048,8]{1,0:T(8,128)S(1)} copy(f32[2048,8]{0,1:T(8,128)} %param.17) | data formatting | bytes 131072 | tf_op args[8]
  14.6 0.5 reshape.39.prior_ref
  15.1 30.4 %all-to-all-done = f32[32,82,1,128]{3,2,1,0:T(1,128)S(1)} async-done(((f32[32,82,1,128]{3,2,1,0:T(1,128)}), f32[32,82,1,128]{3,2,1,0:T(1,128)S(1)}, u32[]{:S(2)}, u32[]{:S(2)}) %all-to-all-start) | async-done | bytes 1343520 | tf_op jit(solution)/shard_map/all_to_all | solution.py:678
  45.5 2.0 %sort_by_road.1 = (s32[40,128]{1,0:T(8,128)S(1)}, s32[8,128]{1,0:T(8,128)S(1)}, s32[8,128]{1,0:T(8,128)S(1)}, f32[16,128]{1,0:T(8,128)S(1)}) custom-call(f32[2624,128]{1,0:T(8,128)S(1)} %bitcast.13, f32[256,1]{1,0:T(8,128)S(1)} %copy.23.off_ref), custom_call_target="tpu_custom_call" | custom-call | tf_op jit(solution)/shard_map/sort_by_road/pallas_call | solution.py:687
  47.5 0.1 broadcast_in_dim.18.off_rows_ref.off_ref
  47.6 7.7 %lay_and_assemble_edges.1 = (f32[2056,8,128]{2,1,0:T(8,128)S(1)}, f32[256,128,128]{2,1,0:T(8,128)S(1)}, f32[256,128]{1,0:T(8,128)S(1)}, f32[552,128]{1,0:T(8,128)S(1)}, f32[296,128]{1,0:T(8,128)S(1)}) custom-call(s32[1024]{0:T(1024)S(1)} %bitcast.22, s32[5120]{0:T(1024)S(1)} %bitcast.17, s32[1024]{0:T(1024)S(1)} %bitcast.20, f32[2624,128]{1,0:T(8,128)S(1)} %bitcast.14, ...), custom_call_target="tpu_custom_call" | custom-call | tf_op jit(solution)/shard_map/lay_and_assemble_edges/pallas_call | solution.py:707
  55.4 0.1 collective-permute-start
  55.4 5.3 %collective-permute-start.1 = (f32[296,128]{1,0:T(8,128)S(1)}, f32[296,128]{1,0:T(8,128)S(1)}, u32[]{:S(2)}, u32[]{:S(2)}) collective-permute-start(f32[296,128]{1,0:T(8,128)S(1)} %get-tuple-element.29), channel_id=1, source_target_pairs={{0,31},{1,0},{2,1},{3,2},{4,3},{5,4},{6,5},{7,6},{8,7},{9,8},{10,9... | collective-permute-start | bytes 454664 | tf_op jit(solution)/shard_map/ppermute | solution.py:627
  60.7 10.4 %assemble_blocks.1 = (f32[256,128,128]{2,1,0:T(8,128)}, f32[256,128,128]{2,1,0:T(8,128)S(1)}, f32[256,128]{1,0:T(8,128)S(1)}) custom-call(s32[1024]{0:T(1024)S(1)} %bitcast.23, s32[5120]{0:T(1024)S(1)} %bitcast.18, s32[1024]{0:T(1024)S(1)} %bitcast.21, ...), custom_call_target="tpu_custom_call", output_to_operand_aliasing={{1}: (4, {}), {2}: (5, {})} | custom-call | tf_op jit(solution)/shard_map/assemble_blocks/pallas_call | solution.py:725
  71.1 0.0 collective-permute-done.1.from_next_ref
  71.1 0.0 collective-permute-done.from_prev_ref
  71.2 10.5 %two_products.1 = (f32[128,128]{1,0:T(8,128)S(1)}, f32[128,128]{1,0:T(8,128)S(1)}, f32[32,1,128]{2,1,0:T(1,128)}) custom-call(f32[256,128,128]{2,1,0:T(8,128)S(1)} %get-tuple-element.26.held, f32[256,128]{1,0:T(8,128)S(1)} %get-tuple-element.27.sums_ref, f32[256,128]{1,0:T(8,128)S(1)} %broadcast_in_dim.18.off_rows_ref.off_ref, ...), custom_call_target="tpu_custom_call" | custom-call | tf_op jit(solution)/shard_map/two_products/pallas_call | solution.py:746
  81.7 3.9 %all-to-all-start.1 = ((f32[32,1,128]{2,1,0:T(1,128)}), f32[32,1,128]{2,1,0:T(1,128)S(1)}, u32[]{:S(2)}, u32[]{:S(2)}) async-start(f32[32,1,128]{2,1,0:T(1,128)} %get-tuple-element.31), calls=%async_computation.1 | async-start | bytes 32768 | tf_op jit(solution)/shard_map/all_to_all | solution.py:755
  85.6 0.6 reshape.40
  86.2 0.3 copy.27
  86.5 0.0 copy-start
  86.5 0.6 reshape.42
  87.1 0.3 copy.26
  87.4 5.3 %all-to-all-done.1 = f32[32,1,128]{2,1,0:T(1,128)S(1)} async-done(((f32[32,1,128]{2,1,0:T(1,128)}), f32[32,1,128]{2,1,0:T(1,128)S(1)}, u32[]{:S(2)}, u32[]{:S(2)}) %all-to-all-start.1) | async-done | bytes 16416 | tf_op jit(solution)/shard_map/all_to_all | solution.py:755
  92.7 1.5 %combine.1 = f32[8,2048]{1,0:T(8,128)} custom-call(f32[32,128]{1,0:T(8,128)S(1)} %bitcast.19, f32[8,2048]{1,0:T(8,128)S(1)} %bitcast.15, f32[8,2048]{1,0:T(8,128)S(1)} %bitcast.16), custom_call_target="tpu_custom_call" | custom-call | tf_op jit(solution)/shard_map/combine/pallas_call | solution.py:758
  94.2 0.0 copy-done
Async XLA Ops:
  5.3 40.2 %all-to-all-start = ((f32[32,82,1,128]{3,2,1,0:T(1,128)}), f32[32,82,1,128]{3,2,1,0:T(1,128)S(1)}, u32[]{:S(2)}, u32[]{:S(2)}) async-start(f32[32,82,1,128]{3,2,1,0:T(1,128)} %bitcast.24), calls=%async_computation | async-start | bytes 2686976 | tf_op jit(solution)/shard_map/all_to_all | solution.py:678
  55.4 15.8 %collective-permute-start = (f32[552,128]{1,0:T(8,128)S(1)}, f32[552,128]{1,0:T(8,128)S(1)}, u32[]{:S(2)}, u32[]{:S(2)}) collective-permute-start(f32[552,128]{1,0:T(8,128)S(1)} %get-tuple-element.28), channel_id=1, source_target_pairs={{0,1},{1,2},{2,3},{3,4},{4,5},{5,6},{6,7},{7,8},{8,9},{9,10},{10,1... | collective-permute-start | bytes 847880 | tf_op jit(solution)/shard_map/ppermute | solution.py:627
  55.4 15.7 %collective-permute-start.1 = (f32[296,128]{1,0:T(8,128)S(1)}, f32[296,128]{1,0:T(8,128)S(1)}, u32[]{:S(2)}, u32[]{:S(2)}) collective-permute-start(f32[296,128]{1,0:T(8,128)S(1)} %get-tuple-element.29), channel_id=1, source_target_pairs={{0,31},{1,0},{2,1},{3,2},{4,3},{5,4},{6,5},{7,6},{8,7},{9,8},{10,9... | collective-permute-start | bytes 454664 | tf_op jit(solution)/shard_map/ppermute | solution.py:627
  81.7 11.0 %all-to-all-start.1 = ((f32[32,1,128]{2,1,0:T(1,128)}), f32[32,1,128]{2,1,0:T(1,128)S(1)}, u32[]{:S(2)}, u32[]{:S(2)}) async-start(f32[32,1,128]{2,1,0:T(1,128)} %get-tuple-element.31), calls=%async_computation.1 | async-start | bytes 32768 | tf_op jit(solution)/shard_map/all_to_all | solution.py:755
  86.5 7.7 %copy-start = (f32[2048,8]{0,1:T(8,128)}, f32[2048,8]{0,1:T(8,128)S(1)}, u32[]{:S(2)}) copy-start(f32[2048,8]{0,1:T(8,128)S(1)} %copy.27) | copy-start | bytes 196612

commit v4 on v3

--- a/solution.py
+++ b/solution.py
@@ -52,12 +52,9 @@
     )
 
 
-def split_three(value):
+def split_two(value):
     high = value.astype(BF16)
-    rest = value - high.astype(F32)
-    middle = rest.astype(BF16)
-    low = (rest - middle.astype(F32)).astype(BF16)
-    return high, middle, low
+    return high, (value - high.astype(F32)).astype(BF16)
 
 
 def householder(rows, first, column):
@@ -169,13 +166,13 @@
     for a in range(NLOC):
         words_ref[R_PROJ[a] : R_PROJ[a] + NHIT - a, :] = proj[a][a:]
     words_ref[PART + USED :, :] = jnp.zeros((PART - USED, tracks), F32)
-    for num, part in enumerate(split_three(words_ref[...])):
+    for num, part in enumerate(split_two(words_ref[...])):
         parts_ref[num * ROWS : (num + 1) * ROWS, :] = part
     lower_half = iota((USED, LANES), 1) < LANES // 2
     step = 2 * LANES
     for at in range(0, hot_ref.shape[0], step):
         moved = dot(parts_ref[...], hot_ref[at : at + step, :], 1, 1)
-        moved = moved[:ROWS] + moved[ROWS : 2 * ROWS] + moved[2 * ROWS :]
+        moved = moved[:ROWS] + moved[ROWS:]
         if not folded(cap):
             out_ref[:, at : at + step] = moved
             continue
@@ -315,31 +312,25 @@
 def item_steps(list_ref, item_ref, tiles_ref, out_ref, held_ref):
     width = ROAD * NPAR
     row_kind = iota((PER_ITEM * 8, width), 0) % 8
-    is_proj = row_kind < NLOC
-    is_own = row_kind == NLOC
+    proj = jnp.where(row_kind < NLOC, 1.0, 0.0).astype(BF16)
+    own = jnp.where(row_kind == NLOC, 1.0, 0.0).astype(BF16)
     same_slot = iota((width, width), 0) // NPAR == iota((width, width), 1) // NPAR
     spare = list_ref.shape[0] // PER_ITEM - 1
 
-    def step(begin, end, num):
+    def step(item_at, count, num):
         for u in range(UNROLL):
-            item = begin + num * UNROLL + u
-            live = item < end
-            item = jnp.where(live, item, spare)
+            item = num * UNROLL + u
+            live = item < count
+            item = jnp.where(live, item_at(item), spare)
             info = item_ref[item]
             first = (info & 1) == 1
             road = jnp.where(live, info >> 1, 0)
             at = item * PER_ITEM
             parts = [tiles_ref[list_ref[at + j]] for j in range(PER_ITEM)]
             tall = jnp.concatenate(parts, axis=0)
-            high = tall.astype(BF16)
-            high32 = high.astype(F32)
-            low32 = tall - high32
-            low = low32.astype(BF16)
+            high, low = split_two(tall)
             left = jnp.concatenate([high, high, low], axis=0)
-            high_p = jnp.where(is_proj, high32, 0.0).astype(BF16)
-            high_o = jnp.where(is_own, high32, 0.0).astype(BF16)
-            low_p = jnp.where(is_proj, low32, 0.0).astype(BF16)
-            low_o = jnp.where(is_own, low32, 0.0).astype(BF16)
+            high_p, low_p, high_o, low_o = high * proj, low * proj, high * own, low * own
             right = jnp.concatenate(
                 [
                     jnp.concatenate([high_p, low_p, high_p], axis=0),
@@ -366,14 +357,15 @@
     edge = roads // GROUPS
     lay_tiles(cap, recv_ref, off_ref, tiles_ref, words_ref, shift_ref)
     step = item_steps(list_ref, item_ref, tiles_ref, out_ref, held_ref)
-    for group in (0, GROUPS - 1):
-        begin, end = bound_ref[group], bound_ref[group + 1]
-
-        def body(num, carry, begin=begin, end=end):
-            step(begin, end, num)
-            return carry
-
-        lax.fori_loop(0, (end - begin + UNROLL - 1) // UNROLL, body, 0)
+    low = bound_ref[1]
+    high = bound_ref[GROUPS - 1]
+    count = low + bound_ref[GROUPS] - high
+
+    def body(num, carry):
+        step(lambda item: jnp.where(item < low, item, item - low + high), count, num)
+        return carry
+
+    lax.fori_loop(0, (count + UNROLL - 1) // UNROLL, body, 0)
     sums_ref[:edge] = held_ref[:edge, SUM_ROW, :]
     sums_ref[roads - edge :] = held_ref[roads - edge :, SUM_ROW, :]
     two = 2 * EDGE
@@ -411,7 +403,7 @@
         until = (bound_ref[group + 2] - begin + UNROLL - 1) // UNROLL
 
         def body(num, carry):
-            step(begin, end, num)
+            step(lambda item: item + begin, end - begin, num)
             return carry
 
         lax.fori_loop(done, until, body, 0)
@@ -475,13 +467,10 @@
 def krylov_kernel(
     held, sums_ref, off_ref, prior_ref, from_prev_ref, from_next_ref,
     first_ref, second_ref, dots_ref,
-    even_sum, odd_sum, even_off, odd_off, prior, even_part, odd_part, turned_even,
-    turned_odd,
+    even_sum, odd_sum, even_off, odd_off, prior, even_part, odd_part, held_halves, edge_halves,
 ):
     roads, width = sums_ref.shape
     half = roads // 2
-    each = min(roads, 64)
-    chunks = roads // each
     own = slice(EDGE, EDGE + half)
     two = 2 * EDGE
     at_prev = PREV_ROADS * width
@@ -508,77 +497,67 @@
             + jnp.concatenate([jnp.zeros((1, LANES), F32), over[:-1]], axis=0)
         )
 
-    def column_product(tile_at, column):
-        acc = None
-        for s in range(width // 8):
-            term = tile_at(s) * column[s * 8 : (s + 1) * 8]
-            acc = term if acc is None else acc + term
-        return acc
-
-    def apply(vector):
-        even = gathered(vector, even_off[...], False)
-        odd = gathered(vector, odd_off[...], True)
-        even_part[...] = jnp.zeros_like(even_part)
-        odd_part[...] = jnp.zeros_like(odd_part)
-        edge_even = jnp.concatenate(
-            [even[:EDGE], even[EDGE + half :], jnp.zeros((LANES - 2 * EDGE, LANES), F32)], axis=0
-        ).T
-        edge_odd = jnp.concatenate(
-            [odd[:EDGE], odd[EDGE + half :], jnp.zeros((LANES - 2 * EDGE, LANES), F32)], axis=0
-        ).T
-        for num in range(PREV_ROADS):
-            row = EDGE - PREV_ROADS // 2 + num // 2
-            column = (edge_even if num % 2 == 0 else edge_odd)[:, row : row + 1]
-            part = even_part if num % 2 == 0 else odd_part
-            part[row] = column_product(
-                lambda s, num=num: from_prev_ref[num * width + s * 8 : num * width + s * 8 + 8],
-                column,
-            )
-        for num in range(NEXT_ROADS):
-            column = (edge_even if num % 2 == 0 else edge_odd)[:, EDGE : EDGE + 1]
-            part = even_part if num % 2 == 0 else odd_part
-            part[EDGE + half] = column_product(
-                lambda s, num=num: from_next_ref[num * width + s * 8 : num * width + s * 8 + 8],
-                column,
-            )
-        turned_even[:, :half] = even[own].T
-        turned_odd[:, :half] = odd[own].T
-        per = each // 2
-
-        copies_of = iota((3 * per, per * width), 0) % per == iota((3 * per, per * width), 1) // width
-        copies_of = jnp.where(copies_of, 1.0, 0.0).astype(BF16)
+    def row_products(rows, tiles_at):
+        lane_block = iota((8, 8 * width), 1) // width
+        diagonal = lane_block == iota((8, 8 * width), 0)
+        left = jnp.concatenate(
+            [jnp.where(diagonal, jnp.concatenate([part.astype(F32)] * 8, axis=1), 0.0)
+             for part in split_two(rows)],
+            axis=0,
+        ).astype(BF16)
+        right = jnp.concatenate([tiles_at(k) for k in range(8)], axis=0)
+        both = dot(left, right, 1, 0)
+        both = both[:, :width] + both[:, width:]
+        return both[:8] + both[8:]
+
+    def halves(block):
+        return jnp.concatenate(split_two(block), axis=1)
+
+    edge_blocks = [(from_prev_ref, num) for num in range(PREV_ROADS)]
+    edge_blocks += [(from_next_ref, num) for num in range(NEXT_ROADS)]
+    edge_blocks += edge_blocks[:2]
+    edge_rows = [(EDGE - PREV_ROADS // 2 + num // 2, num % 2) for num in range(PREV_ROADS)]
+    edge_rows += [(EDGE + half, num) for num in range(NEXT_ROADS)]
+
+    def apply(vector, again):
+        even_part[...] = gathered(vector, even_off[...], False)
+        odd_part[...] = gathered(vector, odd_off[...], True)
+        outer = [(odd_part if odd else even_part)[row : row + 1, :] for row, odd in edge_rows]
+        outer = jnp.concatenate(outer + [jnp.zeros((2, LANES), F32)], axis=0)
+
+        def edge_tile(k):
+            if again:
+                return edge_halves[k]
+            ref, num = edge_blocks[k]
+            edge_halves[k] = halves(ref[num * width : (num + 1) * width, :])
+            return edge_halves[k]
+
+        outer = row_products(outer, edge_tile)
+        for part, parity in ((even_part, 0), (odd_part, 1)):
+            part[EDGE + half :, :] = jnp.zeros((EDGE, LANES), F32)
+            part[:EDGE, :] = jnp.zeros((EDGE, LANES), F32)
+        for num, (row, odd) in enumerate(edge_rows):
+            (odd_part if odd else even_part)[row : row + 1, :] = outer[num : num + 1]
 
         def chunk(c, carry):
-            columns_even = turned_even[...]
-            columns_odd = turned_odd[...]
-            spread_odd = dot(
-                jnp.concatenate(split_three(columns_odd[:, :per]), axis=1), copies_of, 1, 0
-            )
-            for j in range(per):
-                road = c * each + 2 * j
-                even_part[EDGE + c * per + j] = column_product(
-                    lambda s, road=road: held[road, s * 8 : s * 8 + 8, :],
-                    columns_even[:, j : j + 1],
-                )
-                odd_part[EDGE + c * per + j] = column_product(
-                    lambda s, road=road: held[road + 1, s * 8 : s * 8 + 8, :],
-                    spread_odd[:, j * width : (j + 1) * width],
-                )
-            turned_even[...] = pltpu.roll(columns_even, columns_even.shape[1] - per, 1)
-            turned_odd[...] = pltpu.roll(columns_odd, columns_odd.shape[1] - per, 1)
+            for part, parity in ((even_part, 0), (odd_part, 1)):
+                where = pl.ds(pl.multiple_of(EDGE + c * 8, 8), 8)
+
+                def tile(k, parity=parity):
+                    road = c * 16 + 2 * k + parity
+                    if not again:
+                        held_halves[road] = halves(held[road])
+                    return held_halves[road]
+
+                part[where, :] = row_products(part[where, :], tile)
             return carry
 
-        lax.fori_loop(0, chunks, chunk, 0)
-        even = even_part[:, 0, :]
-        odd = odd_part[:, 0, :]
-        for k in range(1, 8):
-            even = even + even_part[:, k, :]
-            odd = odd + odd_part[:, k, :]
-        return prior[...] * vector + spread(even, odd)
+        lax.fori_loop(0, half // 8, chunk, 0, unroll=min(8, half // 8))
+        return prior[...] * vector + spread(even_part[...], odd_part[...])
 
     first = spread(even_sum[...], odd_sum[...])
-    second = apply(first)
-    third = apply(second)
+    second = apply(first, False)
+    third = apply(second, True)
     first, second, third = first[own], second[own], third[own]
     first_ref[...] = first
     second_ref[...] = second
@@ -647,7 +626,7 @@
     smem = pl.BlockSpec(memory_space=pltpu.SMEM)
     limit = pltpu.CompilerParams(vmem_limit_bytes=32 * 1024 * 1024)
     large = pltpu.CompilerParams(vmem_limit_bytes=LARGE * 1024 * 1024)
-    small = pltpu.CompilerParams(vmem_limit_bytes=12 * 1024 * 1024)
+    small = pltpu.CompilerParams(vmem_limit_bytes=20 * 1024 * 1024)
 
     sent = (
         local_deriv, jnp.transpose(global_deriv, (1, 0, 2)), measured, hit_weight, hit_module,
@@ -661,7 +640,7 @@
         out_specs=vmem,
         scratch_shapes=[
             pltpu.VMEM((ROWS, tracks), F32),
-            pltpu.VMEM((3 * ROWS, tracks), BF16),
+            pltpu.VMEM((2 * ROWS, tracks), BF16),
             pltpu.VMEM((NHIT, 8, tracks), F32),
             pltpu.VMEM((NHIT, 8, tracks), F32),
             pltpu.VMEM((slots, tracks), BF16),
@@ -741,14 +720,16 @@
     total = half + 2 * EDGE
     rows = pltpu.VMEM((total, LANES), F32)
     int_rows = pltpu.VMEM((total, LANES), jnp.int32)
-    parts = pltpu.VMEM((total, 8, LANES), F32)
-    turned = pltpu.VMEM((LANES, LANES), F32)
+    halves = pltpu.VMEM((roads, width, 2 * width), BF16)
+    edge_halves = pltpu.VMEM((8, width, 2 * width), BF16)
     first, second, dots = pl.pallas_call(
         krylov_kernel,
         out_shape=(shape(half, width), shape(half, width), shape(devices, 1, LANES)),
         in_specs=[vmem] * 6,
         out_specs=(vmem,) * 3,
-        scratch_shapes=[rows, rows, int_rows, int_rows, rows, parts, parts, turned, turned],
+        scratch_shapes=[
+            rows, rows, int_rows, int_rows, rows, rows, rows, halves, edge_halves,
+        ],
         compiler_params=small,
         name="two_products",
     )(held_blocks, sums, off_rows, prior, from_prev, from_next)

time: 94.7 us -> 91 us (0.961)
  Pallas kernels: 36.8 us -> 34.5 us
  starting transfers between devices: 16.6 us -> 15.2 us
    pallas_call x1, Pallas kernels: 10.5 us -> 8.49 us  [on_device(): pl.pallas_call(krylov_kernel, out_shape=(shape(half, width), shape(half,...]
    all_to_all x1, starting transfers between devices: 3.9 us -> 2.54 us  [on_device(): lax.all_to_all(dots, AXES, split_axis=0, concat_axis=0, tiled=True)]
  transfers between devices with their start and end apart: 4 -> 4, of which waited for: 2 -> 2; matrix products, arithmetic and copies ran while one was open for 4% -> 5% of each run, Pallas kernels for 11% -> 11%
where the time goes in v4:
time: 91 us; the launch traced here: 90.7 us
  waiting for transfers between devices  35.7 us (39%)
  Pallas kernels  34.5 us (38%)
  starting transfers between devices  15.2 us (17%)
  local copies, waits for them, and re-layouts  3.64 us (4%)
  between operations  0.91 us (1%)
    all_to_all x1, waiting for transfers between devices, on_device(): recv = lax.all_to_all(send, AXES, split_axis=0, concat_axis=0, tiled=True)  30.4 us
    pallas_call x1, Pallas kernels, on_device(): pl.pallas_call(inner_kernel, out_shape=(shape(roads, width, width), shape...  10.4 us
    pallas_call x1, Pallas kernels, on_device(): pl.pallas_call(krylov_kernel, out_shape=(shape(half, width), shape(half,...  8.49 us
    pallas_call x1, Pallas kernels, on_device(): pl.pallas_call(functools.partial(edge_kernel, cap), out_shape=(shape(slot...  7.78 us
    all_to_all x1, starting transfers between devices, on_device(): recv = lax.all_to_all(send, AXES, split_axis=0, concat_axis=0, tiled=True)  7.31 us
    ppermute x2, starting transfers between devices, neighbour(): lax.ppermute(value, AXES, [(s, (s + steps) % count) for s in range(count)])  5.39 us
    all_to_all x1, waiting for transfers between devices, on_device(): lax.all_to_all(dots, AXES, split_axis=0, concat_axis=0, tiled=True)  5.31 us
    pallas_call x1, Pallas kernels, on_device(): pl.pallas_call(functools.partial(pack_kernel, cap, roads, modules * devic...  4.32 us
  transfers between devices with their start and end apart: 4, of which 2 were waited for; matrix products, arithmetic and copies ran while one was open for 5% of the time, Pallas kernels for 11%

profile of v4, /device:TPU:0, one launch (start us, length us, event | category | flops | bytes accessed | tf_op | source)
XLA Modules:
  0.0 90.7 jit_solution(5283996454927044571)
XLA Ops:
  0.6 4.3 %fit_and_pack.1 = f32[2624,128]{1,0:T(8,128)} custom-call(f32[5,12,512]{2,1,0:T(8,128)} %ld_hbm.1, f32[12,8,512]{2,1,0:T(8,128)} %bitcast.25, f32[12,512]{1,0:T(8,128)} %me_hbm.1, f32[12,512]{1,0:T(8,128)} %hw_hbm.1, s32[12,512]{1,0:T(8,128)} %hm_hbm.1, s32[1,512]{1,0:T(1,128)} %bitcast.28, s32[1,512]{1,0:T(1,128)} %bitcast.29), custom_call_target="tpu_custom_call" | custom-call | tf_op jit(solution)/shard_map/fit_and_pack/pallas_call | solution.py:636
  5.0 7.3 %all-to-all-start = ((f32[32,82,1,128]{3,2,1,0:T(1,128)}), f32[32,82,1,128]{3,2,1,0:T(1,128)S(1)}, u32[]{:S(2)}, u32[]{:S(2)}) async-start(f32[32,82,1,128]{3,2,1,0:T(1,128)} %bitcast.24), calls=%async_computation | async-start | bytes 2686976 | tf_op jit(solution)/shard_map/all_to_all | solution.py:657
  12.3 0.7 fusion
  13.0 0.1 copy.23.off_ref
  13.1 1.2 %copy.24 = f32[2048,8]{1,0:T(8,128)S(1)} copy(f32[2048,8]{0,1:T(8,128)} %param.17) | data formatting | bytes 131072 | tf_op args[8]
  14.3 0.5 reshape.39.prior_ref
  14.8 30.4 %all-to-all-done = f32[32,82,1,128]{3,2,1,0:T(1,128)S(1)} async-done(((f32[32,82,1,128]{3,2,1,0:T(1,128)}), f32[32,82,1,128]{3,2,1,0:T(1,128)S(1)}, u32[]{:S(2)}, u32[]{:S(2)}) %all-to-all-start) | async-done | bytes 1343520 | tf_op jit(solution)/shard_map/all_to_all | solution.py:657
  45.2 2.0 %sort_by_road.1 = (s32[40,128]{1,0:T(8,128)S(1)}, s32[8,128]{1,0:T(8,128)S(1)}, s32[8,128]{1,0:T(8,128)S(1)}, f32[16,128]{1,0:T(8,128)S(1)}) custom-call(f32[2624,128]{1,0:T(8,128)S(1)} %bitcast.13, f32[256,1]{1,0:T(8,128)S(1)} %copy.23.off_ref), custom_call_target="tpu_custom_call" | custom-call | tf_op jit(solution)/shard_map/sort_by_road/pallas_call | solution.py:666
  47.2 0.1 broadcast_in_dim.18.off_rows_ref.off_ref
  47.3 7.8 %lay_and_assemble_edges.1 = (f32[2056,8,128]{2,1,0:T(8,128)S(1)}, f32[256,128,128]{2,1,0:T(8,128)S(1)}, f32[256,128]{1,0:T(8,128)S(1)}, f32[552,128]{1,0:T(8,128)S(1)}, f32[296,128]{1,0:T(8,128)S(1)}) custom-call(s32[1024]{0:T(1024)S(1)} %bitcast.22, s32[5120]{0:T(1024)S(1)} %bitcast.17, s32[1024]{0:T(1024)S(1)} %bitcast.20, f32[2624,128]{1,0:T(8,128)S(1)} %bitcast.14, ...), custom_call_target="tpu_custom_call" | custom-call | tf_op jit(solution)/shard_map/lay_and_assemble_edges/pallas_call | solution.py:686
  55.1 0.1 collective-permute-start
  55.1 5.3 %collective-permute-start.1 = (f32[296,128]{1,0:T(8,128)S(1)}, f32[296,128]{1,0:T(8,128)S(1)}, u32[]{:S(2)}, u32[]{:S(2)}) collective-permute-start(f32[296,128]{1,0:T(8,128)S(1)} %get-tuple-element.29), channel_id=1, source_target_pairs={{0,31},{1,0},{2,1},{3,2},{4,3},{5,4},{6,5},{7,6},{8,7},{9,8},{10,9... | collective-permute-start | bytes 454664 | tf_op jit(solution)/shard_map/ppermute | solution.py:606
  60.5 10.4 %assemble_blocks.1 = (f32[256,128,128]{2,1,0:T(8,128)}, f32[256,128,128]{2,1,0:T(8,128)S(1)}, f32[256,128]{1,0:T(8,128)S(1)}) custom-call(s32[1024]{0:T(1024)S(1)} %bitcast.23, s32[5120]{0:T(1024)S(1)} %bitcast.18, s32[1024]{0:T(1024)S(1)} %bitcast.21, ...), custom_call_target="tpu_custom_call", output_to_operand_aliasing={{1}: (4, {}), {2}: (5, {})} | custom-call | tf_op jit(solution)/shard_map/assemble_blocks/pallas_call | solution.py:704
  70.9 0.0 collective-permute-done.1.from_next_ref
  70.9 0.0 collective-permute-done.from_prev_ref
  70.9 8.5 %two_products.1 = (f32[128,128]{1,0:T(8,128)S(1)}, f32[128,128]{1,0:T(8,128)S(1)}, f32[32,1,128]{2,1,0:T(1,128)}) custom-call(f32[256,128,128]{2,1,0:T(8,128)S(1)} %get-tuple-element.26.held, f32[256,128]{1,0:T(8,128)S(1)} %get-tuple-element.27.sums_ref, f32[256,128]{1,0:T(8,128)S(1)} %broadcast_in_dim.18.off_rows_ref.off_ref, ...), custom_call_target="tpu_custom_call" | custom-call | tf_op jit(solution)/shard_map/two_products/pallas_call | solution.py:725
  79.4 2.5 %all-to-all-start.1 = ((f32[32,1,128]{2,1,0:T(1,128)}), f32[32,1,128]{2,1,0:T(1,128)S(1)}, u32[]{:S(2)}, u32[]{:S(2)}) async-start(f32[32,1,128]{2,1,0:T(1,128)} %get-tuple-element.31), calls=%async_computation.1 | async-start | bytes 32768 | tf_op jit(solution)/shard_map/all_to_all | solution.py:736
  81.9 0.6 reshape.40
  82.5 0.3 copy.27
  82.8 0.0 copy-start
  82.8 0.6 reshape.42
  83.4 0.3 copy.26
  83.7 5.3 %all-to-all-done.1 = f32[32,1,128]{2,1,0:T(1,128)S(1)} async-done(((f32[32,1,128]{2,1,0:T(1,128)}), f32[32,1,128]{2,1,0:T(1,128)S(1)}, u32[]{:S(2)}, u32[]{:S(2)}) %all-to-all-start.1) | async-done | bytes 16416 | tf_op jit(solution)/shard_map/all_to_all | solution.py:736
  89.0 1.5 %combine.1 = f32[8,2048]{1,0:T(8,128)} custom-call(f32[32,128]{1,0:T(8,128)S(1)} %bitcast.19, f32[8,2048]{1,0:T(8,128)S(1)} %bitcast.15, f32[8,2048]{1,0:T(8,128)S(1)} %bitcast.16), custom_call_target="tpu_custom_call" | custom-call | tf_op jit(solution)/shard_map/combine/pallas_call | solution.py:739
  90.5 0.0 copy-done
Async XLA Ops:
  5.0 40.2 %all-to-all-start = ((f32[32,82,1,128]{3,2,1,0:T(1,128)}), f32[32,82,1,128]{3,2,1,0:T(1,128)S(1)}, u32[]{:S(2)}, u32[]{:S(2)}) async-start(f32[32,82,1,128]{3,2,1,0:T(1,128)} %bitcast.24), calls=%async_computation | async-start | bytes 2686976 | tf_op jit(solution)/shard_map/all_to_all | solution.py:657
  55.1 15.8 %collective-permute-start = (f32[552,128]{1,0:T(8,128)S(1)}, f32[552,128]{1,0:T(8,128)S(1)}, u32[]{:S(2)}, u32[]{:S(2)}) collective-permute-start(f32[552,128]{1,0:T(8,128)S(1)} %get-tuple-element.28), channel_id=1, source_target_pairs={{0,1},{1,2},{2,3},{3,4},{4,5},{5,6},{6,7},{7,8},{8,9},{9,10},{10,1... | collective-permute-start | bytes 847880 | tf_op jit(solution)/shard_map/ppermute | solution.py:606
  55.1 15.7 %collective-permute-start.1 = (f32[296,128]{1,0:T(8,128)S(1)}, f32[296,128]{1,0:T(8,128)S(1)}, u32[]{:S(2)}, u32[]{:S(2)}) collective-permute-start(f32[296,128]{1,0:T(8,128)S(1)} %get-tuple-element.29), channel_id=1, source_target_pairs={{0,31},{1,0},{2,1},{3,2},{4,3},{5,4},{6,5},{7,6},{8,7},{9,8},{10,9... | collective-permute-start | bytes 454664 | tf_op jit(solution)/shard_map/ppermute | solution.py:606
  79.4 9.6 %all-to-all-start.1 = ((f32[32,1,128]{2,1,0:T(1,128)}), f32[32,1,128]{2,1,0:T(1,128)S(1)}, u32[]{:S(2)}, u32[]{:S(2)}) async-start(f32[32,1,128]{2,1,0:T(1,128)} %get-tuple-element.31), calls=%async_computation.1 | async-start | bytes 32768 | tf_op jit(solution)/shard_map/all_to_all | solution.py:736
  82.8 7.7 %copy-start = (f32[2048,8]{0,1:T(8,128)}, f32[2048,8]{0,1:T(8,128)S(1)}, u32[]{:S(2)}) copy-start(f32[2048,8]{0,1:T(8,128)S(1)} %copy.27) | copy-start | bytes 196612

commit v5 on v4

--- a/solution.py
+++ b/solution.py
@@ -112,14 +112,13 @@
     order = jnp.zeros((NHIT, tracks), F32)
     for i in range(NHIT):
         order = order + jnp.where(ahead[i : i + 1] < ahead, 1.0, 0.0)
-    for a in range(NLOC):
-        mixed_ref[:, a, :] = ld_ref[a] * root
-    mixed_ref[:, NLOC, :] = me_ref[...] * root
-    mixed_ref[:, NLOC + 1, :] = ahead
-    mixed_ref[:, NLOC + 2, :] = order
+    rows = [ld_ref[a] * root for a in range(NLOC)] + [me_ref[...] * root, ahead, order]
     for at in range(0, tracks, LANES):
         lanes = slice(at, at + LANES)
-        tiles = [mixed_ref[i, :, lanes] for i in range(NHIT)]
+        mixed, ordered = mixed_ref.at[at // LANES], sorted_ref.at[at // LANES]
+        for num, row in enumerate(rows):
+            mixed[pl.ds(num, NHIT, stride=8), :] = row[:, lanes]
+        tiles = [mixed[i * 8 : i * 8 + 8, :] for i in range(NHIT)]
         places = [jnp.broadcast_to(tile[NLOC + 2 : NLOC + 3], (8, LANES)) for tile in tiles]
         derivs = [gd_ref[i, :, lanes] * root[i : i + 1, lanes] for i in range(NHIT)]
         for k in range(NHIT):
@@ -128,10 +127,17 @@
                 here = places[i] == float(k)
                 tile = jnp.where(here, tiles[i], tile)
                 deriv = jnp.where(here, derivs[i], deriv)
-            sorted_ref[k, :, lanes] = tile
+            ordered[k * 8 : k * 8 + 8, :] = tile
             row = derivative_row(k)
             words_ref[row : row + NPAR, lanes] = deriv
-    scaled = [sorted_ref[:, a, :] for a in range(NLOC)]
+
+    def in_order(num):
+        parts = [
+            sorted_ref[at, pl.ds(num, NHIT, stride=8), :] for at in range(tracks // LANES)
+        ]
+        return jnp.concatenate(parts, axis=1)
+
+    scaled = [in_order(a) for a in range(NLOC)]
     factor = {}
     for a in range(NLOC):
         for b in range(a + 1):
@@ -147,13 +153,13 @@
         for b in range(a):
             running = running - factor[a, b] * proj[b]
         proj.append(running / factor[a, a])
-    residual = sorted_ref[:, NLOC, :]
+    residual = in_order(NLOC)
     solved = residual
     for a in range(NLOC):
         solved = solved - proj[a] * jnp.sum(proj[a] * residual, axis=0, keepdims=True)
     for a in range(NLOC - 1):
         proj = householder(proj, a, a)
-    ahead = sorted_ref[:, NLOC + 1, :]
+    ahead = in_order(NLOC + 1)
     skipped = ahead - ahead[0:1] - iota((NHIT, tracks), 0).astype(F32)
     words_ref[R_ROAD:R_FIRST, :] = (tr_ref[...] % road_dev + 1).astype(F32)
     words_ref[R_FIRST:USED, :] = ahead[0:1]
@@ -237,7 +243,7 @@
         total = total + dot(pick, values.astype(BF16), 1, 1)
     found = total[:, :LANES]
     track = jnp.where(found > 0.5, (found - 1.0) * LANES + total[:, LANES:], float(blocks * LANES))
-    list_ref[...] = track.astype(jnp.int32)
+    list_ref[...] = (8.0 * track).astype(jnp.int32)
     item_rows = item_ref.shape[0]
     for row in range(item_rows):
         item = (iota((1, LANES), 1) + row * LANES).astype(F32)
@@ -257,7 +263,7 @@
     width = ROAD * NPAR
     lower_half = iota((USED, LANES), 1) < LANES // 2
     slot_num = iota((ROAD, LANES), 0)
-    tiles_ref[blocks * LANES] = jnp.zeros((8, width), F32)
+    tiles_ref[blocks * LANES * 8 : (blocks * LANES + 1) * 8] = jnp.zeros((8, width), F32)
     shift_ref[:, :8, :] = jnp.full((2, 8, LANES), -1.0, F32)
 
     def lay(num, held):
@@ -294,12 +300,14 @@
                     row = R_PROJ[a] - a - move
                     valid = jnp.logical_and(match, slot_num >= a + move) if a else match
                 placed[a] = jnp.where(valid, words[row : row + ROAD, :], placed[a])
-        start = pl.multiple_of(e * LANES, LANES)
+        start = pl.multiple_of(e * LANES * 8, LANES * 8)
         for a in range(NLOC + 1):
             mixed = jnp.concatenate([laid[s] * placed[a][s : s + 1] for s in range(ROAD)], axis=0)
-            tiles_ref[pl.ds(start, LANES), a if a < NLOC else SUM_ROW, :] = mixed.T
-        tiles_ref[pl.ds(start, LANES), NLOC, :] = jnp.concatenate(laid, axis=0).T
-        tiles_ref[pl.ds(start, LANES), SUM_ROW + 1, :] = jnp.zeros((LANES, width), F32)
+            row = a if a < NLOC else SUM_ROW
+            tiles_ref[pl.ds(start + row, LANES, stride=8), :] = mixed.T
+        tiles_ref[pl.ds(start + NLOC, LANES, stride=8), :] = jnp.concatenate(laid, axis=0).T
+        empty = jnp.zeros((LANES, width), F32)
+        tiles_ref[pl.ds(start + SUM_ROW + 1, LANES, stride=8), :] = empty
 
     def lay_two(num, carry):
         lay(num, 0)
@@ -326,7 +334,9 @@
             first = (info & 1) == 1
             road = jnp.where(live, info >> 1, 0)
             at = item * PER_ITEM
-            parts = [tiles_ref[list_ref[at + j]] for j in range(PER_ITEM)]
+            parts = [
+                tiles_ref[pl.ds(pl.multiple_of(list_ref[at + j], 8), 8), :] for j in range(PER_ITEM)
+            ]
             tall = jnp.concatenate(parts, axis=0)
             high, low = split_two(tall)
             left = jnp.concatenate([high, high, low], axis=0)
@@ -344,7 +354,8 @@
             added = parts[0]
             for part in parts[1:]:
                 added = added + part
-            held_ref[road] = added + jnp.where(first, 0.0, held_ref[road])
+            where = pl.ds(pl.multiple_of(road * 8, 8), 8)
+            held_ref[where, :] = added + jnp.where(first, 0.0, held_ref[where, :])
 
     return step
 
@@ -366,8 +377,8 @@
         return carry
 
     lax.fori_loop(0, (count + UNROLL - 1) // UNROLL, body, 0)
-    sums_ref[:edge] = held_ref[:edge, SUM_ROW, :]
-    sums_ref[roads - edge :] = held_ref[roads - edge :, SUM_ROW, :]
+    for start in (0, roads - edge):
+        sums_ref[start : start + edge] = held_ref[pl.ds(start * 8 + SUM_ROW, edge, stride=8), :]
     two = 2 * EDGE
     for ref, first_block, count, first_road, first_row in (
         (to_next_ref, roads - PREV_ROADS, PREV_ROADS, roads - two, prior_ref.shape[0] - EDGE),
@@ -415,7 +426,9 @@
         copies[-1].start()
     for copy in outer:
         copy.start()
-    sums_ref[edge : roads - edge] = held_ref[edge : roads - edge, SUM_ROW, :]
+    sums_ref[edge : roads - edge] = held_ref[
+        pl.ds(edge * 8 + SUM_ROW, roads - 2 * edge, stride=8), :
+    ]
     for copy in outer + copies:
         copy.wait()
     del edge_ref, edge_sums_ref
@@ -641,8 +654,8 @@
         scratch_shapes=[
             pltpu.VMEM((ROWS, tracks), F32),
             pltpu.VMEM((2 * ROWS, tracks), BF16),
-            pltpu.VMEM((NHIT, 8, tracks), F32),
-            pltpu.VMEM((NHIT, 8, tracks), F32),
+            pltpu.VMEM((tracks // LANES, NHIT * 8, LANES), F32),
+            pltpu.VMEM((tracks // LANES, NHIT * 8, LANES), F32),
             pltpu.VMEM((slots, tracks), BF16),
             *(pltpu.VMEM(x.shape, x.dtype) for x in sent),
             pltpu.SemaphoreType.DMA((len(sent),)),
@@ -686,7 +699,7 @@
     tiles, edge_blocks, edge_sums, to_next, to_prev = pl.pallas_call(
         functools.partial(edge_kernel, cap),
         out_shape=(
-            shape(slots + 8, 8, width), shape(roads, width, width), shape(roads, width),
+            shape((slots + 8) * 8, width), shape(roads, width, width), shape(roads, width),
             shape(PREV_ROADS * width + halo, width), shape(NEXT_ROADS * width + halo, width),
         ),
         in_specs=[smem] * 3 + [vmem] * 4,
@@ -694,7 +707,7 @@
         scratch_shapes=[
             pltpu.VMEM((2, ROWS, LANES), F32),
             pltpu.VMEM((2, 8 + ROAD, LANES), F32),
-            pltpu.VMEM((roads, 8, width), F32),
+            pltpu.VMEM((roads * 8, width), F32),
         ],
         compiler_params=small,
         name="lay_and_assemble_edges",
@@ -709,7 +722,7 @@
         in_specs=[smem] * 3 + [vmem] * 3,
         out_specs=(pl.BlockSpec(memory_space=pltpu.HBM), vmem, vmem),
         scratch_shapes=[
-            pltpu.VMEM((roads, 8, width), F32),
+            pltpu.VMEM((roads * 8, width), F32),
             pltpu.SemaphoreType.DMA((2 + (GROUPS - 2) // 2,)),
         ],
         input_output_aliases={4: 1, 5: 2},

time: 91 us -> 88.6 us (0.974)
  Pallas kernels: 34.5 us -> 32.2 us
    pallas_call x1, Pallas kernels: 7.78 us -> 5.74 us  [on_device(): pl.pallas_call(functools.partial(edge_kernel, cap), out_shape=(shape((slo...]
  transfers between devices with their start and end apart: 4 -> 4, of which waited for: 2 -> 2; matrix products, arithmetic and copies ran while one was open for 5% -> 5% of each run, Pallas kernels for 11% -> 12%
where the time goes in v5:
time: 88.6 us; the launch traced here: 88.3 us
  waiting for transfers between devices  35.7 us (40%)
  Pallas kernels  32.2 us (36%)
  starting transfers between devices  15.2 us (17%)
  local copies, waits for them, and re-layouts  3.64 us (4%)
  between operations  0.91 us (1%)
    all_to_all x1, waiting for transfers between devices, on_device(): recv = lax.all_to_all(send, AXES, split_axis=0, concat_axis=0, tiled=True)  30.4 us
    pallas_call x1, Pallas kernels, on_device(): pl.pallas_call(inner_kernel, out_shape=(shape(roads, width, width), shape...  10.3 us
    pallas_call x1, Pallas kernels, on_device(): pl.pallas_call(krylov_kernel, out_shape=(shape(half, width), shape(half,...  8.49 us
    all_to_all x1, starting transfers between devices, on_device(): recv = lax.all_to_all(send, AXES, split_axis=0, concat_axis=0, tiled=True)  7.3 us
    pallas_call x1, Pallas kernels, on_device(): pl.pallas_call(functools.partial(edge_kernel, cap), out_shape=(shape((slo...  5.74 us
    ppermute x2, starting transfers between devices, neighbour(): lax.ppermute(value, AXES, [(s, (s + steps) % count) for s in range(count)])  5.39 us
    all_to_all x1, waiting for transfers between devices, on_device(): lax.all_to_all(dots, AXES, split_axis=0, concat_axis=0, tiled=True)  5.31 us
    pallas_call x1, Pallas kernels, on_device(): pl.pallas_call(functools.partial(pack_kernel, cap, roads, modules * devic...  4.08 us
  transfers between devices with their start and end apart: 4, of which 2 were waited for; matrix products, arithmetic and copies ran while one was open for 5% of the time, Pallas kernels for 12%

profile of v5, /device:TPU:0, one launch (start us, length us, event | category | flops | bytes accessed | tf_op | source)
XLA Modules:
  0.0 88.3 jit_solution(7668269626315889425)
XLA Ops:
  0.6 4.1 %fit_and_pack.1 = f32[2624,128]{1,0:T(8,128)} custom-call(f32[5,12,512]{2,1,0:T(8,128)} %ld_hbm.1, f32[12,8,512]{2,1,0:T(8,128)} %bitcast.25, f32[12,512]{1,0:T(8,128)} %me_hbm.1, f32[12,512]{1,0:T(8,128)} %hw_hbm.1, s32[12,512]{1,0:T(8,128)} %hm_hbm.1, s32[1,512]{1,0:T(1,128)} %bitcast.28, s32[1,512]{1,0:T(1,128)} %bitcast.29), custom_call_target="tpu_custom_call" | custom-call | tf_op jit(solution)/shard_map/fit_and_pack/pallas_call | solution.py:649
  4.7 7.3 %all-to-all-start = ((f32[32,82,1,128]{3,2,1,0:T(1,128)}), f32[32,82,1,128]{3,2,1,0:T(1,128)S(1)}, u32[]{:S(2)}, u32[]{:S(2)}) async-start(f32[32,82,1,128]{3,2,1,0:T(1,128)} %bitcast.24), calls=%async_computation | async-start | bytes 2686976 | tf_op jit(solution)/shard_map/all_to_all | solution.py:670
  12.0 0.7 fusion
  12.7 0.1 copy.23.off_ref
  12.9 1.2 %copy.24 = f32[2048,8]{1,0:T(8,128)S(1)} copy(f32[2048,8]{0,1:T(8,128)} %param.17) | data formatting | bytes 131072 | tf_op args[8]
  14.0 0.5 reshape.39.prior_ref
  14.5 30.4 %all-to-all-done = f32[32,82,1,128]{3,2,1,0:T(1,128)S(1)} async-done(((f32[32,82,1,128]{3,2,1,0:T(1,128)}), f32[32,82,1,128]{3,2,1,0:T(1,128)S(1)}, u32[]{:S(2)}, u32[]{:S(2)}) %all-to-all-start) | async-done | bytes 1343520 | tf_op jit(solution)/shard_map/all_to_all | solution.py:670
  44.9 2.0 %sort_by_road.1 = (s32[40,128]{1,0:T(8,128)S(1)}, s32[8,128]{1,0:T(8,128)S(1)}, s32[8,128]{1,0:T(8,128)S(1)}, f32[16,128]{1,0:T(8,128)S(1)}) custom-call(f32[2624,128]{1,0:T(8,128)S(1)} %bitcast.13, f32[256,1]{1,0:T(8,128)S(1)} %copy.23.off_ref), custom_call_target="tpu_custom_call" | custom-call | tf_op jit(solution)/shard_map/sort_by_road/pallas_call | solution.py:679
  46.9 0.1 broadcast_in_dim.18.off_rows_ref.off_ref
  47.0 5.7 %lay_and_assemble_edges.1 = (f32[16448,128]{1,0:T(8,128)S(1)}, f32[256,128,128]{2,1,0:T(8,128)S(1)}, f32[256,128]{1,0:T(8,128)S(1)}, f32[552,128]{1,0:T(8,128)S(1)}, f32[296,128]{1,0:T(8,128)S(1)}) custom-call(s32[1024]{0:T(1024)S(1)} %bitcast.22, s32[5120]{0:T(1024)S(1)} %bitcast.17, s32[1024]{0:T(1024)S(1)} %bitcast.20, f32[2624,128]{1,0:T(8,128)S(1)} %bitcast.14, ...), custom_call_target="tpu_custom_call" | custom-call | tf_op jit(solution)/shard_map/lay_and_assemble_edges/pallas_call | solution.py:699
  52.8 0.1 collective-permute-start
  52.8 5.3 %collective-permute-start.1 = (f32[296,128]{1,0:T(8,128)S(1)}, f32[296,128]{1,0:T(8,128)S(1)}, u32[]{:S(2)}, u32[]{:S(2)}) collective-permute-start(f32[296,128]{1,0:T(8,128)S(1)} %get-tuple-element.29), channel_id=1, source_target_pairs={{0,31},{1,0},{2,1},{3,2},{4,3},{5,4},{6,5},{7,6},{8,7},{9,8},{10,9... | collective-permute-start | bytes 454664 | tf_op jit(solution)/shard_map/ppermute | solution.py:619
  58.2 10.3 %assemble_blocks.1 = (f32[256,128,128]{2,1,0:T(8,128)}, f32[256,128,128]{2,1,0:T(8,128)S(1)}, f32[256,128]{1,0:T(8,128)S(1)}) custom-call(s32[1024]{0:T(1024)S(1)} %bitcast.23, s32[5120]{0:T(1024)S(1)} %bitcast.18, s32[1024]{0:T(1024)S(1)} %bitcast.21, f32[16448,128]{1,0:T(8,128)S(1)} %get-tuple-element.22.tiles_ref, ...), custom_call_target="tpu_custom_call", output_to_operand_aliasing={{1}: (4, {}), {2}: (5, {})} | custom-call | tf_op jit(solution)/shard_map/assemble_blocks/pallas_call | solution.py:717
  68.5 0.0 collective-permute-done.1.from_next_ref
  68.5 0.0 collective-permute-done.from_prev_ref
  68.5 8.5 %two_products.1 = (f32[128,128]{1,0:T(8,128)S(1)}, f32[128,128]{1,0:T(8,128)S(1)}, f32[32,1,128]{2,1,0:T(1,128)}) custom-call(f32[256,128,128]{2,1,0:T(8,128)S(1)} %get-tuple-element.26.held, f32[256,128]{1,0:T(8,128)S(1)} %get-tuple-element.27.sums_ref, f32[256,128]{1,0:T(8,128)S(1)} %broadcast_in_dim.18.off_rows_ref.off_ref, ...), custom_call_target="tpu_custom_call" | custom-call | tf_op jit(solution)/shard_map/two_products/pallas_call | solution.py:738
  77.0 2.5 %all-to-all-start.1 = ((f32[32,1,128]{2,1,0:T(1,128)}), f32[32,1,128]{2,1,0:T(1,128)S(1)}, u32[]{:S(2)}, u32[]{:S(2)}) async-start(f32[32,1,128]{2,1,0:T(1,128)} %get-tuple-element.31), calls=%async_computation.1 | async-start | bytes 32768 | tf_op jit(solution)/shard_map/all_to_all | solution.py:749
  79.6 0.6 reshape.40
  80.2 0.3 copy.27
  80.5 0.0 copy-start
  80.5 0.6 reshape.42
  81.0 0.3 copy.26
  81.3 5.3 %all-to-all-done.1 = f32[32,1,128]{2,1,0:T(1,128)S(1)} async-done(((f32[32,1,128]{2,1,0:T(1,128)}), f32[32,1,128]{2,1,0:T(1,128)S(1)}, u32[]{:S(2)}, u32[]{:S(2)}) %all-to-all-start.1) | async-done | bytes 16416 | tf_op jit(solution)/shard_map/all_to_all | solution.py:749
  86.7 1.5 %combine.1 = f32[8,2048]{1,0:T(8,128)} custom-call(f32[32,128]{1,0:T(8,128)S(1)} %bitcast.19, f32[8,2048]{1,0:T(8,128)S(1)} %bitcast.15, f32[8,2048]{1,0:T(8,128)S(1)} %bitcast.16), custom_call_target="tpu_custom_call" | custom-call | tf_op jit(solution)/shard_map/combine/pallas_call | solution.py:752
  88.1 0.0 copy-done
Async XLA Ops:
  4.7 40.2 %all-to-all-start = ((f32[32,82,1,128]{3,2,1,0:T(1,128)}), f32[32,82,1,128]{3,2,1,0:T(1,128)S(1)}, u32[]{:S(2)}, u32[]{:S(2)}) async-start(f32[32,82,1,128]{3,2,1,0:T(1,128)} %bitcast.24), calls=%async_computation | async-start | bytes 2686976 | tf_op jit(solution)/shard_map/all_to_all | solution.py:670
  52.8 15.7 %collective-permute-start = (f32[552,128]{1,0:T(8,128)S(1)}, f32[552,128]{1,0:T(8,128)S(1)}, u32[]{:S(2)}, u32[]{:S(2)}) collective-permute-start(f32[552,128]{1,0:T(8,128)S(1)} %get-tuple-element.28), channel_id=1, source_target_pairs={{0,1},{1,2},{2,3},{3,4},{4,5},{5,6},{6,7},{7,8},{8,9},{9,10},{10,1... | collective-permute-start | bytes 847880 | tf_op jit(solution)/shard_map/ppermute | solution.py:619
  52.8 15.7 %collective-permute-start.1 = (f32[296,128]{1,0:T(8,128)S(1)}, f32[296,128]{1,0:T(8,128)S(1)}, u32[]{:S(2)}, u32[]{:S(2)}) collective-permute-start(f32[296,128]{1,0:T(8,128)S(1)} %get-tuple-element.29), channel_id=1, source_target_pairs={{0,31},{1,0},{2,1},{3,2},{4,3},{5,4},{6,5},{7,6},{8,7},{9,8},{10,9... | collective-permute-start | bytes 454664 | tf_op jit(solution)/shard_map/ppermute | solution.py:619
  77.0 9.6 %all-to-all-start.1 = ((f32[32,1,128]{2,1,0:T(1,128)}), f32[32,1,128]{2,1,0:T(1,128)S(1)}, u32[]{:S(2)}, u32[]{:S(2)}) async-start(f32[32,1,128]{2,1,0:T(1,128)} %get-tuple-element.31), calls=%async_computation.1 | async-start | bytes 32768 | tf_op jit(solution)/shard_map/all_to_all | solution.py:749
  80.5 7.7 %copy-start = (f32[2048,8]{0,1:T(8,128)}, f32[2048,8]{0,1:T(8,128)S(1)}, u32[]{:S(2)}) copy-start(f32[2048,8]{0,1:T(8,128)S(1)} %copy.27) | copy-start | bytes 196612

commit v6 on v5

--- a/solution.py
+++ b/solution.py
@@ -32,7 +32,7 @@
 
 LARGE = 60
 PER_ITEM = 8
-UNROLL = 16
+UNROLL = 24
 GROUPS = 16
 SUM_ROW = NLOC + 1
 EDGE = 8
@@ -434,47 +434,26 @@
     del edge_ref, edge_sums_ref
 
 
-def lane_bits(offset, bit):
-    return (offset // (1 << bit)) % 2 == 1
-
-
 def gathered(rows, offset, odd):
-    lane = iota(rows.shape, 1)
-    here = rows
-    there = jnp.concatenate([rows[1:], jnp.zeros((1, LANES), F32)], axis=0)
+    amount = offset * NPAR + (LANES // 2 if odd else 0)
+    below = jnp.concatenate([rows[1:], jnp.zeros((1, LANES), F32)], axis=0)
+    moved = jnp.where(iota(rows.shape, 1) >= amount, rows, below)
     if odd:
-        half = LANES // 2
-        turned_here, turned_there = pltpu.roll(here, half, 1), pltpu.roll(there, half, 1)
-        here = jnp.where(lane < LANES - half, turned_here, turned_there)
-        there = turned_there
+        moved = pltpu.roll(moved, LANES // 2, 1)
     for bit in range(3):
-        step = NPAR << bit
-        take = lane_bits(offset, bit)
-        turned_here, turned_there = (
-            pltpu.roll(here, LANES - step, 1),
-            pltpu.roll(there, LANES - step, 1),
-        )
-        moved = jnp.where(lane < LANES - step, turned_here, turned_there)
-        here = jnp.where(take, moved, here)
-        there = jnp.where(take, turned_there, there)
-    return here
+        turned = pltpu.roll(moved, LANES - (NPAR << bit), 1)
+        moved = jnp.where((offset & (1 << bit)) != 0, turned, moved)
+    return moved
 
 
 def scattered(rows, offset, odd):
-    lane = iota(rows.shape, 1)
-    here, there = rows, jnp.zeros_like(rows)
-    steps = [(NPAR << bit, bit) for bit in range(3)] + ([(LANES // 2, None)] if odd else [])
-    for step, bit in steps:
-        turned_here, turned_there = pltpu.roll(here, step, 1), pltpu.roll(there, step, 1)
-        new_here = jnp.where(lane < step, 0.0, turned_here)
-        new_there = jnp.where(lane < step, turned_here, turned_there)
-        if bit is None:
-            here, there = new_here, new_there
-        else:
-            take = lane_bits(offset, bit)
-            here = jnp.where(take, new_here, here)
-            there = jnp.where(take, new_there, there)
-    return here, there
+    amount = offset * NPAR + (LANES // 2 if odd else 0)
+    moved = pltpu.roll(rows, LANES // 2, 1) if odd else rows
+    for bit in range(3):
+        turned = pltpu.roll(moved, NPAR << bit, 1)
+        moved = jnp.where((offset & (1 << bit)) != 0, turned, moved)
+    here = iota(rows.shape, 1) >= amount
+    return jnp.where(here, moved, 0.0), jnp.where(here, 0.0, moved)
 
 
 def krylov_kernel(

time: 88.6 us -> 88.4 us (level)
  no operation moved by 1% of the time
where the time goes in v6:
time: 88.4 us; the launch traced here: 88 us
  waiting for transfers between devices  35.7 us (40%)
  Pallas kernels  31.8 us (36%)
  starting transfers between devices  15.2 us (17%)
  local copies, waits for them, and re-layouts  3.64 us (4%)
  between operations  0.91 us (1%)
    all_to_all x1, waiting for transfers between devices, on_device(): recv = lax.all_to_all(send, AXES, split_axis=0, concat_axis=0, tiled=True)  30.4 us
    pallas_call x1, Pallas kernels, on_device(): pl.pallas_call(inner_kernel, out_shape=(shape(roads, width, width), shape...  10.2 us
    pallas_call x1, Pallas kernels, on_device(): pl.pallas_call(krylov_kernel, out_shape=(shape(half, width), shape(half,...  7.93 us
    all_to_all x1, starting transfers between devices, on_device(): recv = lax.all_to_all(send, AXES, split_axis=0, concat_axis=0, tiled=True)  7.3 us
    pallas_call x1, Pallas kernels, on_device(): pl.pallas_call(functools.partial(edge_kernel, cap), out_shape=(shape((slo...  6.15 us
    ppermute x2, starting transfers between devices, neighbour(): lax.ppermute(value, AXES, [(s, (s + steps) % count) for s in range(count)])  5.39 us
    all_to_all x1, waiting for transfers between devices, on_device(): lax.all_to_all(dots, AXES, split_axis=0, concat_axis=0, tiled=True)  5.31 us
    pallas_call x1, Pallas kernels, on_device(): pl.pallas_call(functools.partial(pack_kernel, cap, roads, modules * devic...  4.08 us
  transfers between devices with their start and end apart: 4, of which 2 were waited for; matrix products, arithmetic and copies ran while one was open for 5% of the time, Pallas kernels for 12%

profile of v6, /device:TPU:0, one launch (start us, length us, event | category | flops | bytes accessed | tf_op | source)
XLA Modules:
  0.0 88.0 jit_solution(14569313917916122858)
XLA Ops:
  0.6 4.1 %fit_and_pack.1 = f32[2624,128]{1,0:T(8,128)} custom-call(f32[5,12,512]{2,1,0:T(8,128)} %ld_hbm.1, f32[12,8,512]{2,1,0:T(8,128)} %bitcast.25, f32[12,512]{1,0:T(8,128)} %me_hbm.1, f32[12,512]{1,0:T(8,128)} %hw_hbm.1, s32[12,512]{1,0:T(8,128)} %hm_hbm.1, s32[1,512]{1,0:T(1,128)} %bitcast.28, s32[1,512]{1,0:T(1,128)} %bitcast.29), custom_call_target="tpu_custom_call" | custom-call | tf_op jit(solution)/shard_map/fit_and_pack/pallas_call | solution.py:628
  4.7 7.3 %all-to-all-start = ((f32[32,82,1,128]{3,2,1,0:T(1,128)}), f32[32,82,1,128]{3,2,1,0:T(1,128)S(1)}, u32[]{:S(2)}, u32[]{:S(2)}) async-start(f32[32,82,1,128]{3,2,1,0:T(1,128)} %bitcast.24), calls=%async_computation | async-start | bytes 2686976 | tf_op jit(solution)/shard_map/all_to_all | solution.py:649
  12.0 0.7 fusion
  12.7 0.1 copy.23.off_ref
  12.9 1.2 %copy.24 = f32[2048,8]{1,0:T(8,128)S(1)} copy(f32[2048,8]{0,1:T(8,128)} %param.17) | data formatting | bytes 131072 | tf_op args[8]
  14.0 0.5 reshape.39.prior_ref
  14.5 30.4 %all-to-all-done = f32[32,82,1,128]{3,2,1,0:T(1,128)S(1)} async-done(((f32[32,82,1,128]{3,2,1,0:T(1,128)}), f32[32,82,1,128]{3,2,1,0:T(1,128)S(1)}, u32[]{:S(2)}, u32[]{:S(2)}) %all-to-all-start) | async-done | bytes 1343520 | tf_op jit(solution)/shard_map/all_to_all | solution.py:649
  44.9 2.0 %sort_by_road.1 = (s32[40,128]{1,0:T(8,128)S(1)}, s32[8,128]{1,0:T(8,128)S(1)}, s32[8,128]{1,0:T(8,128)S(1)}, f32[16,128]{1,0:T(8,128)S(1)}) custom-call(f32[2624,128]{1,0:T(8,128)S(1)} %bitcast.13, f32[256,1]{1,0:T(8,128)S(1)} %copy.23.off_ref), custom_call_target="tpu_custom_call" | custom-call | tf_op jit(solution)/shard_map/sort_by_road/pallas_call | solution.py:658
  46.9 0.1 broadcast_in_dim.18.off_rows_ref.off_ref
  47.0 6.1 %lay_and_assemble_edges.1 = (f32[16448,128]{1,0:T(8,128)S(1)}, f32[256,128,128]{2,1,0:T(8,128)S(1)}, f32[256,128]{1,0:T(8,128)S(1)}, f32[552,128]{1,0:T(8,128)S(1)}, f32[296,128]{1,0:T(8,128)S(1)}) custom-call(s32[1024]{0:T(1024)S(1)} %bitcast.22, s32[5120]{0:T(1024)S(1)} %bitcast.17, s32[1024]{0:T(1024)S(1)} %bitcast.20, f32[2624,128]{1,0:T(8,128)S(1)} %bitcast.14, ...), custom_call_target="tpu_custom_call" | custom-call | tf_op jit(solution)/shard_map/lay_and_assemble_edges/pallas_call | solution.py:678
  53.2 0.1 collective-permute-start
  53.2 5.3 %collective-permute-start.1 = (f32[296,128]{1,0:T(8,128)S(1)}, f32[296,128]{1,0:T(8,128)S(1)}, u32[]{:S(2)}, u32[]{:S(2)}) collective-permute-start(f32[296,128]{1,0:T(8,128)S(1)} %get-tuple-element.29), channel_id=1, source_target_pairs={{0,31},{1,0},{2,1},{3,2},{4,3},{5,4},{6,5},{7,6},{8,7},{9,8},{10,9... | collective-permute-start | bytes 454664 | tf_op jit(solution)/shard_map/ppermute | solution.py:598
  58.6 10.2 %assemble_blocks.1 = (f32[256,128,128]{2,1,0:T(8,128)}, f32[256,128,128]{2,1,0:T(8,128)S(1)}, f32[256,128]{1,0:T(8,128)S(1)}) custom-call(s32[1024]{0:T(1024)S(1)} %bitcast.23, s32[5120]{0:T(1024)S(1)} %bitcast.18, s32[1024]{0:T(1024)S(1)} %bitcast.21, f32[16448,128]{1,0:T(8,128)S(1)} %get-tuple-element.22.tiles_ref, ...), custom_call_target="tpu_custom_call", output_to_operand_aliasing={{1}: (4, {}), {2}: (5, {})} | custom-call | tf_op jit(solution)/shard_map/assemble_blocks/pallas_call | solution.py:696
  68.7 0.0 collective-permute-done.1.from_next_ref
  68.7 0.0 collective-permute-done.from_prev_ref
  68.8 7.9 %two_products.1 = (f32[128,128]{1,0:T(8,128)S(1)}, f32[128,128]{1,0:T(8,128)S(1)}, f32[32,1,128]{2,1,0:T(1,128)}) custom-call(f32[256,128,128]{2,1,0:T(8,128)S(1)} %get-tuple-element.26.held, f32[256,128]{1,0:T(8,128)S(1)} %get-tuple-element.27.sums_ref, f32[256,128]{1,0:T(8,128)S(1)} %broadcast_in_dim.18.off_rows_ref.off_ref, ...), custom_call_target="tpu_custom_call" | custom-call | tf_op jit(solution)/shard_map/two_products/pallas_call | solution.py:717
  76.7 2.5 %all-to-all-start.1 = ((f32[32,1,128]{2,1,0:T(1,128)}), f32[32,1,128]{2,1,0:T(1,128)S(1)}, u32[]{:S(2)}, u32[]{:S(2)}) async-start(f32[32,1,128]{2,1,0:T(1,128)} %get-tuple-element.31), calls=%async_computation.1 | async-start | bytes 32768 | tf_op jit(solution)/shard_map/all_to_all | solution.py:728
  79.2 0.6 reshape.40
  79.8 0.3 copy.27
  80.1 0.0 copy-start
  80.1 0.6 reshape.42
  80.7 0.3 copy.26
  81.0 5.3 %all-to-all-done.1 = f32[32,1,128]{2,1,0:T(1,128)S(1)} async-done(((f32[32,1,128]{2,1,0:T(1,128)}), f32[32,1,128]{2,1,0:T(1,128)S(1)}, u32[]{:S(2)}, u32[]{:S(2)}) %all-to-all-start.1) | async-done | bytes 16416 | tf_op jit(solution)/shard_map/all_to_all | solution.py:728
  86.3 1.5 %combine.1 = f32[8,2048]{1,0:T(8,128)} custom-call(f32[32,128]{1,0:T(8,128)S(1)} %bitcast.19, f32[8,2048]{1,0:T(8,128)S(1)} %bitcast.15, f32[8,2048]{1,0:T(8,128)S(1)} %bitcast.16), custom_call_target="tpu_custom_call" | custom-call | tf_op jit(solution)/shard_map/combine/pallas_call | solution.py:731
  87.8 0.0 copy-done
Async XLA Ops:
  4.7 40.2 %all-to-all-start = ((f32[32,82,1,128]{3,2,1,0:T(1,128)}), f32[32,82,1,128]{3,2,1,0:T(1,128)S(1)}, u32[]{:S(2)}, u32[]{:S(2)}) async-start(f32[32,82,1,128]{3,2,1,0:T(1,128)} %bitcast.24), calls=%async_computation | async-start | bytes 2686976 | tf_op jit(solution)/shard_map/all_to_all | solution.py:649
  53.2 15.6 %collective-permute-start = (f32[552,128]{1,0:T(8,128)S(1)}, f32[552,128]{1,0:T(8,128)S(1)}, u32[]{:S(2)}, u32[]{:S(2)}) collective-permute-start(f32[552,128]{1,0:T(8,128)S(1)} %get-tuple-element.28), channel_id=1, source_target_pairs={{0,1},{1,2},{2,3},{3,4},{4,5},{5,6},{6,7},{7,8},{8,9},{9,10},{10,1... | collective-permute-start | bytes 847880 | tf_op jit(solution)/shard_map/ppermute | solution.py:598
  53.2 15.5 %collective-permute-start.1 = (f32[296,128]{1,0:T(8,128)S(1)}, f32[296,128]{1,0:T(8,128)S(1)}, u32[]{:S(2)}, u32[]{:S(2)}) collective-permute-start(f32[296,128]{1,0:T(8,128)S(1)} %get-tuple-element.29), channel_id=1, source_target_pairs={{0,31},{1,0},{2,1},{3,2},{4,3},{5,4},{6,5},{7,6},{8,7},{9,8},{10,9... | collective-permute-start | bytes 454664 | tf_op jit(solution)/shard_map/ppermute | solution.py:598
  76.7 9.6 %all-to-all-start.1 = ((f32[32,1,128]{2,1,0:T(1,128)}), f32[32,1,128]{2,1,0:T(1,128)S(1)}, u32[]{:S(2)}, u32[]{:S(2)}) async-start(f32[32,1,128]{2,1,0:T(1,128)} %get-tuple-element.31), calls=%async_computation.1 | async-start | bytes 32768 | tf_op jit(solution)/shard_map/all_to_all | solution.py:728
  80.1 7.7 %copy-start = (f32[2048,8]{0,1:T(8,128)}, f32[2048,8]{0,1:T(8,128)S(1)}, u32[]{:S(2)}) copy-start(f32[2048,8]{0,1:T(8,128)S(1)} %copy.27) | copy-start | bytes 196612
